TPU v7x, 32 devices: a whole 2x2x4 slice. The times are simulated.
32 devices in a mesh: dp: 16 (over z, y, x), pipe: 2 (over core).
Axes of the slice: x: 2, y: 2, z: 4, core: 2. Of those that a mesh axis runs over, the one named last changes fastest.
Arguments:
- hidden_in: bfloat16 [4096, 2048], P(('dp', 'pipe')), may hold values from -6 to 6
- grad_out: bfloat16 [4096, 2048], P(('dp', 'pipe')), may hold values from -1.1953125 to 1.1953125
- w_query: bfloat16 [2, 2048, 512], P('pipe'), may hold values from -0.125 to 0.125
- w_key: bfloat16 [2, 2048, 512], P('pipe'), may hold values from -0.125 to 0.125
- w_value: bfloat16 [2, 2048, 512], P('pipe'), may hold values from -0.125 to 0.125
- w_out: bfloat16 [2, 512, 2048], P('pipe'), may hold values from -0.1875 to 0.1875
- pattern: int32 [4, 3], replicated, may hold values from 0 to 3, as said below
Outputs:
- hidden_out: bfloat16 [4096, 2048], P(('dp', 'pipe'))
- grad_in: bfloat16 [4096, 2048], P(('dp', 'pipe'))
- grad_query: float32 [2, 2048, 512], P('pipe', 'dp')
- grad_key: float32 [2, 2048, 512], P('pipe', 'dp')
- grad_value: float32 [2, 2048, 512], P('pipe', 'dp')
- grad_wout: float32 [2, 512, 2048], P('pipe', 'dp')
Inputs may be any that keep to these rules, and one draw needn't show every extreme that they name: `pattern`: row i lists key blocks for query block i: entry 0 is i, entry 1 is the block before i (i itself for the first block), the others are blocks no later than i; a row may repeat an entry.
All inputs are finite; a program needn't handle non-finite values.
Results may differ from a plain program's by a relative error of at most 0.023.
Values may be sent and summed in bfloat16 or wider, within the bound.
No kernel may reach another device: no remote copies, remote signals or barrier semaphores. Data moves between devices by JAX's collectives and lax.ppermute only.
A program may use at most 128 MiB of HBM per device.

v0:
```python
import math

import jax
import jax.numpy as jnp
from jax import lax
from jax.sharding import PartitionSpec as P

HDIM = 64
BLK = 32


NORM_EPS = 1e-05


def partner(x, axis, apart):
    return lax.ppermute(x, axis, [(i, i ^ 1 << apart) for i in range(lax.axis_size(axis))])


def visible_mask(pattern, block_len):
    blocks, slot_count = pattern.shape
    equal_slot = pattern[:, :, None] == pattern[:, None, :]
    before = jnp.arange(slot_count)[None, :] < jnp.arange(slot_count)[:, None]
    repeated = jnp.any(equal_slot & before[None, :, :], axis=2)
    row_ids = jnp.arange(block_len)[:, None]
    column_ids = jnp.arange(block_len)[None, :]
    diagonal = pattern == jnp.arange(blocks, dtype=jnp.int32)[:, None]
    allowed = jnp.where(diagonal[:, :, None, None], (column_ids <= row_ids)[None, None], True)
    visible = allowed & jnp.logical_not(repeated)[:, :, None, None]
    return jnp.transpose(visible, (0, 2, 1, 3))


def contract(left_factor, right_factor):
    return lax.dot_general(
        left_factor, right_factor, (((0,), (0,)), ((), ())), preferred_element_type=jnp.float32
    )


def attend_forward(inputs, query_w, key_w, value_w, out_w, pattern, head_dim, block_len):
    amount, seq_len, features = inputs.shape
    blocks = seq_len // block_len
    head_count = query_w.shape[1] // head_dim
    input_f32 = inputs.astype(jnp.float32)
    factor = lax.rsqrt(jnp.mean(input_f32 * input_f32, axis=-1, keepdims=True) + NORM_EPS)
    normed = (input_f32 * factor).astype(jnp.bfloat16).reshape(amount * seq_len, features)
    query = jnp.dot(normed, query_w, preferred_element_type=jnp.float32).astype(jnp.bfloat16)
    key_proj = jnp.dot(normed, key_w, preferred_element_type=jnp.float32).astype(jnp.bfloat16)
    values = jnp.dot(normed, value_w, preferred_element_type=jnp.float32).astype(jnp.bfloat16)
    blocked = (amount, blocks, block_len, head_count, head_dim)
    query_blocks = query.reshape(blocked)
    keys_seen = jnp.take(key_proj.reshape(blocked), pattern, axis=1)
    values_seen = jnp.take(values.reshape(blocked), pattern, axis=1)
    inv_sqrt = 1.0 / math.sqrt(head_dim)
    scores = (
        jnp.einsum(
            "mqihd,mqsjhd->mqhisj", query_blocks, keys_seen, preferred_element_type=jnp.float32
        )
        * inv_sqrt
    )
    visible = visible_mask(pattern, block_len)[None, :, None]
    expo = jnp.where(visible, jnp.exp(scores), 0.0)
    totals = jnp.sum(expo, axis=(4, 5), keepdims=True)
    prob_f32 = expo / totals
    prob_bf16 = prob_f32.astype(jnp.bfloat16)
    attended = jnp.einsum(
        "mqhisj,mqsjhd->mqihd", prob_bf16, values_seen, preferred_element_type=jnp.float32
    )
    attended = attended.astype(jnp.bfloat16).reshape(amount * seq_len, head_count * head_dim)
    contrib = jnp.dot(attended, out_w, preferred_element_type=jnp.float32).astype(jnp.bfloat16)
    stash_fwd = (
        input_f32,
        factor,
        normed,
        query_blocks,
        keys_seen,
        values_seen,
        prob_f32,
        prob_bf16,
        attended,
    )
    return (contrib.reshape(amount, seq_len, features), stash_fwd)


def attend_backward(
    stash_fwd, cotangent, query_w, key_w, value_w, out_w, pattern, head_dim, block_len
):
    (
        input_f32,
        factor,
        normed,
        query_blocks,
        keys_seen,
        values_seen,
        prob_f32,
        prob_bf16,
        attended,
    ) = stash_fwd
    amount, seq_len, features = cotangent.shape
    blocks = seq_len // block_len
    head_count = query_w.shape[1] // head_dim
    inv_sqrt = 1.0 / math.sqrt(head_dim)
    grad_flat = cotangent.reshape(amount * seq_len, features)
    grad_attended = lax.dot_general(
        grad_flat, out_w, (((1,), (1,)), ((), ())), preferred_element_type=jnp.float32
    )
    grad_attended = grad_attended.astype(jnp.bfloat16).reshape(
        amount, blocks, block_len, head_count, head_dim
    )
    grad_prob = jnp.einsum(
        "mqihd,mqsjhd->mqhisj", grad_attended, values_seen, preferred_element_type=jnp.float32
    )
    grad_valseen = jnp.einsum(
        "mqhisj,mqihd->mqsjhd", prob_bf16, grad_attended, preferred_element_type=jnp.float32
    )
    inner_sum = jnp.sum(prob_f32 * grad_prob, axis=(4, 5), keepdims=True)
    grad_score = (prob_f32 * (grad_prob - inner_sum) * inv_sqrt).astype(jnp.bfloat16)
    grad_querypos = jnp.einsum(
        "mqhisj,mqsjhd->mqihd", grad_score, keys_seen, preferred_element_type=jnp.float32
    )
    grad_querypos = grad_querypos.astype(jnp.bfloat16).reshape(
        amount * seq_len, head_count * head_dim
    )
    grad_keyseen = jnp.einsum(
        "mqhisj,mqihd->mqsjhd", grad_score, query_blocks, preferred_element_type=jnp.float32
    )
    onehot = (pattern[:, :, None] == jnp.arange(blocks, dtype=jnp.int32)[None, None, :]).astype(
        jnp.float32
    )
    grad_keypos = jnp.einsum(
        "qsk,mqsjhd->mkjhd", onehot, grad_keyseen, precision=lax.Precision.HIGHEST
    )
    grad_keypos = grad_keypos.astype(jnp.bfloat16).reshape(amount * seq_len, head_count * head_dim)
    grad_valuepos = jnp.einsum(
        "qsk,mqsjhd->mkjhd", onehot, grad_valseen, precision=lax.Precision.HIGHEST
    )
    grad_valuepos = grad_valuepos.astype(jnp.bfloat16).reshape(
        amount * seq_len, head_count * head_dim
    )
    dims = (((1,), (1,)), ((), ()))
    grad_normed = lax.dot_general(grad_querypos, query_w, dims, preferred_element_type=jnp.float32)
    grad_normed = grad_normed + lax.dot_general(
        grad_keypos, key_w, dims, preferred_element_type=jnp.float32
    )
    grad_normed = grad_normed + lax.dot_general(
        grad_valuepos, value_w, dims, preferred_element_type=jnp.float32
    )
    grad_normed = grad_normed.reshape(amount, seq_len, features)
    mean_term = jnp.mean(input_f32 * grad_normed, axis=-1, keepdims=True)
    returned = (factor * grad_normed - input_f32 * factor * factor * factor * mean_term).astype(
        jnp.bfloat16
    )
    factor_pairs = (
        (normed, grad_querypos),
        (normed, grad_keypos),
        (normed, grad_valuepos),
        (attended, grad_flat),
    )
    return (returned, factor_pairs)


def on_device(hidden_in, grad_out, w_query, w_key, w_value, w_out, pattern):
    bit_count = lax.axis_size("pipe").bit_length() - 1
    bit_order = list(range(bit_count))
    query_w = w_query[0]
    key_w = w_key[0]
    value_w = w_value[0]
    out_w = w_out[0]

    def mirror_single(payload):
        for bit_index in bit_order:
            payload = partner(payload, "pipe", bit_index)
        return payload

    mirror_input = mirror_single(hidden_in)
    contrib, stash_fwd = attend_forward(
        jnp.stack([hidden_in, mirror_input]), query_w, key_w, value_w, out_w, pattern, HDIM, BLK
    )
    contrib_other = mirror_single(contrib[1])
    mirror_grad = mirror_single(grad_out)
    returned, factor_pairs = attend_backward(
        stash_fwd,
        jnp.stack([grad_out, mirror_grad]),
        query_w,
        key_w,
        value_w,
        out_w,
        pattern,
        HDIM,
        BLK,
    )
    returned_other = mirror_single(returned[1])
    hidden_out = (
        hidden_in.astype(jnp.float32)
        + contrib[0].astype(jnp.float32)
        + contrib_other.astype(jnp.float32)
    ).astype(jnp.bfloat16)
    grad_in = (
        grad_out.astype(jnp.float32)
        + returned[0].astype(jnp.float32)
        + returned_other.astype(jnp.float32)
    ).astype(jnp.bfloat16)
    full_grads = [contract(factor_pair[0], factor_pair[1]) for factor_pair in factor_pairs]
    shares = (
        lax.psum_scatter(
            full_grads[0].astype(jnp.bfloat16), "dp", scatter_dimension=0, tiled=True
        ).astype(jnp.float32),
        lax.psum_scatter(
            full_grads[1].astype(jnp.bfloat16), "dp", scatter_dimension=0, tiled=True
        ).astype(jnp.float32),
        lax.psum_scatter(
            full_grads[2].astype(jnp.bfloat16), "dp", scatter_dimension=0, tiled=True
        ).astype(jnp.float32),
        lax.psum_scatter(
            full_grads[3].astype(jnp.bfloat16), "dp", scatter_dimension=0, tiled=True
        ).astype(jnp.float32),
    )
    return (hidden_out, grad_in, shares[0][None], shares[1][None], shares[2][None], shares[3][None])


def solution(mesh):
    in_specs = (
        P(("dp", "pipe"), None),
        P(("dp", "pipe"), None),
        P("pipe", None, None),
        P("pipe", None, None),
        P("pipe", None, None),
        P("pipe", None, None),
        P(),
    )
    out_specs = (
        P(("dp", "pipe"), None),
        P(("dp", "pipe"), None),
        P("pipe", "dp", None),
        P("pipe", "dp", None),
        P("pipe", "dp", None),
        P("pipe", "dp", None),
    )
    return jax.shard_map(
        on_device, mesh=mesh, in_specs=in_specs, out_specs=out_specs, check_vma=False
    )
```

profile of v0, /device:TPU:0, one launch (start us, length us, event | category | flops | bytes accessed | tf_op | source)
XLA Modules:
  0.0 383.5 jit_solution(8304726255953538325)
XLA Ops:
  20.5 2.3 fusion.45
  25.7 3.0 gather_fusion
  28.7 3.0 gather_fusion.1
  31.7 2.2 select_bitcast_fusion.1
  39.1 2.4 multiply_convert_fusion
  42.8 5.0 %fusion.34 = bf16[2,4,32,8,64]{4,1,3,2,0:T(4,128)(2,1)S(1)} fusion(f32[2,4,3,32,8,64]{5,3,2,4,1,0:T(8,128)S(1)} %bitcast.174, s32[4,3]{0,1:T(4,128)S(1)} %copy.31), kind=kOutput, calls=%fused_computation.46 | convolution fusion | flops 19005488 | bytes 1835056 | tf_op jit(solution)/shard_map/qsk,mqsjhd->mkjhd/dot_general | solution.py:128
  50.1 2.1 convolution_convert_fusion.2
  52.2 2.1 fusion.56
  54.3 4.8 %fusion.37 = bf16[2,4,32,8,64]{4,1,3,2,0:T(4,128)(2,1)S(1)} fusion(f32[2,4,3,32,8,64]{5,3,2,4,1,0:T(8,128)S(1)} %bitcast.173, s32[4,3]{0,1:T(4,128)S(1)} %copy.31), kind=kOutput, calls=%fused_computation.47 | convolution fusion | flops 19005488 | bytes 1835056 | tf_op jit(solution)/shard_map/qsk,mqsjhd->mkjhd/dot_general | solution.py:132
  61.3 2.1 convolution_convert_fusion.1
  63.5 2.4 fusion.41
  68.3 3.3 convolution_convert_fusion
  71.9 2.5 fusion.40
  75.4 2.1 reshape.269
  77.5 2.4 convolution_convert_fusion.4
  82.2 2.1 convolution_convert_fusion.3
  85.3 2.5 fusion.13
  91.1 2.1 add_convert_fusion
  94.3 41.4 %reduce-scatter.7.cloned.1.call-done = bf16[128,512]{1,0:T(8,128)(2,1)} async-done(((bf16[2048,512]{1,0:T(8,128)(2,1)}), bf16[128,512]{1,0:T(8,128)(2,1)}) %reduce-scatter.7.cloned.1.call-update) | async-done | bytes 131088 | tf_op jit(solution)/shard_map/reduce_scatter | solution.py:206
  135.6 1.6 bitcast_convert_fusion.2
  137.3 78.3 %reduce-scatter.9.cloned.1.call-done = bf16[128,512]{1,0:T(8,128)(2,1)} async-done(((bf16[2048,512]{1,0:T(8,128)(2,1)}), bf16[128,512]{1,0:T(8,128)(2,1)}) %reduce-scatter.9.cloned.1.call-update) | async-done | bytes 131088 | tf_op jit(solution)/shard_map/reduce_scatter | solution.py:209
  215.6 1.6 bitcast_convert_fusion.1
  217.2 78.3 %reduce-scatter.11.cloned.1.call-done = bf16[32,2048]{1,0:T(8,128)(2,1)} async-done(((bf16[512,2048]{1,0:T(8,128)(2,1)}), bf16[32,2048]{1,0:T(8,128)(2,1)}) %reduce-scatter.11.cloned.1.call-update) | async-done | bytes 131088 | tf_op jit(solution)/shard_map/reduce_scatter | solution.py:212
  297.1 78.1 %reduce-scatter.5.cloned.1.call-done = bf16[128,512]{1,0:T(8,128)(2,1)} async-done(((bf16[2048,512]{1,0:T(8,128)(2,1)}), bf16[128,512]{1,0:T(8,128)(2,1)}) %reduce-scatter.5.cloned.1.call-update) | async-done | bytes 131088 | tf_op jit(solution)/shard_map/reduce_scatter | solution.py:203
  (105 shorter events, 41.7 us)
Async XLA Ops:
  7.2 16.7 %copy-start = (bf16[1,2048,512]{2,1,0:T(8,128)(2,1)S(1)}, bf16[1,2048,512]{2,1,0:T(8,128)(2,1)}, u32[]{:S(2)}) copy-start(bf16[1,2048,512]{2,1,0:T(8,128)(2,1)} %param.13) | copy-start | bytes 6291460
  7.2 128.5 %reduce-scatter.7.cloned.1.call-start = ((), (), s32[]{:S(2)}) async-start(), calls=%async_computation.5 | async-start | bytes 2228224 | tf_op jit(solution)/shard_map/reduce_scatter | solution.py:206
  7.2 4.0 %collective-permute-start = (bf16[128,2048]{1,0:T(8,128)(2,1)}, bf16[128,2048]{1,0:T(8,128)(2,1)S(1)}, u32[]{:S(2)}, u32[]{:S(2)}) collective-permute-start(bf16[128,2048]{1,0:T(8,128)(2,1)} %param.9), channel_id=1, source_target_pairs={{0,1},{1,0},{2,3},{3,2},{4,5},{5,4},{6,7},{7,6},{8,9},{9,8},{10,11... | collective-permute-start | bytes 1572872 | tf_op jit(solution)/shard_map/ppermute | solution.py:16
  7.7 5.1 %collective-permute-start.2 = (bf16[128,2048]{1,0:T(8,128)(2,1)}, bf16[128,2048]{1,0:T(8,128)(2,1)S(1)}, u32[]{:S(2)}, u32[]{:S(2)}) collective-permute-start(bf16[128,2048]{1,0:T(8,128)(2,1)} %param.10), channel_id=1, source_target_pairs={{0,1},{1,0},{2,3},{3,2},{4,5},{5,4},{6,7},{7,6},{8,9},{9,8},{10,11... | collective-permute-start | bytes 1572872 | tf_op jit(solution)/shard_map/ppermute | solution.py:16
  11.1 3.9 %copy-start.20 = (bf16[1,512,2048]{2,1,0:T(8,128)(2,1)S(1)}, bf16[1,512,2048]{2,1,0:T(8,128)(2,1)}, u32[]{:S(2)}) copy-start(bf16[1,512,2048]{2,1,0:T(8,128)(2,1)} %param.14) | copy-start | bytes 6291460
  11.2 4.5 %copy-start.5 = (bf16[128,2048]{1,0:T(8,128)(2,1)}, bf16[128,2048]{1,0:T(8,128)(2,1)S(1)}, u32[]{:S(2)}) copy-start(bf16[128,2048]{1,0:T(8,128)(2,1)S(1)} %collective-permute-done) | copy-start | bytes 1572868
  16.8 1.9 copy-start.18
  33.9 1.6 copy-start.3
  34.2 1.4 copy-start.7
  41.6 1.2 copy-start.1
  50.0 2.1 copy-start.12
  52.2 163.4 %reduce-scatter.9.cloned.1.call-start = ((), (), s32[]{:S(2)}) async-start(), calls=%async_computation.6 | async-start | bytes 2228224 | tf_op jit(solution)/shard_map/reduce_scatter | solution.py:209
  61.3 2.1 copy-start.14
  63.4 232.1 %reduce-scatter.11.cloned.1.call-start = ((), (), s32[]{:S(2)}) async-start(), calls=%async_computation.7 | async-start | bytes 2228224 | tf_op jit(solution)/shard_map/reduce_scatter | solution.py:212
  71.7 303.6 %reduce-scatter.5.cloned.1.call-start = ((), (), s32[]{:S(2)}) async-start(), calls=%async_computation.4 | async-start | bytes 2228224 | tf_op jit(solution)/shard_map/reduce_scatter | solution.py:203
  77.5 4.7 %copy-start.16 = (bf16[256,512]{1,0:T(8,128)(2,1)S(1)}, bf16[256,512]{1,0:T(8,128)(2,1)}, u32[]{:S(2)}) copy-start(bf16[256,512]{1,0:T(8,128)(2,1)} %reshape.269) | copy-start | bytes 786436
  81.8 9.0 %collective-permute-start.1 = (bf16[128,2048]{1,0:T(8,128)(2,1)}, bf16[128,2048]{1,0:T(8,128)(2,1)}, u32[]{:S(2)}, u32[]{:S(2)}) collective-permute-start(bf16[128,2048]{1,0:T(8,128)(2,1)} %slice.23), channel_id=1, source_target_pairs={{0,1},{1,0},{2,3},{3,2},{4,5},{5,4},{6,7},{7,6},{8,9},{9,8},{10,11... | collective-permute-start | bytes 1572872 | tf_op jit(solution)/shard_map/ppermute | solution.py:16
  85.3 2.5 copy-start.13
  85.3 2.5 copy-start.19
  87.8 1.2 copy-start.6
  87.8 1.3 copy-start.15
  89.9 1.2 copy-start.10
  90.5 2.7 copy-start.21
  90.6 2.6 collective-permute-start.3
  (6 other events, 6.2 us)
Sparse Core Ops, SparseCore 0:
  52.3 83.3 reduce-scatter.6
  137.9 77.6 reduce-scatter.8
  217.9 77.6 reduce-scatter.10
  297.7 77.5 reduce-scatter.4
where the time goes:
time: 384 us; the launch traced here: 383 us
  waiting for transfers between devices  276 us (72%)
  matrix products  38.8 us (10%)
  local copies, waits for them, and re-layouts  29.2 us (8%)
  other arithmetic  23.5 us (6%)
  between operations  14.1 us (4%)
    reduce_scatter x1, waiting for transfers between devices, on_device(): lax.psum_scatter(full_grads[3].astype(jnp.bfloat16), 'dp', scatter_dimens...  78.3 us
    reduce_scatter x1, waiting for transfers between devices, on_device(): lax.psum_scatter(full_grads[2].astype(jnp.bfloat16), 'dp', scatter_dimens...  78.3 us
    reduce_scatter x1, waiting for transfers between devices, on_device(): lax.psum_scatter(full_grads[0].astype(jnp.bfloat16), 'dp', scatter_dimens...  78.1 us
    reduce_scatter x1, waiting for transfers between devices, on_device(): lax.psum_scatter(full_grads[1].astype(jnp.bfloat16), 'dp', scatter_dimens...  41.4 us
    dot_general x4, matrix products, contract(): lax.dot_general(left_factor, right_factor, (((0,), (0,)), ((), ())), pref...  9.55 us
  transfers between devices with their start and end apart: 8, of which 4 were waited for; matrix products, arithmetic and copies ran while one was open for 12% of the time, Pallas kernels for 0%

commit v1 on v0

v1 whole, which is shorter than its diff:
```python
import functools
import math

import jax
import jax.numpy as jnp
from jax import lax
from jax.experimental import pallas as pl
from jax.experimental.pallas import tpu as pltpu
from jax.sharding import PartitionSpec as P

HDIM = 64
NORM_EPS = 1e-05
PAIR = 2 * HDIM
VMEM_BYTES = 40 * 1024 * 1024

F32 = jnp.float32
BF16 = jnp.bfloat16
NT = (((1,), (1,)), ((), ()))
TN = (((0,), (0,)), ((), ()))

ROW_BIT = 0
COL_BIT = 2


def dot(left, right):
    return jnp.dot(left, right, preferred_element_type=F32)


def dot_nt(left, right):
    return lax.dot_general(left, right, NT, preferred_element_type=F32)


def dot_tn(left, right):
    return lax.dot_general(left, right, TN, preferred_element_type=F32)


def call(body, name, inputs, outs, scratch=(), flops=0, scalars=1):
    specs = [pl.BlockSpec(memory_space=pltpu.SMEM)] * scalars
    specs += [pl.BlockSpec(memory_space=pltpu.VMEM)] * (len(inputs) - scalars)
    moved = sum(x.size * x.dtype.itemsize for x in inputs)
    moved += sum(x.size * x.dtype.itemsize for x in outs)
    return pl.pallas_call(
        body,
        name=name,
        out_shape=outs,
        in_specs=specs,
        out_specs=[pl.BlockSpec(memory_space=pltpu.VMEM)] * len(outs),
        scratch_shapes=list(scratch),
        compiler_params=pltpu.CompilerParams(vmem_limit_bytes=VMEM_BYTES),
        cost_estimate=pl.CostEstimate(flops=flops, bytes_accessed=moved, transcendentals=0),
    )(*inputs)


def row_chunks(bit_count, halved_bits):
    order = list(halved_bits) + [COL_BIT]
    chunks = []
    for index in range(1 << len(order)):
        chunk = 0
        for place, bit in enumerate(reversed(order)):
            chunk |= ((index >> place) & 1) << bit
        chunks.append(chunk)
    return chunks


def copy_chunks(source, target, chunks, size, row_bit):
    for place, chunk in enumerate(chunks):
        start = pl.multiple_of((chunk + (row_bit << ROW_BIT)) * size, size)
        target[place * size : (place + 1) * size, :] = source[pl.ds(start, size), :]


def prep_body(chunks, bits, hidden, grad, x_keep, x_send, g_keep, g_send, turned):
    row_bit, col_bit = bits[0], bits[1]
    size = hidden.shape[1] // (2 * len(chunks))
    width = hidden.shape[1] // 2
    turned[...] = hidden[...].astype(F32).T.astype(BF16)
    copy_chunks(turned, x_keep, chunks, size, row_bit)
    copy_chunks(turned, x_send, chunks, size, 1 - row_bit)
    g_keep[...] = grad[:, pl.ds(pl.multiple_of(col_bit * width, width), width)]
    g_send[...] = grad[:, pl.ds(pl.multiple_of((1 - col_bit) * width, width), width)]


def seen_mask(pattern, seq_len, blocks, slots):
    block_len = seq_len // blocks
    rows = lax.broadcasted_iota(jnp.int32, (seq_len, seq_len), 0)
    columns = lax.broadcasted_iota(jnp.int32, (seq_len, seq_len), 1)
    row_block, column_block = rows // block_len, columns // block_len
    seen = jnp.zeros((seq_len, seq_len), F32)
    for block in range(blocks):
        for slot in range(slots):
            hit = (row_block == block) & (column_block == pattern[block, slot])
            seen = jnp.where(hit, 1.0, seen)
    return jnp.where((row_block == column_block) & (columns > rows), 0.0, seen)


def scale_of(x):
    return lax.rsqrt(jnp.mean(x * x, axis=-1, keepdims=True) + NORM_EPS)


def attention_body(
    chunks,
    bits,
    pattern,
    x_own,
    x_mirror,
    g_own,
    g_mirror,
    w_query,
    w_key,
    w_value,
    w_out,
    attended,
    att_keep,
    att_send,
    value_keep,
    value_send,
    key_keep,
    key_send,
    query_keep,
    query_send,
    query,
    key,
    values,
    grad_att,
    turned,
):
    row_bit, col_bit = bits[0], bits[1]
    seq_len = x_own.shape[0]
    half = w_query.shape[1]
    x = jnp.concatenate([x_own[...], x_mirror[...]], axis=0)
    factor = scale_of(x.astype(F32))
    query[...] = (dot(x, w_query[...]) * factor).astype(BF16)
    key[...] = (dot(x, w_key[...]) * factor).astype(BF16)
    values[...] = (dot(x, w_value[...]) * factor).astype(BF16)
    grad = jnp.concatenate([g_own[...], g_mirror[...]], axis=0)
    grad_att[...] = dot_nt(grad, w_out[...]).astype(BF16)

    seen = seen_mask(pattern, seq_len, pattern.shape[0], pattern.shape[1])
    seen = jnp.concatenate([seen, seen], axis=0) > 0.0
    low = lax.broadcasted_iota(jnp.int32, (seq_len, PAIR), 1) < HDIM
    inv_sqrt = 1.0 / math.sqrt(HDIM)
    zero = jnp.zeros((), BF16)

    def stacked(block):
        return jnp.concatenate([jnp.where(low, block, zero), jnp.where(low, zero, block)], axis=0)

    def merged(both):
        return jnp.where(low, both[:seq_len], both[seq_len:])

    width = half // 2
    for side, outs in (
        (col_bit, (value_keep, key_keep, query_keep)),
        (1 - col_bit, (value_send, key_send, query_send)),
    ):
        for pair in range(width // PAIR):
            columns = pl.ds(pl.multiple_of(side * width + pair * PAIR, PAIR), PAIR)
            here = slice(pair * PAIR, (pair + 1) * PAIR)
            for seq in range(2):
                rows = slice(seq * seq_len, (seq + 1) * seq_len)
                q2 = stacked(query[rows, columns])
                k = key[rows, columns]
                v = values[rows, columns]
                ga2 = stacked(grad_att[rows, columns])
                r = factor[rows]
                expo = jnp.where(seen, jnp.exp(dot_nt(q2, k) * inv_sqrt), 0.0)
                prob = expo / jnp.sum(expo, axis=-1, keepdims=True)
                prob_bf = prob.astype(BF16)
                attended[rows, columns] = merged(dot(prob_bf, v)).astype(BF16)
                grad_prob = dot_nt(ga2, v)
                inner = jnp.sum(prob * grad_prob, axis=-1, keepdims=True)
                score = (prob * (grad_prob - inner) * inv_sqrt).astype(BF16)
                outs[0][rows, here] = (dot_tn(prob_bf, ga2) * r).astype(BF16)
                outs[1][rows, here] = (dot_tn(score, q2) * r).astype(BF16)
                outs[2][rows, here] = (merged(dot(score, k)) * r).astype(BF16)

    turned[...] = attended[...].astype(F32).T.astype(BF16)
    size = half // (2 * len(chunks))
    copy_chunks(turned, att_keep, chunks, size, row_bit)
    copy_chunks(turned, att_send, chunks, size, 1 - row_bit)


def returned_body(
    bits,
    x_own,
    x_mirror,
    attended,
    value_keep,
    value_send,
    key_keep,
    key_send,
    query_keep,
    query_send,
    w_query,
    w_key,
    w_value,
    w_out,
    contrib_own,
    contrib_mirror,
    returned_own,
    returned_mirror,
):
    col_bit = bits[1]
    seq_len = x_own.shape[0]
    width = value_keep.shape[1]
    contrib = dot(attended[...], w_out[...]).astype(BF16)
    contrib_own[...] = contrib[:seq_len]
    contrib_mirror[...] = contrib[seq_len:]
    keep = pl.ds(pl.multiple_of(col_bit * width, width), width)
    send = pl.ds(pl.multiple_of((1 - col_bit) * width, width), width)
    grad = dot_nt(query_keep[...], w_query[:, keep])
    grad += dot_nt(query_send[...], w_query[:, send])
    grad += dot_nt(key_keep[...], w_key[:, keep])
    grad += dot_nt(key_send[...], w_key[:, send])
    grad += dot_nt(value_keep[...], w_value[:, keep])
    grad += dot_nt(value_send[...], w_value[:, send])
    x = jnp.concatenate([x_own[...], x_mirror[...]], axis=0).astype(F32)
    factor = scale_of(x)
    mean_term = jnp.mean(x * grad, axis=-1, keepdims=True)
    returned = (grad - x * (factor * factor * mean_term)).astype(BF16)
    returned_own[...] = returned[:seq_len]
    returned_mirror[...] = returned[seq_len:]


def weight_grad_body(left_count, bits, *refs):
    first_bit = bits[2]
    lefts = refs[:left_count]
    rights = refs[left_count:-2]
    keep, send = refs[-2:]
    rows = keep.shape[0]
    right = jnp.concatenate([ref[...] for ref in rights], axis=0)
    for target, side in ((send, 1 - first_bit), (keep, first_bit)):
        part = pl.ds(pl.multiple_of(side * rows, rows), rows)
        left = jnp.concatenate([ref[part, :] for ref in lefts], axis=1)
        target[...] = dot(left, right).astype(BF16)


def on_device(hidden_in, grad_out, w_query, w_key, w_value, w_out, pattern):
    replicas = lax.axis_size("dp")
    pipe = lax.axis_size("pipe")
    bit_count = replicas.bit_length() - 1
    halved_bits = [bit for bit in range(bit_count) if bit not in (ROW_BIT, COL_BIT)]
    index = lax.axis_index("dp")
    seq_len, features = hidden_in.shape
    half = w_query.shape[2]
    w_query, w_key, w_value, w_out = w_query[0], w_key[0], w_value[0], w_out[0]

    def bit_of(bit):
        return (index >> bit) & 1

    def swap(x, bit):
        return lax.ppermute(x, "dp", [(i, i ^ (1 << bit)) for i in range(replicas)])

    def mirror(x):
        return lax.ppermute(x, "pipe", [(i, pipe - 1 - i) for i in range(pipe)])

    bits = jnp.stack([bit_of(ROW_BIT), bit_of(COL_BIT), bit_of(halved_bits[0])]).astype(jnp.int32)
    chunks = row_chunks(bit_count, halved_bits)

    def bf16(*shape):
        return jax.ShapeDtypeStruct(shape, BF16)

    x_mirror = mirror(hidden_in)
    g_mirror = mirror(grad_out)
    x_keep, x_send, g_keep, g_send = call(
        functools.partial(prep_body, chunks),
        "prep",
        (bits, hidden_in, grad_out),
        [bf16(features // 2, seq_len)] * 2 + [bf16(seq_len, features // 2)] * 2,
        [pltpu.VMEM((features, seq_len), BF16)],
    )

    def gather(keep, send, send_bit, keep_bit):
        near = swap(send, send_bit)
        far = swap(keep, keep_bit)
        last = swap(near, keep_bit)
        if send_bit == ROW_BIT:
            return [keep, near, far, last]
        return [keep, far, near, last]

    g_pieces = gather(g_keep, g_send, COL_BIT, ROW_BIT)
    x_pieces = gather(x_keep, x_send, ROW_BIT, COL_BIT)
    g_all = [piece for own in g_pieces for piece in (own, mirror(own))]
    x_all = [piece for own in x_pieces for piece in (own, mirror(own))]

    tokens = 2 * seq_len
    outs = call(
        functools.partial(attention_body, chunks),
        "attention",
        (bits, pattern, hidden_in, x_mirror, grad_out, g_mirror, w_query, w_key, w_value, w_out),
        [bf16(tokens, half)] + [bf16(half // 2, tokens)] * 2 + [bf16(tokens, half // 2)] * 6,
        [pltpu.VMEM((tokens, half), BF16)] * 4 + [pltpu.VMEM((half, tokens), BF16)],
        flops=8 * tokens * features * half,
        scalars=2,
    )
    attended, att_keep, att_send = outs[:3]
    grads = outs[3:]

    def reduced(lefts, rights, name):
        rows = lefts[0].shape[0] // 2
        columns = rights[0].shape[1]
        keep, send = call(
            functools.partial(weight_grad_body, len(lefts)),
            name,
            (bits, *lefts, *rights),
            [bf16(rows, columns)] * 2,
            flops=4 * rows * columns * tokens * 4,
        )
        for place, bit in enumerate(halved_bits):
            arrived = swap(send, bit)
            total = (keep.astype(F32) + arrived.astype(F32)).astype(BF16)
            after = halved_bits[place + 1] if place + 1 < len(halved_bits) else COL_BIT
            parts = total.reshape(2, total.shape[0] // 2, columns)
            keep = lax.dynamic_index_in_dim(parts, bit_of(after), 0, keepdims=False)
            send = lax.dynamic_index_in_dim(parts, 1 - bit_of(after), 0, keepdims=False)
        other = swap(send, COL_BIT)
        own_low = bit_of(COL_BIT) == 0
        low = jnp.where(own_low, keep, other)
        high = jnp.where(own_low, other, keep)
        return jnp.concatenate([low, high], axis=1).astype(F32)[None]

    att_pieces = gather(att_keep, att_send, ROW_BIT, COL_BIT)
    grad_wout = reduced(att_pieces, g_all, "grad_wout")
    grad_value = reduced(x_all, gather(grads[0], grads[1], COL_BIT, ROW_BIT), "grad_value")
    grad_key = reduced(x_all, gather(grads[2], grads[3], COL_BIT, ROW_BIT), "grad_key")
    grad_query = reduced(x_all, gather(grads[4], grads[5], COL_BIT, ROW_BIT), "grad_query")

    contrib, contrib_mirror, returned, returned_mirror = call(
        returned_body,
        "returned",
        (bits, hidden_in, x_mirror, attended, *grads, w_query, w_key, w_value, w_out),
        [bf16(seq_len, features)] * 4,
        flops=8 * tokens * features * half,
    )
    contrib_other = mirror(contrib_mirror)
    returned_other = mirror(returned_mirror)
    hidden_out = (
        hidden_in.astype(F32) + contrib.astype(F32) + contrib_other.astype(F32)
    ).astype(BF16)
    grad_in = (
        grad_out.astype(F32) + returned.astype(F32) + returned_other.astype(F32)
    ).astype(BF16)
    return (hidden_out, grad_in, grad_query, grad_key, grad_value, grad_wout)


def solution(mesh):
    in_specs = (
        P(("dp", "pipe"), None),
        P(("dp", "pipe"), None),
        P("pipe", None, None),
        P("pipe", None, None),
        P("pipe", None, None),
        P("pipe", None, None),
        P(),
    )
    out_specs = (
        P(("dp", "pipe"), None),
        P(("dp", "pipe"), None),
        P("pipe", "dp", None),
        P("pipe", "dp", None),
        P("pipe", "dp", None),
        P("pipe", "dp", None),
    )
    return jax.shard_map(
        on_device, mesh=mesh, in_specs=in_specs, out_specs=out_specs, check_vma=False
    )
```

time: 384 us -> 135 us (0.35)
  waiting for transfers between devices: 276 us -> 26.1 us
  starting transfers between devices: 1.56 us -> 40.7 us
  matrix products: 38.8 us -> 0 us
  Pallas kernels: 0 us -> 18.2 us
  other arithmetic: 23.5 us -> 5.54 us
  local copies, waits for them, and re-layouts: 29.2 us -> 42.9 us
  between operations: 14.1 us -> 1 us
    reduce_scatter x4 -> x0, waiting for transfers between devices: 276 us -> none  [the longest x1 78.3 us: on_device(): lax.psum_scatter(full_grads[3].astype(jnp.bfloat16), 'dp', scatter_dimens...]
    ppermute x4 -> x42, starting transfers between devices: 1.18 us -> 40.7 us  [the longest x30 38.6 us: swap(): return lax.ppermute(x, 'dp', [(i, i ^ 1 << bit) for i in range(replicas)])]
    unnamed x45 -> x108, local copies, waits for them, and re-layouts: 7.29 us -> 42.8 us
    dot_general x16 -> x0, matrix products: 35.1 us -> none  [the longest x4 9.55 us: contract(): lax.dot_general(left_factor, right_factor, (((0,), (0,)), ((), ())), pref...]
    ppermute x4 -> x42, waiting for transfers between devices: 0.01 us -> 26.1 us  [the longest x30 26 us: swap(): return lax.ppermute(x, 'dp', [(i, i ^ 1 << bit) for i in range(replicas)])]
    pallas_call x0 -> x7, Pallas kernels: none -> 18.2 us  [call(): pl.pallas_call(body, name=name, out_shape=outs, in_specs=specs, out_specs...]
    reshape x8 -> x0, local copies, waits for them, and re-layouts: 10.5 us -> none  [the longest x1 2.08 us: attend_backward(): grad_querypos.astype(jnp.bfloat16)]
    broadcast_in_dim x4 -> x0, other arithmetic: 6.52 us -> none  [the longest x1 1.63 us: on_device(): shares[1][None]]
  transfers between devices with their start and end apart: 8 -> 42, of which waited for: 4 -> 11; matrix products, arithmetic and copies ran while one was open for 12% -> 4% of each run, Pallas kernels for 0% -> 13%
where the time goes in v1:
time: 135 us; the launch traced here: 134 us
  local copies, waits for them, and re-layouts  42.9 us (32%)
  starting transfers between devices  40.7 us (30%)
  waiting for transfers between devices  26.1 us (19%)
  Pallas kernels  18.2 us (13%)
  other arithmetic  5.54 us (4%)
    unnamed x108, local copies, waits for them, and re-layouts  42.8 us
    ppermute x30, starting transfers between devices, swap(): return lax.ppermute(x, 'dp', [(i, i ^ 1 << bit) for i in range(replicas)])  38.6 us
    ppermute x30, waiting for transfers between devices, swap(): return lax.ppermute(x, 'dp', [(i, i ^ 1 << bit) for i in range(replicas)])  26 us
    pallas_call x7, Pallas kernels, call(): pl.pallas_call(body, name=name, out_shape=outs, in_specs=specs, out_specs...  18.2 us
    convert_element_type x4, other arithmetic, reduced(): return jnp.concatenate([low, high], axis=1).astype(F32)[None]  2.91 us
  transfers between devices with their start and end apart: 42, of which 11 were waited for; matrix products, arithmetic and copies ran while one was open for 4% of the time, Pallas kernels for 13%

profile of v1, /device:TPU:0, one launch (start us, length us, event | category | flops | bytes accessed | tf_op | source)
XLA Modules:
  0.0 134.3 jit_solution(13168264615940728850)
XLA Ops:
  3.6 3.1 %collective-permute-start.35 = (bf16[128,1024]{1,0:T(8,128)(2,1)S(1)}, bf16[128,1024]{1,0:T(8,128)(2,1)S(1)}, u32[]{:S(2)}, u32[]{:S(2)}) collective-permute-start(bf16[128,1024]{1,0:T(8,128)(2,1)S(1)} %get-tuple-element.53), channel_id=1, source_target_pairs={{0,8},{2,10},{4,12},{6,14},{8,0},{10,2},{12,4},{14,6},{16,24},{18,... | collective-permute-start | bytes 786440 | tf_op jit(solution)/shard_map/ppermute | solution.py:250
  9.4 3.6 %collective-permute-done.35.refs_8_ = bf16[128,1024]{1,0:T(8,128)(2,1)S(1)} collective-permute-done((bf16[128,1024]{1,0:T(8,128)(2,1)S(1)}, bf16[128,1024]{1,0:T(8,128)(2,1)S(1)}, u32[]{:S(2)}, u32[]{:S(2)}) %collective-permute-start.35) | collective-permute-done | bytes 262176 | tf_op jit(solution)/shard_map/ppermute | solution.py:250
  13.0 1.7 %collective-permute-start.5 = (bf16[1024,128]{1,0:T(8,128)(2,1)S(1)}, bf16[1024,128]{1,0:T(8,128)(2,1)S(1)}, u32[]{:S(2)}, u32[]{:S(2)}) collective-permute-start(bf16[1024,128]{1,0:T(8,128)(2,1)S(1)} %get-tuple-element.43), channel_id=1, source_target_pairs={{0,2},{2,0},{4,6},{6,4},{8,10},{10,8},{12,14},{14,12},{16,18},{18,... | collective-permute-start | bytes 786440 | tf_op jit(solution)/shard_map/ppermute | solution.py:250
  16.9 3.6 %collective-permute-done.5.refs_2_ = bf16[1024,128]{1,0:T(8,128)(2,1)S(1)} collective-permute-done((bf16[1024,128]{1,0:T(8,128)(2,1)S(1)}, bf16[1024,128]{1,0:T(8,128)(2,1)S(1)}, u32[]{:S(2)}, u32[]{:S(2)}) %collective-permute-start.5) | collective-permute-done | bytes 262176 | tf_op jit(solution)/shard_map/ppermute | solution.py:250
  28.3 1.6 %copy-done = bf16[1,2048,512]{2,1,0:T(8,128)(2,1)S(1)} copy-done((bf16[1,2048,512]{2,1,0:T(8,128)(2,1)S(1)}, bf16[1,2048,512]{2,1,0:T(8,128)(2,1)}, u32[]{:S(2)}) %copy-start) | copy-done | bytes 2097176
  29.9 1.6 %copy-done.2 = bf16[1,2048,512]{2,1,0:T(8,128)(2,1)S(1)} copy-done((bf16[1,2048,512]{2,1,0:T(8,128)(2,1)S(1)}, bf16[1,2048,512]{2,1,0:T(8,128)(2,1)}, u32[]{:S(2)}) %copy-start.2) | copy-done | bytes 2097176
  31.4 1.6 %copy-done.4 = bf16[1,2048,512]{2,1,0:T(8,128)(2,1)S(1)} copy-done((bf16[1,2048,512]{2,1,0:T(8,128)(2,1)S(1)}, bf16[1,2048,512]{2,1,0:T(8,128)(2,1)}, u32[]{:S(2)}) %copy-start.4) | copy-done | bytes 2097176
  33.0 1.6 %copy-done.6 = bf16[1,512,2048]{2,1,0:T(8,128)(2,1)S(1)} copy-done((bf16[1,512,2048]{2,1,0:T(8,128)(2,1)S(1)}, bf16[1,512,2048]{2,1,0:T(8,128)(2,1)}, u32[]{:S(2)}) %copy-start.6) | copy-done | bytes 2097176
  37.4 6.9 %attention.1 = (bf16[256,512]{1,0:T(8,128)(2,1)S(1)}, bf16[256,256]{1,0:T(8,128)(2,1)S(1)}, bf16[256,256]{1,0:T(8,128)(2,1)S(1)}, bf16[256,256]{1,0:T(8,128)(2,1...) custom-call(s32[3]{0:T(128)S(1)} %pad_add_fusion.bits, ...), custom_call_target="tpu_custom_call" | custom-call | flops 2147483648 | bytes 11796540 | tf_op jit(solution)/shard_map/attention/pallas_call | solution.py:42
  78.8 1.6 %copy-done.3 = bf16[1,2048,512]{2,1,0:T(8,128)(2,1)S(1)} copy-done((bf16[1,2048,512]{2,1,0:T(8,128)(2,1)S(1)}, bf16[1,2048,512]{2,1,0:T(8,128)(2,1)}, u32[]{:S(2)}) %copy-start.3) | copy-done | bytes 2097176
  80.4 1.6 %copy-done.5 = bf16[1,2048,512]{2,1,0:T(8,128)(2,1)S(1)} copy-done((bf16[1,2048,512]{2,1,0:T(8,128)(2,1)S(1)}, bf16[1,2048,512]{2,1,0:T(8,128)(2,1)}, u32[]{:S(2)}) %copy-start.5) | copy-done | bytes 2097176
  82.0 1.6 %copy-done.7 = bf16[1,512,2048]{2,1,0:T(8,128)(2,1)S(1)} copy-done((bf16[1,512,2048]{2,1,0:T(8,128)(2,1)S(1)}, bf16[1,512,2048]{2,1,0:T(8,128)(2,1)}, u32[]{:S(2)}) %copy-start.7) | copy-done | bytes 2097176
  87.4 3.8 %returned.1 = (bf16[128,2048]{1,0:T(8,128)(2,1)S(1)}, bf16[128,2048]{1,0:T(8,128)(2,1)S(1)}, bf16[128,2048]{1,0:T(8,128)(2,1)S(1)}, bf16[128,2048]{1,0:T(8,128)(2,1)S(1)}) custom-call(s32[3]{0:T(128)S(1)} %pad_add_fusion.bits, bf16[128,2048]{1,0:T(8,128)(2,1)S(1)} %copy-done.10, bf16[128,2048]{1,0:T(8,128)(2,1)S(1)} %copy-done.21, ...), custom_call_target="tpu_custom_call" | custom-call | flops 2147483648 | bytes 12582924 | tf_op jit(solution)/shard_map/returned/pallas_call | solution.py:42
  91.2 2.0 %grad_value.1 = (bf16[512,256]{1,0:T(8,128)(2,1)S(1)}, bf16[512,256]{1,0:T(8,128)(2,1)S(1)}) custom-call(s32[3]{0:T(128)S(1)} %pad_add_fusion.bits, bf16[1024,128]{1,0:T(8,128)(2,1)S(1)} %get-tuple-element.42.refs_0_, bf16[1024,128]{1,0:T(8,128)(2,1)S(1)} %copy-done.15, bf16[1024,128]{1,0:T(8,128)(2,1)S(1)} %collective-permute-done.5.refs_2_, ...), custom_call_target="tpu_custom_call" | custom-call | flops 536870912 | bytes 3145740 | tf_op jit(solution)/shard_map/grad_value/pallas_call | solution.py:42
  93.7 1.8 %grad_key.1 = (bf16[512,256]{1,0:T(8,128)(2,1)S(1)}, bf16[512,256]{1,0:T(8,128)(2,1)S(1)}) custom-call(s32[3]{0:T(128)S(1)} %pad_add_fusion.bits, bf16[1024,128]{1,0:T(8,128)(2,1)S(1)} %get-tuple-element.42.refs_0_, bf16[1024,128]{1,0:T(8,128)(2,1)S(1)} %copy-done.15, bf16[1024,128]{1,0:T(8,128)(2,1)S(1)} %collective-permute-done.5.refs_2_, ...), custom_call_target="tpu_custom_call" | custom-call | flops 536870912 | bytes 3145740 | tf_op jit(solution)/shard_map/grad_key/pallas_call | solution.py:42
  97.6 1.8 %grad_query.1 = (bf16[512,256]{1,0:T(8,128)(2,1)S(1)}, bf16[512,256]{1,0:T(8,128)(2,1)S(1)}) custom-call(s32[3]{0:T(128)S(1)} %pad_add_fusion.bits, bf16[1024,128]{1,0:T(8,128)(2,1)S(1)} %get-tuple-element.42.refs_0_, bf16[1024,128]{1,0:T(8,128)(2,1)S(1)} %copy-done.15, bf16[1024,128]{1,0:T(8,128)(2,1)S(1)} %collective-permute-done.5.refs_2_, ...), custom_call_target="tpu_custom_call" | custom-call | flops 536870912 | bytes 3145740 | tf_op jit(solution)/shard_map/grad_query/pallas_call | solution.py:42
  100.1 4.7 %collective-permute-done.26 = bf16[512,256]{1,0:T(8,128)(2,1)S(1)} collective-permute-done((bf16[512,256]{1,0:T(8,128)(2,1)S(1)}, bf16[512,256]{1,0:T(8,128)(2,1)S(1)}, u32[]{:S(2)}, u32[]{:S(2)}) %collective-permute-start.26) | collective-permute-done | bytes 262176 | tf_op jit(solution)/shard_map/ppermute | solution.py:250
  104.8 2.6 %collective-permute-start.40 = (bf16[64,1024]{1,0:T(8,128)(2,1)S(1)}, bf16[64,1024]{1,0:T(8,128)(2,1)S(1)}, u32[]{:S(2)}, u32[]{:S(2)}) collective-permute-start(bf16[64,1024]{1,0:T(8,128)(2,1)S(1)} %dynamic-slice_bitcast_fusion), channel_id=1, source_target_pairs={{0,16},{2,18},{4,20},{6,22},{8,24},{10,26},{12,28},{14,30},{16,0},... | collective-permute-start | bytes 393224 | tf_op jit(solution)/shard_map/ppermute | solution.py:250
  107.4 2.9 %collective-permute-done.20 = bf16[512,256]{1,0:T(8,128)(2,1)S(1)} collective-permute-done((bf16[512,256]{1,0:T(8,128)(2,1)S(1)}, bf16[512,256]{1,0:T(8,128)(2,1)S(1)}, u32[]{:S(2)}, u32[]{:S(2)}) %collective-permute-start.20) | collective-permute-done | bytes 262176 | tf_op jit(solution)/shard_map/ppermute | solution.py:250
  110.4 2.6 %collective-permute-start.27 = (bf16[256,256]{1,0:T(8,128)(2,1)S(1)}, bf16[256,256]{1,0:T(8,128)(2,1)S(1)}, u32[]{:S(2)}, u32[]{:S(2)}) collective-permute-start(bf16[256,256]{1,0:T(8,128)(2,1)S(1)} %dynamic-slice_bitcast_fusion.1), channel_id=1, source_target_pairs={{0,16},{2,18},{4,20},{6,22},{8,24},{10,26},{12,28},{14,30},{16,0},... | collective-permute-start | bytes 393224 | tf_op jit(solution)/shard_map/ppermute | solution.py:250
  113.1 2.1 %collective-permute-done.14 = bf16[512,256]{1,0:T(8,128)(2,1)S(1)} collective-permute-done((bf16[512,256]{1,0:T(8,128)(2,1)S(1)}, bf16[512,256]{1,0:T(8,128)(2,1)S(1)}, u32[]{:S(2)}, u32[]{:S(2)}) %collective-permute-start.14) | collective-permute-done | bytes 262176 | tf_op jit(solution)/shard_map/ppermute | solution.py:250
  115.1 2.6 %collective-permute-start.21 = (bf16[256,256]{1,0:T(8,128)(2,1)S(1)}, bf16[256,256]{1,0:T(8,128)(2,1)S(1)}, u32[]{:S(2)}, u32[]{:S(2)}) collective-permute-start(bf16[256,256]{1,0:T(8,128)(2,1)S(1)} %dynamic-slice_bitcast_fusion.2), channel_id=1, source_target_pairs={{0,16},{2,18},{4,20},{6,22},{8,24},{10,26},{12,28},{14,30},{16,0},... | collective-permute-start | bytes 393224 | tf_op jit(solution)/shard_map/ppermute | solution.py:250
  122.6 4.4 %collective-permute-done.21 = bf16[256,256]{1,0:T(8,128)(2,1)S(1)} collective-permute-done((bf16[256,256]{1,0:T(8,128)(2,1)S(1)}, bf16[256,256]{1,0:T(8,128)(2,1)S(1)}, u32[]{:S(2)}, u32[]{:S(2)}) %collective-permute-start.21) | collective-permute-done | bytes 131104 | tf_op jit(solution)/shard_map/ppermute | solution.py:250
  127.3 1.9 %collective-permute-done.15 = bf16[256,256]{1,0:T(8,128)(2,1)S(1)} collective-permute-done((bf16[256,256]{1,0:T(8,128)(2,1)S(1)}, bf16[256,256]{1,0:T(8,128)(2,1)S(1)}, u32[]{:S(2)}, u32[]{:S(2)}) %collective-permute-start.15) | collective-permute-done | bytes 131104 | tf_op jit(solution)/shard_map/ppermute | solution.py:250
  (202 shorter events, 70.5 us)
Async XLA Ops:
  8.9 15.6 %collective-permute-start = (bf16[128,2048]{1,0:T(8,128)(2,1)S(1)}, bf16[128,2048]{1,0:T(8,128)(2,1)S(1)}, u32[]{:S(2)}, u32[]{:S(2)}) collective-permute-start(bf16[128,2048]{1,0:T(8,128)(2,1)S(1)} %copy-done.8), channel_id=1, source_target_pairs={{0,1},{1,0},{2,3},{3,2},{4,5},{5,4},{6,7},{7,6},{8,9},{9,8},{10,11... | collective-permute-start | bytes 1572872 | tf_op jit(solution)/shard_map/ppermute | solution.py:253
  9.4 16.6 %collective-permute-start.1 = (bf16[128,2048]{1,0:T(8,128)(2,1)S(1)}, bf16[128,2048]{1,0:T(8,128)(2,1)S(1)}, u32[]{:S(2)}, u32[]{:S(2)}) collective-permute-start(bf16[128,2048]{1,0:T(8,128)(2,1)S(1)} %copy-done.11), channel_id=1, source_target_pairs={{0,1},{1,0},{2,3},{3,2},{4,5},{5,4},{6,7},{7,6},{8,9},{9,8},{10,11... | collective-permute-start | bytes 1572872 | tf_op jit(solution)/shard_map/ppermute | solution.py:253
  23.2 22.4 %collective-permute-start.36 = (bf16[128,1024]{1,0:T(8,128)(2,1)S(1)}, bf16[128,1024]{1,0:T(8,128)(2,1)S(1)}, u32[]{:S(2)}, u32[]{:S(2)}) collective-permute-start(bf16[128,1024]{1,0:T(8,128)(2,1)S(1)} %collective-permute-done.35.refs_8_), channel_id=1, source_target_pairs={{0,1},{1,0},{2,3},{3,2},{4,5},{5,4},{6,7},{7,6},{8,9},{9,8},{10,11... | collective-permute-start | bytes 786440 | tf_op jit(solution)/shard_map/ppermute | solution.py:253
  24.4 23.0 %collective-permute-start.9 = (bf16[1024,128]{1,0:T(8,128)(2,1)S(1)}, bf16[1024,128]{1,0:T(8,128)(2,1)}, u32[]{:S(2)}, u32[]{:S(2)}) collective-permute-start(bf16[1024,128]{1,0:T(8,128)(2,1)S(1)} %collective-permute-done.5.refs_2_), channel_id=1, source_target_pairs={{0,8},{2,10},{4,12},{6,14},{8,0},{10,2},{12,4},{14,6},{16,24},{18,... | collective-permute-start | bytes 786440 | tf_op jit(solution)/shard_map/ppermute | solution.py:250
  26.0 25.5 %collective-permute-start.6 = (bf16[1024,128]{1,0:T(8,128)(2,1)S(1)}, bf16[1024,128]{1,0:T(8,128)(2,1)S(1)}, u32[]{:S(2)}, u32[]{:S(2)}) collective-permute-start(bf16[1024,128]{1,0:T(8,128)(2,1)S(1)} %collective-permute-done.5.refs_2_), channel_id=1, source_target_pairs={{0,1},{1,0},{2,3},{3,2},{4,5},{5,4},{6,7},{7,6},{8,9},{9,8},{10,11... | collective-permute-start | bytes 786440 | tf_op jit(solution)/shard_map/ppermute | solution.py:253
  27.1 22.7 %collective-permute-start.8 = (bf16[1024,128]{1,0:T(8,128)(2,1)S(1)}, bf16[1024,128]{1,0:T(8,128)(2,1)S(1)}, u32[]{:S(2)}, u32[]{:S(2)}) collective-permute-start(bf16[1024,128]{1,0:T(8,128)(2,1)S(1)} %collective-permute-done.7.refs_4_), channel_id=1, source_target_pairs={{0,1},{1,0},{2,3},{3,2},{4,5},{5,4},{6,7},{7,6},{8,9},{9,8},{10,11... | collective-permute-start | bytes 786440 | tf_op jit(solution)/shard_map/ppermute | solution.py:253
  27.8 29.4 %collective-permute-start.38 = (bf16[128,1024]{1,0:T(8,128)(2,1)S(1)}, bf16[128,1024]{1,0:T(8,128)(2,1)S(1)}, u32[]{:S(2)}, u32[]{:S(2)}) collective-permute-start(bf16[128,1024]{1,0:T(8,128)(2,1)S(1)} %collective-permute-done.37.refs_10_), channel_id=1, source_target_pairs={{0,1},{1,0},{2,3},{3,2},{4,5},{5,4},{6,7},{7,6},{8,9},{9,8},{10,11... | collective-permute-start | bytes 786440 | tf_op jit(solution)/shard_map/ppermute | solution.py:253
  52.2 23.7 %collective-permute-start.10 = (bf16[1024,128]{1,0:T(8,128)(2,1)}, bf16[1024,128]{1,0:T(8,128)(2,1)}, u32[]{:S(2)}, u32[]{:S(2)}) collective-permute-start(bf16[1024,128]{1,0:T(8,128)(2,1)} %collective-permute-done.9.refs_6_), channel_id=1, source_target_pairs={{0,1},{1,0},{2,3},{3,2},{4,5},{5,4},{6,7},{7,6},{8,9},{9,8},{10,11... | collective-permute-start | bytes 786440 | tf_op jit(solution)/shard_map/ppermute | solution.py:253
  55.2 18.0 %collective-permute-start.23 = (bf16[256,256]{1,0:T(8,128)(2,1)}, bf16[256,256]{1,0:T(8,128)(2,1)}, u32[]{:S(2)}, u32[]{:S(2)}) collective-permute-start(bf16[256,256]{1,0:T(8,128)(2,1)} %get-tuple-element.32.value_keep.refs_8_), channel_id=1, source_target_pairs={{0,2},{2,0},{4,6},{6,4},{8,10},{10,8},{12,14},{14,12},{16,18},{18,... | collective-permute-start | bytes 393224 | tf_op jit(solution)/shard_map/ppermute | solution.py:250
  55.8 18.0 %collective-permute-start.18 = (bf16[256,256]{1,0:T(8,128)(2,1)}, bf16[256,256]{1,0:T(8,128)(2,1)}, u32[]{:S(2)}, u32[]{:S(2)}) collective-permute-start(bf16[256,256]{1,0:T(8,128)(2,1)} %get-tuple-element.35.key_send), channel_id=1, source_target_pairs={{0,8},{2,10},{4,12},{6,14},{8,0},{10,2},{12,4},{14,6},{16,24},{18,... | collective-permute-start | bytes 393224 | tf_op jit(solution)/shard_map/ppermute | solution.py:250
  57.9 17.3 %collective-permute-start.12 = (bf16[256,256]{1,0:T(8,128)(2,1)}, bf16[256,256]{1,0:T(8,128)(2,1)}, u32[]{:S(2)}, u32[]{:S(2)}) collective-permute-start(bf16[256,256]{1,0:T(8,128)(2,1)} %get-tuple-element.37.query_send), channel_id=1, source_target_pairs={{0,8},{2,10},{4,12},{6,14},{8,0},{10,2},{12,4},{14,6},{16,24},{18,... | collective-permute-start | bytes 393224 | tf_op jit(solution)/shard_map/ppermute | solution.py:250
  59.3 18.0 %collective-permute-start.25 = (bf16[256,256]{1,0:T(8,128)(2,1)}, bf16[256,256]{1,0:T(8,128)(2,1)}, u32[]{:S(2)}, u32[]{:S(2)}) collective-permute-start(bf16[256,256]{1,0:T(8,128)(2,1)} %collective-permute-done.24.refs_10_), channel_id=1, source_target_pairs={{0,2},{2,0},{4,6},{6,4},{8,10},{10,8},{12,14},{14,12},{16,18},{18,... | collective-permute-start | bytes 393224 | tf_op jit(solution)/shard_map/ppermute | solution.py:250
  73.1 20.0 %collective-permute-start.17 = (bf16[256,256]{1,0:T(8,128)(2,1)}, bf16[256,256]{1,0:T(8,128)(2,1)S(1)}, u32[]{:S(2)}, u32[]{:S(2)}) collective-permute-start(bf16[256,256]{1,0:T(8,128)(2,1)} %copy-done.22), channel_id=1, source_target_pairs={{0,2},{2,0},{4,6},{6,4},{8,10},{10,8},{12,14},{14,12},{16,18},{18,... | collective-permute-start | bytes 393224 | tf_op jit(solution)/shard_map/ppermute | solution.py:250
  73.9 21.6 %collective-permute-start.11 = (bf16[256,256]{1,0:T(8,128)(2,1)S(1)}, bf16[256,256]{1,0:T(8,128)(2,1)S(1)}, u32[]{:S(2)}, u32[]{:S(2)}) collective-permute-start(bf16[256,256]{1,0:T(8,128)(2,1)S(1)} %get-tuple-element.36.query_keep.refs_8_), channel_id=1, source_target_pairs={{0,2},{2,0},{4,6},{6,4},{8,10},{10,8},{12,14},{14,12},{16,18},{18,... | collective-permute-start | bytes 393224 | tf_op jit(solution)/shard_map/ppermute | solution.py:250
  75.2 18.0 %collective-permute-start.19 = (bf16[256,256]{1,0:T(8,128)(2,1)}, bf16[256,256]{1,0:T(8,128)(2,1)S(1)}, u32[]{:S(2)}, u32[]{:S(2)}) collective-permute-start(bf16[256,256]{1,0:T(8,128)(2,1)} %collective-permute-done.18.refs_10_), channel_id=1, source_target_pairs={{0,2},{2,0},{4,6},{6,4},{8,10},{10,8},{12,14},{14,12},{16,18},{18,... | collective-permute-start | bytes 393224 | tf_op jit(solution)/shard_map/ppermute | solution.py:250
  75.9 20.2 %collective-permute-start.13 = (bf16[256,256]{1,0:T(8,128)(2,1)}, bf16[256,256]{1,0:T(8,128)(2,1)S(1)}, u32[]{:S(2)}, u32[]{:S(2)}) collective-permute-start(bf16[256,256]{1,0:T(8,128)(2,1)} %collective-permute-done.12.refs_10_), channel_id=1, source_target_pairs={{0,2},{2,0},{4,6},{6,4},{8,10},{10,8},{12,14},{14,12},{16,18},{18,... | collective-permute-start | bytes 393224 | tf_op jit(solution)/shard_map/ppermute | solution.py:250
  77.3 22.1 %collective-permute-start.39 = (bf16[128,1024]{1,0:T(8,128)(2,1)S(1)}, bf16[128,1024]{1,0:T(8,128)(2,1)S(1)}, u32[]{:S(2)}, u32[]{:S(2)}) collective-permute-start(bf16[128,1024]{1,0:T(8,128)(2,1)S(1)} %get-tuple-element.55), channel_id=1, source_target_pairs={{0,4},{2,6},{4,0},{6,2},{8,12},{10,14},{12,8},{14,10},{16,20},{18,... | collective-permute-start | bytes 786440 | tf_op jit(solution)/shard_map/ppermute | solution.py:250
  93.1 24.7 %collective-permute-start.3 = (bf16[128,2048]{1,0:T(8,128)(2,1)S(1)}, bf16[128,2048]{1,0:T(8,128)(2,1)S(1)}, u32[]{:S(2)}, u32[]{:S(2)}) collective-permute-start(bf16[128,2048]{1,0:T(8,128)(2,1)S(1)} %get-tuple-element.41), channel_id=1, source_target_pairs={{0,1},{1,0},{2,3},{3,2},{4,5},{5,4},{6,7},{7,6},{8,9},{9,8},{10,11... | collective-permute-start | bytes 1572872 | tf_op jit(solution)/shard_map/ppermute | solution.py:253
  93.2 26.0 %collective-permute-start.2 = (bf16[128,2048]{1,0:T(8,128)(2,1)S(1)}, bf16[128,2048]{1,0:T(8,128)(2,1)S(1)}, u32[]{:S(2)}, u32[]{:S(2)}) collective-permute-start(bf16[128,2048]{1,0:T(8,128)(2,1)S(1)} %get-tuple-element.39), channel_id=1, source_target_pairs={{0,1},{1,0},{2,3},{3,2},{4,5},{5,4},{6,7},{7,6},{8,9},{9,8},{10,11... | collective-permute-start | bytes 1572872 | tf_op jit(solution)/shard_map/ppermute | solution.py:253
  96.1 14.3 %collective-permute-start.20 = (bf16[512,256]{1,0:T(8,128)(2,1)S(1)}, bf16[512,256]{1,0:T(8,128)(2,1)S(1)}, u32[]{:S(2)}, u32[]{:S(2)}) collective-permute-start(bf16[512,256]{1,0:T(8,128)(2,1)S(1)} %get-tuple-element.47), channel_id=1, source_target_pairs={{0,4},{2,6},{4,0},{6,2},{8,12},{10,14},{12,8},{14,10},{16,20},{18,... | collective-permute-start | bytes 786440 | tf_op jit(solution)/shard_map/ppermute | solution.py:250
  99.4 15.7 %collective-permute-start.14 = (bf16[512,256]{1,0:T(8,128)(2,1)S(1)}, bf16[512,256]{1,0:T(8,128)(2,1)S(1)}, u32[]{:S(2)}, u32[]{:S(2)}) collective-permute-start(bf16[512,256]{1,0:T(8,128)(2,1)S(1)} %get-tuple-element.45), channel_id=1, source_target_pairs={{0,4},{2,6},{4,0},{6,2},{8,12},{10,14},{12,8},{14,10},{16,20},{18,... | collective-permute-start | bytes 786440 | tf_op jit(solution)/shard_map/ppermute | solution.py:250
  104.8 15.5 %collective-permute-start.40 = (bf16[64,1024]{1,0:T(8,128)(2,1)S(1)}, bf16[64,1024]{1,0:T(8,128)(2,1)S(1)}, u32[]{:S(2)}, u32[]{:S(2)}) collective-permute-start(bf16[64,1024]{1,0:T(8,128)(2,1)S(1)} %dynamic-slice_bitcast_fusion), channel_id=1, source_target_pairs={{0,16},{2,18},{4,20},{6,22},{8,24},{10,26},{12,28},{14,30},{16,0},... | collective-permute-start | bytes 393224 | tf_op jit(solution)/shard_map/ppermute | solution.py:250
  115.1 11.9 %collective-permute-start.21 = (bf16[256,256]{1,0:T(8,128)(2,1)S(1)}, bf16[256,256]{1,0:T(8,128)(2,1)S(1)}, u32[]{:S(2)}, u32[]{:S(2)}) collective-permute-start(bf16[256,256]{1,0:T(8,128)(2,1)S(1)} %dynamic-slice_bitcast_fusion.2), channel_id=1, source_target_pairs={{0,16},{2,18},{4,20},{6,22},{8,24},{10,26},{12,28},{14,30},{16,0},... | collective-permute-start | bytes 393224 | tf_op jit(solution)/shard_map/ppermute | solution.py:250
  117.8 11.4 %collective-permute-start.15 = (bf16[256,256]{1,0:T(8,128)(2,1)S(1)}, bf16[256,256]{1,0:T(8,128)(2,1)S(1)}, u32[]{:S(2)}, u32[]{:S(2)}) collective-permute-start(bf16[256,256]{1,0:T(8,128)(2,1)S(1)} %dynamic-slice_bitcast_fusion.3), channel_id=1, source_target_pairs={{0,16},{2,18},{4,20},{6,22},{8,24},{10,26},{12,28},{14,30},{16,0},... | collective-permute-start | bytes 393224 | tf_op jit(solution)/shard_map/ppermute | solution.py:250
  (72 other events, 308.2 us)

commit v2 on v1

v2 whole, which is shorter than its diff:
```python
import functools
import math

import jax
import jax.numpy as jnp
from jax import lax
from jax.experimental import pallas as pl
from jax.experimental.pallas import tpu as pltpu
from jax.sharding import PartitionSpec as P

HDIM = 64
NORM_EPS = 1e-05
PAIR = 2 * HDIM
VMEM_BYTES = 62 * 1024 * 1024

F32 = jnp.float32
BF16 = jnp.bfloat16
NT = (((1,), (1,)), ((), ()))
TN = (((0,), (0,)), ((), ()))

ROW_BIT = 0
COL_BIT = 2

CHUNKS = ((True, (0,)), (False, (1,)), (False, (2,)))


def dot(left, right):
    return jnp.dot(left, right, preferred_element_type=F32)


def dot_nt(left, right):
    return lax.dot_general(left, right, NT, preferred_element_type=F32)


def dot_tn(left, right):
    return lax.dot_general(left, right, TN, preferred_element_type=F32)


def call(body, name, inputs, outs, scratch=(), flops=0, scalars=1, far=0):
    near = len(inputs) - scalars - far
    specs = [pl.BlockSpec(memory_space=pltpu.SMEM)] * scalars
    specs += [pl.BlockSpec(memory_space=pltpu.VMEM)] * near
    specs += [pl.BlockSpec(memory_space=pltpu.HBM)] * far
    moved = sum(x.size * x.dtype.itemsize for x in inputs)
    moved += sum(x.size * x.dtype.itemsize for x in outs)
    return pl.pallas_call(
        body,
        name=name,
        out_shape=outs,
        in_specs=specs,
        out_specs=[pl.BlockSpec(memory_space=pltpu.VMEM)] * len(outs),
        scratch_shapes=list(scratch),
        compiler_params=pltpu.CompilerParams(vmem_limit_bytes=VMEM_BYTES),
        cost_estimate=pl.CostEstimate(flops=flops, bytes_accessed=moved, transcendentals=0),
    )(*inputs)


def fetch(pairs, sems):
    copies = [
        pltpu.make_async_copy(source, target, sems.at[place])
        for place, (source, target) in enumerate(pairs)
    ]
    for copy in copies:
        copy.start()
    return copies


def finish(copies):
    for copy in copies:
        copy.wait()


def row_chunks(bit_count, halved_bits):
    order = list(halved_bits) + [COL_BIT]
    chunks = []
    for index in range(1 << len(order)):
        chunk = 0
        for place, bit in enumerate(reversed(order)):
            chunk |= ((index >> place) & 1) << bit
        chunks.append(chunk)
    return chunks


def copy_chunks(source, target, first, chunks, size, row_bit):
    for place, chunk in enumerate(chunks):
        start = pl.multiple_of((chunk + (row_bit << ROW_BIT)) * size, size)
        here = first + place * size
        target[here : here + size, :] = source[pl.ds(start, size), :]


def prep_body(
    chunks, bits, hidden, grad, keep, by_row, by_col, x, g, turned_x, turned_g, sems
):
    row_bit, col_bit = bits[0], bits[1]
    features, seq_len = turned_x.shape
    size = features // (2 * len(chunks))
    part = features // 2
    x_copy, g_copy = fetch([(hidden, x), (grad, g)], sems)
    x_copy.wait()
    turned_x[...] = x[...].astype(F32).T.astype(BF16)
    copy_chunks(turned_x, by_row, 0, chunks, size, 1 - row_bit)
    copy_chunks(turned_x, by_col, part, chunks, size, row_bit)
    g_copy.wait()
    turned_g[...] = g[...].astype(F32).T.astype(BF16)
    by_row[part:, :] = turned_g[pl.ds(pl.multiple_of(col_bit * part, part), part), :]
    by_col[:part, :] = turned_g[pl.ds(pl.multiple_of((1 - col_bit) * part, part), part), :]
    keep[:part, :] = by_col[part:, :]
    keep[part:, :] = by_row[part:, :]


def seen_mask(pattern, seq_len, blocks, slots):
    block_len = seq_len // blocks
    rows = lax.broadcasted_iota(jnp.int32, (seq_len, seq_len), 0)
    columns = lax.broadcasted_iota(jnp.int32, (seq_len, seq_len), 1)
    row_block, column_block = rows // block_len, columns // block_len
    seen = jnp.zeros((seq_len, seq_len), F32)
    for block in range(blocks):
        for slot in range(slots):
            hit = (row_block == block) & (column_block == pattern[block, slot])
            seen = jnp.where(hit, 1.0, seen)
    return jnp.where((row_block == column_block) & (columns > rows), 0.0, seen)


def scale_of(x):
    return lax.rsqrt(jnp.mean(x * x, axis=-1, keepdims=True) + NORM_EPS)


def attention_body(
    chunks,
    bits,
    pattern,
    x_own,
    x_mirror,
    w_query,
    w_key,
    w_value,
    g_own,
    g_mirror,
    w_out,
    attended,
    *rest,
):
    sends = rest[: 2 * len(CHUNKS)]
    x_all, weights, weight_out, g_all, query, key, values, grad_att, turned, sems = rest[
        2 * len(CHUNKS) :
    ]
    row_bit, col_bit = bits[0], bits[1]
    seq_len = x_own.shape[0]
    tokens = 2 * seq_len
    half = w_query.shape[1]
    own, other = pl.ds(0, seq_len), pl.ds(seq_len, seq_len)
    copies = fetch(
        [
            (x_own, x_all.at[own]),
            (x_mirror, x_all.at[other]),
            (w_query, weights.at[0]),
            (w_key, weights.at[1]),
            (w_value, weights.at[2]),
            (g_own, g_all.at[own]),
            (g_mirror, g_all.at[other]),
            (w_out, weight_out),
        ],
        sems,
    )
    finish(copies[:2])
    x = x_all[...]
    factor = scale_of(x.astype(F32))
    for place, target in enumerate((query, key, values)):
        copies[2 + place].wait()
        target[...] = (dot(x, weights[place]) * factor).astype(BF16)
    finish(copies[5:])
    grad_att[...] = dot_nt(g_all[...], weight_out[...]).astype(BF16)

    seen = seen_mask(pattern, seq_len, pattern.shape[0], pattern.shape[1])
    seen = jnp.concatenate([seen, seen], axis=0) > 0.0
    low = lax.broadcasted_iota(jnp.int32, (seq_len, PAIR), 1) < HDIM
    inv_sqrt = 1.0 / math.sqrt(HDIM)
    zero = jnp.zeros((), BF16)

    def stacked(block):
        return jnp.concatenate([jnp.where(low, block, zero), jnp.where(low, zero, block)], axis=0)

    def merged(both):
        return jnp.where(low, both[:seq_len], both[seq_len:])

    width = half // 2
    places = {}
    att_place = None
    for (has_out, members), by_row, by_col in zip(CHUNKS, sends[::2], sends[1::2]):
        for place, member in enumerate(members):
            places[member] = (by_row, by_col, place * tokens)
        if has_out:
            att_place = (by_row, by_col, len(members) * tokens)

    for outs_at, side in ((0, col_bit), (1, 1 - col_bit)):
        for pair in range(width // PAIR):
            columns = pl.ds(pl.multiple_of(side * width + pair * PAIR, PAIR), PAIR)
            here = slice(pair * PAIR, (pair + 1) * PAIR)
            for seq in range(2):
                rows = slice(seq * seq_len, (seq + 1) * seq_len)
                q2 = stacked(query[rows, columns])
                k = key[rows, columns]
                v = values[rows, columns]
                ga2 = stacked(grad_att[rows, columns])
                r = factor[rows]

                def put(member, value):
                    target, first = places[member][outs_at], places[member][2] + seq * seq_len
                    target[first : first + seq_len, here] = (value * r).astype(BF16)

                expo = jnp.where(seen, jnp.exp(dot_nt(q2, k) * inv_sqrt), 0.0)
                prob = expo / jnp.sum(expo, axis=-1, keepdims=True)
                prob_bf = prob.astype(BF16)
                attended[rows, columns] = merged(dot(prob_bf, v)).astype(BF16)
                grad_prob = dot_nt(ga2, v)
                inner = jnp.sum(prob * grad_prob, axis=-1, keepdims=True)
                score = (prob * (grad_prob - inner) * inv_sqrt).astype(BF16)
                put(0, dot_tn(prob_bf, ga2))
                put(1, dot_tn(score, q2))
                put(2, merged(dot(score, k)))

    turned[...] = attended[...].astype(F32).T.astype(BF16)
    size = half // (2 * len(chunks))
    copy_chunks(turned, att_place[0], att_place[2], chunks, size, 1 - row_bit)
    copy_chunks(turned, att_place[1], att_place[2], chunks, size, row_bit)


def returned_body(bits, x_own, x_mirror, attended, w_out, w_query, w_key, w_value, *rest):
    sends = rest[: 2 * len(CHUNKS)]
    contrib_own, contrib_mirror, returned_own, returned_mirror = rest[
        2 * len(CHUNKS) : 2 * len(CHUNKS) + 4
    ]
    x_all, att, weight_out, weights, grads, sems = rest[2 * len(CHUNKS) + 4 :]
    col_bit = bits[1]
    seq_len = x_own.shape[0]
    tokens, half = att.shape
    width = half // 2
    keep = pl.ds(pl.multiple_of(col_bit * width, width), width)
    send = pl.ds(pl.multiple_of((1 - col_bit) * width, width), width)
    pairs = [
        (attended, att),
        (w_out, weight_out),
        (x_own, x_all.at[pl.ds(0, seq_len)]),
        (x_mirror, x_all.at[pl.ds(seq_len, seq_len)]),
    ]
    for (_, members), by_row, by_col in zip(CHUNKS, sends[::2], sends[1::2]):
        for place, member in enumerate(members):
            rows = pl.ds(place * tokens, tokens)
            pairs.append((by_row.at[rows], grads.at[member, :, keep]))
            pairs.append((by_col.at[rows], grads.at[member, :, send]))
    pairs += [(w_value, weights.at[0]), (w_key, weights.at[1]), (w_query, weights.at[2])]
    copies = fetch(pairs, sems)
    finish(copies[:2])
    contrib = dot(att[...], weight_out[...]).astype(BF16)
    contrib_own[...] = contrib[:seq_len]
    contrib_mirror[...] = contrib[seq_len:]
    finish(copies[2:-3])
    grad = None
    for member in range(3):
        copies[member - 3].wait()
        term = dot_nt(grads[member], weights[member])
        grad = term if grad is None else grad + term
    x = x_all[...].astype(F32)
    factor = scale_of(x)
    mean_term = jnp.mean(x * grad, axis=-1, keepdims=True)
    returned = (grad - x * (factor * factor * mean_term)).astype(BF16)
    returned_own[...] = returned[:seq_len]
    returned_mirror[...] = returned[seq_len:]


def weight_grad_body(chunk, size, out_size, bits, *refs):
    has_out, members = chunk
    x_pieces, refs = refs[:8], refs[8:]
    g_pieces, refs = refs[:4], refs[4:]
    if has_out:
        out_pieces, att_pieces, refs = refs[:8], refs[8:12], refs[12:]
        send, keep, x_all, right, att, out_right, sems = refs
    else:
        send, keep, x_all, right, sems = refs
    width = send.shape[1]
    count = len(members)
    seq_len = x_all.shape[1] // 8
    tokens = 2 * seq_len
    rows = x_all.shape[0] // 2
    first_bit = bits[2]
    pairs = []

    def add(ref, first, extent, target):
        pairs.append((ref.at[pl.ds(first, extent)], target))

    for place, (ref, first) in enumerate(x_pieces):
        add(ref, first, 2 * rows, x_all.at[:, pl.ds(place * seq_len, seq_len)])
    for place, (ref, first) in enumerate(g_pieces):
        for at in range(count):
            target = right.at[pl.ds(place * tokens, tokens), pl.ds(at * width, width)]
            add(ref, first + at * tokens, tokens, target)
    if has_out:
        for place, (ref, first) in enumerate(out_pieces):
            add(ref, first, out_right.shape[0], out_right.at[:, pl.ds(place * seq_len, seq_len)])
        for place, (ref, first) in enumerate(att_pieces):
            add(ref, first, att.shape[0], att.at[:, pl.ds(place * tokens, tokens)])
    finish(fetch(pairs, sems))

    finals = rows // size
    blocks = out_right.shape[0] // width if has_out else 0
    total = count * size + blocks * out_size
    for target, side in ((send, 1 - first_bit), (keep, first_bit)):
        if count:
            part = pl.ds(pl.multiple_of(side * rows, rows), rows)
            grad = dot(x_all[part, :], right[...]).astype(BF16)
            for final in range(finals):
                for at in range(count):
                    first = final * total + at * size
                    target[first : first + size, :] = grad[
                        final * size : (final + 1) * size, at * width : (at + 1) * width
                    ]
        if has_out:
            out_rows = att.shape[0] // 2
            part = pl.ds(pl.multiple_of(side * out_rows, out_rows), out_rows)
            grad = dot_nt(att[part, :], out_right[...]).astype(BF16)
            for final in range(finals):
                for block in range(blocks):
                    first = final * total + count * size + block * out_size
                    target[first : first + out_size, :] = grad[
                        final * out_size : (final + 1) * out_size,
                        block * width : (block + 1) * width,
                    ]


def on_device(hidden_in, grad_out, w_query, w_key, w_value, w_out, pattern):
    replicas = lax.axis_size("dp")
    pipe = lax.axis_size("pipe")
    bit_count = replicas.bit_length() - 1
    halved_bits = [bit for bit in range(bit_count) if bit not in (ROW_BIT, COL_BIT)]
    index = lax.axis_index("dp")
    seq_len, features = hidden_in.shape
    half = w_query.shape[2]
    w_query, w_key, w_value, w_out = w_query[0], w_key[0], w_value[0], w_out[0]

    def bit_of(bit):
        return (index >> bit) & 1

    def swap(x, bit):
        return lax.ppermute(x, "dp", [(i, i ^ (1 << bit)) for i in range(replicas)])

    def mirror(x):
        return lax.ppermute(x, "pipe", [(i, pipe - 1 - i) for i in range(pipe)])

    bits = jnp.stack([bit_of(ROW_BIT), bit_of(COL_BIT), bit_of(halved_bits[0])]).astype(jnp.int32)
    chunks = row_chunks(bit_count, halved_bits)

    def bf16(*shape):
        return jax.ShapeDtypeStruct(shape, BF16)

    width = half // 2
    part = features // 2
    tokens = 2 * seq_len
    size = features // replicas
    out_size = half // replicas

    x_mirror = mirror(hidden_in)
    g_mirror = mirror(grad_out)
    own, by_row, by_col = call(
        functools.partial(prep_body, chunks),
        "prep",
        (bits, hidden_in, grad_out),
        [bf16(features, seq_len)] * 3,
        [pltpu.VMEM((seq_len, features), BF16)] * 2
        + [pltpu.VMEM((features, seq_len), BF16)] * 2
        + [pltpu.SemaphoreType.DMA((2,))],
        far=2,
    )
    from_row = swap(by_row, ROW_BIT)
    from_col = swap(by_col, COL_BIT)
    own_mirror = mirror(own)
    x_last = swap(from_row[:part], COL_BIT)
    g_last = swap(from_col[:part], ROW_BIT)
    row_mirror, col_mirror = mirror(from_row), mirror(from_col)
    x_last_mirror, g_last_mirror = mirror(x_last), mirror(g_last)
    x_pieces = [(own, 0), (own_mirror, 0), (from_row, 0), (row_mirror, 0)]
    x_pieces += [(from_col, part), (col_mirror, part), (x_last, 0), (x_last_mirror, 0)]
    out_pieces = [(own, part), (own_mirror, part), (from_row, part), (row_mirror, part)]
    out_pieces += [(from_col, 0), (col_mirror, 0), (g_last, 0), (g_last_mirror, 0)]

    heights = [(len(members) + has_out) * tokens for has_out, members in CHUNKS]
    attended, *sends = call(
        functools.partial(attention_body, chunks),
        "attention",
        (bits, pattern, hidden_in, x_mirror, w_query, w_key, w_value, grad_out, g_mirror, w_out),
        [bf16(tokens, half)] + [bf16(height, width) for height in heights for _ in range(2)],
        [
            pltpu.VMEM((tokens, features), BF16),
            pltpu.VMEM((3, features, half), BF16),
            pltpu.VMEM((half, features), BF16),
            pltpu.VMEM((tokens, features), BF16),
        ]
        + [pltpu.VMEM((tokens, half), BF16)] * 4
        + [pltpu.VMEM((half, tokens), BF16), pltpu.SemaphoreType.DMA((8,))],
        flops=8 * tokens * features * half,
        scalars=2,
        far=8,
    )

    def exchanged(chunk, by_row, by_col):
        has_out, members = chunk
        height = len(members) * tokens
        from_row = swap(by_row, ROW_BIT)
        from_col = swap(by_col, COL_BIT)
        g_pieces, att_pieces = [], []
        if members:
            last = swap(from_col[:height], ROW_BIT)
            g_pieces = [(by_row, 0), (from_row, 0), (from_col, 0), (last, 0)]
        if has_out:
            last = swap(from_row[height:], COL_BIT)
            att_pieces = [(by_col, height), (from_row, height), (from_col, height), (last, 0)]
        return g_pieces, att_pieces

    def product(chunk, g_pieces, att_pieces):
        has_out, members = chunk
        pieces = list(x_pieces) + g_pieces
        if has_out:
            pieces += out_pieces + att_pieces
        arrays = []
        for array, _ in pieces:
            if not any(array is known for known in arrays):
                arrays.append(array)
        places = [
            ([array is known for known in arrays].index(True), first) for array, first in pieces
        ]
        blocks = part // width if has_out else 0
        height = (part // 2 // size) * (len(members) * size + blocks * out_size)
        scratch = [
            pltpu.VMEM((part, 8 * seq_len), BF16),
            pltpu.VMEM((8 * seq_len, len(members) * width), BF16),
        ]
        if has_out:
            scratch += [pltpu.VMEM((width, 8 * seq_len), BF16)]
            scratch += [pltpu.VMEM((part, 8 * seq_len), BF16)]
        scratch += [pltpu.SemaphoreType.DMA((8 + 4 * len(members) + 12 * has_out,))]

        def body(bits, *refs):
            inputs = [(refs[place], first) for place, first in places]
            weight_grad_body(chunk, size, out_size, bits, *inputs, *refs[len(arrays) :])

        return call(
            body,
            "weight_grad",
            (bits, *arrays),
            [bf16(height, width)] * 2,
            scratch,
            flops=16 * seq_len * part * width * (len(members) + has_out),
            far=len(arrays),
        )

    def halved(send, keep):
        for place, bit in enumerate(halved_bits):
            arrived = swap(send, bit)
            total = (keep.astype(F32) + arrived.astype(F32)).astype(BF16)
            after = halved_bits[place + 1] if place + 1 < len(halved_bits) else COL_BIT
            parts = total.reshape(2, total.shape[0] // 2, width)
            keep = lax.dynamic_index_in_dim(parts, bit_of(after), 0, keepdims=False)
            send = lax.dynamic_index_in_dim(parts, 1 - bit_of(after), 0, keepdims=False)
        return send, keep

    def placed(chunk, send, keep):
        has_out, members = chunk
        other = swap(send, COL_BIT)
        own_low = bit_of(COL_BIT) == 0
        low = jnp.where(own_low, keep, other)
        high = jnp.where(own_low, other, keep)
        found = {}
        for at, member in enumerate(members):
            rows = slice(at * size, (at + 1) * size)
            found[member] = jnp.concatenate([low[rows], high[rows]], axis=1).astype(F32)[None]
        if has_out:
            first = len(members) * size
            blocks = [
                side[first + at * out_size : first + (at + 1) * out_size]
                for side in (low, high)
                for at in range(part // width)
            ]
            found["out"] = jnp.concatenate(blocks, axis=1).astype(F32)[None]
        return found

    pieces = [exchanged(chunk, *sends[2 * at : 2 * at + 2]) for at, chunk in enumerate(CHUNKS)]
    products = [product(chunk, *piece) for chunk, piece in zip(CHUNKS, pieces)]

    contrib, contrib_mirror, returned, returned_mirror = call(
        returned_body,
        "returned",
        (bits, hidden_in, x_mirror, attended, w_out, w_query, w_key, w_value, *sends),
        [bf16(seq_len, features)] * 4,
        [
            pltpu.VMEM((tokens, features), BF16),
            pltpu.VMEM((tokens, half), BF16),
            pltpu.VMEM((half, features), BF16),
            pltpu.VMEM((3, features, half), BF16),
            pltpu.VMEM((3, tokens, half), BF16),
            pltpu.SemaphoreType.DMA((13,)),
        ],
        flops=8 * tokens * features * half,
        far=7 + len(sends),
    )
    found = {}
    for chunk, (send, keep) in zip(CHUNKS, products):
        found |= placed(chunk, *halved(send, keep))
    contrib_other = mirror(contrib_mirror)
    returned_other = mirror(returned_mirror)
    hidden_out = (
        hidden_in.astype(F32) + contrib.astype(F32) + contrib_other.astype(F32)
    ).astype(BF16)
    grad_in = (
        grad_out.astype(F32) + returned.astype(F32) + returned_other.astype(F32)
    ).astype(BF16)
    return (hidden_out, grad_in, found[2], found[1], found[0], found["out"])


def solution(mesh):
    in_specs = (
        P(("dp", "pipe"), None),
        P(("dp", "pipe"), None),
        P("pipe", None, None),
        P("pipe", None, None),
        P("pipe", None, None),
        P("pipe", None, None),
        P(),
    )
    out_specs = (
        P(("dp", "pipe"), None),
        P(("dp", "pipe"), None),
        P("pipe", "dp", None),
        P("pipe", "dp", None),
        P("pipe", "dp", None),
        P("pipe", "dp", None),
    )
    return jax.shard_map(
        on_device, mesh=mesh, in_specs=in_specs, out_specs=out_specs, check_vma=False
    )
```

time: 135 us -> 120 us (0.89)
  local copies, waits for them, and re-layouts: 42.9 us -> 2.34 us
  Pallas kernels: 18.2 us -> 34.4 us
  waiting for transfers between devices: 26.1 us -> 42 us
  starting transfers between devices: 40.7 us -> 32 us
  other arithmetic: 5.54 us -> 8.2 us
    unnamed x108 -> x49, local copies, waits for them, and re-layouts: 42.8 us -> 0.12 us
    pallas_call x7 -> x6, Pallas kernels: 18.2 us -> 34.4 us  [call(): pl.pallas_call(body, name=name, out_shape=outs, in_specs=specs, out_specs...]
    ppermute x30 -> x23, waiting for transfers between devices: 26 us -> 39.9 us  [swap(): return lax.ppermute(x, 'dp', [(i, i ^ 1 << bit) for i in range(replicas)])]
    ppermute x30 -> x23, starting transfers between devices: 38.6 us -> 30.2 us  [swap(): return lax.ppermute(x, 'dp', [(i, i ^ 1 << bit) for i in range(replicas)])]
    slice x0 -> x4, local copies, waits for them, and re-layouts: none -> 2.1 us  [the longest x1 0.73 us: on_device(): g_last = swap(from_col[:part], ROW_BIT)]
    ppermute x12 -> x9, waiting for transfers between devices: 0.03 us -> 2.07 us  [mirror(): return lax.ppermute(x, 'pipe', [(i, pipe - 1 - i) for i in range(pipe)])]
    convert_element_type x12 -> x10, other arithmetic: 3.34 us -> 3.33 us  [the longest x3 2.19 us: placed(): jnp.concatenate([low[rows], high[rows]], axis=1).astype(F32)[None]]
  transfers between devices with their start and end apart: 42 -> 32, of which waited for: 11 -> 9; matrix products, arithmetic and copies ran while one was open for 4% -> 7% of each run, Pallas kernels for 13% -> 29%
where the time goes in v2:
time: 120 us
  waiting for transfers between devices  42 us (35%)
  Pallas kernels  34.4 us (29%)
  starting transfers between devices  32 us (27%)
  other arithmetic  8.2 us (7%)
  local copies, waits for them, and re-layouts  2.34 us (2%)
    ppermute x23, waiting for transfers between devices, swap(): return lax.ppermute(x, 'dp', [(i, i ^ 1 << bit) for i in range(replicas)])  39.9 us
    pallas_call x6, Pallas kernels, call(): pl.pallas_call(body, name=name, out_shape=outs, in_specs=specs, out_specs...  34.4 us
    ppermute x23, starting transfers between devices, swap(): return lax.ppermute(x, 'dp', [(i, i ^ 1 << bit) for i in range(replicas)])  30.2 us
  transfers between devices with their start and end apart: 32, of which 9 were waited for; matrix products, arithmetic and copies ran while one was open for 7% of the time, Pallas kernels for 29%

profile of v2, /device:TPU:0, one launch (start us, length us, event | category | flops | bytes accessed | tf_op | source)
XLA Modules:
  0.0 119.9 jit_solution(1926417781555796581)
XLA Ops:
  1.8 3.3 %prep.1 = (bf16[2048,128]{1,0:T(8,128)(2,1)}, bf16[2048,128]{1,0:T(8,128)(2,1)}, bf16[2048,128]{1,0:T(8,128)(2,1)}) custom-call(s32[3]{0:T(128)} %pad_add_fusion.bits, bf16[128,2048]{1,0:T(8,128)(2,1)} %hidden.1, bf16[128,2048]{1,0:T(8,128)(2,1)} %grad.1), custom_call_target="tpu_custom_call" | custom-call | bytes 2621452 | tf_op jit(solution)/shard_map/prep/pallas_call | solution.py:46
  5.1 3.0 %collective-permute-start.5 = (bf16[2048,128]{1,0:T(8,128)(2,1)}, bf16[2048,128]{1,0:T(8,128)(2,1)S(1)}, u32[]{:S(2)}, u32[]{:S(2)}) collective-permute-start(bf16[2048,128]{1,0:T(8,128)(2,1)} %get-tuple-element.38), channel_id=1, source_target_pairs={{0,2},{2,0},{4,6},{6,4},{8,10},{10,8},{12,14},{14,12},{16,18},{18,... | collective-permute-start | bytes 1572872 | tf_op jit(solution)/shard_map/ppermute | solution.py:344
  8.1 1.6 %collective-permute-start.7 = (bf16[2048,128]{1,0:T(8,128)(2,1)}, bf16[2048,128]{1,0:T(8,128)(2,1)S(1)}, u32[]{:S(2)}, u32[]{:S(2)}) collective-permute-start(bf16[2048,128]{1,0:T(8,128)(2,1)} %get-tuple-element.39), channel_id=1, source_target_pairs={{0,8},{2,10},{4,12},{6,14},{8,0},{10,2},{12,4},{14,6},{16,24},{18,... | collective-permute-start | bytes 1572872 | tf_op jit(solution)/shard_map/ppermute | solution.py:344
  9.7 9.7 %attention.1 = (bf16[256,512]{1,0:T(8,128)(2,1)}, bf16[512,256]{1,0:T(8,128)(2,1)}, bf16[512,256]{1,0:T(8,128)(2,1)}, bf16[256,256]{1,0:T(8,128)(2,1)}, bf16[256...) custom-call(s32[3]{0:T(128)} %pad_add_fusion.bits, s32[4,3]{1,0:T(4,128)} %pattern.1, ...), custom_call_target="tpu_custom_call" | custom-call | flops 2147483648 | bytes 11796540 | tf_op jit(solution)/shard_map/attention/pallas_call | solution.py:46
  20.5 1.9 %collective-permute-start.9 = (bf16[1024,128]{1,0:T(8,128)(2,1)S(1)}, bf16[1024,128]{1,0:T(8,128)(2,1)S(1)}, u32[]{:S(2)}, u32[]{:S(2)}) collective-permute-start(bf16[1024,128]{1,0:T(8,128)(2,1)S(1)} %slice.56), channel_id=1, source_target_pairs={{0,8},{2,10},{4,12},{6,14},{8,0},{10,2},{12,4},{14,6},{16,24},{18,... | collective-permute-start | bytes 786440 | tf_op jit(solution)/shard_map/ppermute | solution.py:344
  25.2 12.1 %collective-permute-done.18.refs_10_ = bf16[256,256]{1,0:T(8,128)(2,1)S(1)} collective-permute-done((bf16[256,256]{1,0:T(8,128)(2,1)}, bf16[256,256]{1,0:T(8,128)(2,1)S(1)}, u32[]{:S(2)}, u32[]{:S(2)}) %collective-permute-start.18) | collective-permute-done | bytes 131104 | tf_op jit(solution)/shard_map/ppermute | solution.py:344
  39.7 1.5 %collective-permute-start.25 = (bf16[256,256]{1,0:T(8,128)(2,1)}, bf16[256,256]{1,0:T(8,128)(2,1)}, u32[]{:S(2)}, u32[]{:S(2)}) collective-permute-start(bf16[256,256]{1,0:T(8,128)(2,1)} %slice.57), channel_id=1, source_target_pairs={{0,2},{2,0},{4,6},{6,4},{8,10},{10,8},{12,14},{14,12},{16,18},{18,... | collective-permute-start | bytes 393224 | tf_op jit(solution)/shard_map/ppermute | solution.py:344
  41.8 7.5 %returned.1 = (bf16[128,2048]{1,0:T(8,128)(2,1)}, bf16[128,2048]{1,0:T(8,128)(2,1)}, bf16[128,2048]{1,0:T(8,128)(2,1)}, bf16[128,2048]{1,0:T(8,128)(2,1)}) custom-call(s32[3]{0:T(128)} %pad_add_fusion.bits, bf16[128,2048]{1,0:T(8,128)(2,1)} %hidden.1, bf16[128,2048]{1,0:T(8,128)(2,1)} %collective-permute-done.x_mirror, ...), custom_call_target="tpu_custom_call" | custom-call | flops 2147483648 | bytes 12845068 | tf_op jit(solution)/shard_map/returned/pallas_call | solution.py:46
  50.0 2.0 %collective-permute-done.10.refs_7_ = bf16[1024,128]{1,0:T(8,128)(2,1)S(1)} collective-permute-done((bf16[1024,128]{1,0:T(8,128)(2,1)S(1)}, bf16[1024,128]{1,0:T(8,128)(2,1)S(1)}, u32[]{:S(2)}, u32[]{:S(2)}) %collective-permute-start.10) | collective-permute-done | bytes 262176 | tf_op jit(solution)/shard_map/ppermute | solution.py:347
  56.1 6.0 %weight_grad.5 = (bf16[1024,256]{1,0:T(8,128)(2,1)}, bf16[1024,256]{1,0:T(8,128)(2,1)}) custom-call(s32[3]{0:T(128)} %pad_add_fusion.bits, bf16[2048,128]{1,0:T(8,128)(2,1)} %get-tuple-element.37.refs_0_, bf16[2048,128]{1,0:T(8,128)(2,1)} %copy-done.4, bf16[2048,128]{1,0:T(8,128)(2,1)} %copy-done.1, bf16[2048,128]{1,0:T(8,128)(2,1)} %collective-permute-done.6.refs_3_, ...), custom_call_target="tpu_custom_call" | custom-call | flops 1073741824 | bytes 6553612 | tf_op jit(solution)/shard_map/weight_grad/pallas_call | solution.py:46
  62.2 1.6 %collective-permute-start.29 = (bf16[1024,256]{1,0:T(8,128)(2,1)}, bf16[1024,256]{1,0:T(8,128)(2,1)S(1)}, u32[]{:S(2)}, u32[]{:S(2)}) collective-permute-start(bf16[1024,256]{1,0:T(8,128)(2,1)} %get-tuple-element.45), channel_id=1, source_target_pairs={{0,4},{2,6},{4,0},{6,2},{8,12},{10,14},{12,8},{14,10},{16,20},{18,... | collective-permute-start | bytes 1572872 | tf_op jit(solution)/shard_map/ppermute | solution.py:344
  63.8 3.9 %weight_grad.4 = (bf16[512,256]{1,0:T(8,128)(2,1)}, bf16[512,256]{1,0:T(8,128)(2,1)}) custom-call(s32[3]{0:T(128)} %pad_add_fusion.bits, bf16[2048,128]{1,0:T(8,128)(2,1)} %get-tuple-element.37.refs_0_, bf16[2048,128]{1,0:T(8,128)(2,1)} %copy-done.4, bf16[2048,128]{1,0:T(8,128)(2,1)} %copy-done.1, bf16[2048,128]{1,0:T(8,128)(2,1)} %collective-permute-done.6.refs_3_, ...), custom_call_target="tpu_custom_call" | custom-call | flops 536870912 | bytes 4718604 | tf_op jit(solution)/shard_map/weight_grad/pallas_call | solution.py:46
  68.5 3.9 %weight_grad.3 = (bf16[512,256]{1,0:T(8,128)(2,1)}, bf16[512,256]{1,0:T(8,128)(2,1)}) custom-call(s32[3]{0:T(128)} %pad_add_fusion.bits, bf16[2048,128]{1,0:T(8,128)(2,1)} %get-tuple-element.37.refs_0_, bf16[2048,128]{1,0:T(8,128)(2,1)} %copy-done.4, bf16[2048,128]{1,0:T(8,128)(2,1)} %copy-done.1, bf16[2048,128]{1,0:T(8,128)(2,1)} %collective-permute-done.6.refs_3_, ...), custom_call_target="tpu_custom_call" | custom-call | flops 536870912 | bytes 4718604 | tf_op jit(solution)/shard_map/weight_grad/pallas_call | solution.py:46
  72.4 1.5 %collective-permute-start.14 = (bf16[512,256]{1,0:T(8,128)(2,1)}, bf16[512,256]{1,0:T(8,128)(2,1)S(1)}, u32[]{:S(2)}, u32[]{:S(2)}) collective-permute-start(bf16[512,256]{1,0:T(8,128)(2,1)} %get-tuple-element.41), channel_id=1, source_target_pairs={{0,4},{2,6},{4,0},{6,2},{8,12},{10,14},{12,8},{14,10},{16,20},{18,... | collective-permute-start | bytes 786440 | tf_op jit(solution)/shard_map/ppermute | solution.py:344
  73.9 2.1 %add_convert_fusion.1 = bf16[128,2048]{1,0:T(8,128)(2,1)} fusion(bf16[128,2048]{1,0:T(8,128)(2,1)} %collective-permute-done.3, bf16[128,2048]{1,0:T(8,128)(2,1)S(1)} %copy-done.12, bf16[128,2048]{1,0:T(8,128)(2,1)S(1)} %copy-done.3), kind=kLoop, calls=%fused_computation.1 | loop fusion | flops 1572864 | bytes 2097152 | tf_op jit(solution)/shard_map/convert_element_type | solution.py:514
  76.1 2.1 %add_convert_fusion.2 = bf16[128,2048]{1,0:T(8,128)(2,1)} fusion(bf16[128,2048]{1,0:T(8,128)(2,1)} %collective-permute-done.2, bf16[128,2048]{1,0:T(8,128)(2,1)S(1)} %copy-done.11, bf16[128,2048]{1,0:T(8,128)(2,1)S(1)} %copy-done), kind=kLoop, calls=%fused_computation.2 | loop fusion | flops 1572864 | bytes 2097152 | tf_op jit(solution)/shard_map/convert_element_type | solution.py:511
  78.2 4.7 %collective-permute-done.20 = bf16[512,256]{1,0:T(8,128)(2,1)S(1)} collective-permute-done((bf16[512,256]{1,0:T(8,128)(2,1)}, bf16[512,256]{1,0:T(8,128)(2,1)S(1)}, u32[]{:S(2)}, u32[]{:S(2)}) %collective-permute-start.20) | collective-permute-done | bytes 262176 | tf_op jit(solution)/shard_map/ppermute | solution.py:344
  83.0 2.6 %collective-permute-start.21 = (bf16[256,256]{1,0:T(8,128)(2,1)S(1)}, bf16[256,256]{1,0:T(8,128)(2,1)S(1)}, u32[]{:S(2)}, u32[]{:S(2)}) collective-permute-start(bf16[256,256]{1,0:T(8,128)(2,1)S(1)} %dynamic-slice_bitcast_fusion.2), channel_id=1, source_target_pairs={{0,16},{2,18},{4,20},{6,22},{8,24},{10,26},{12,28},{14,30},{16,0},... | collective-permute-start | bytes 393224 | tf_op jit(solution)/shard_map/ppermute | solution.py:344
  85.6 2.4 %collective-permute-done.14 = bf16[512,256]{1,0:T(8,128)(2,1)S(1)} collective-permute-done((bf16[512,256]{1,0:T(8,128)(2,1)}, bf16[512,256]{1,0:T(8,128)(2,1)S(1)}, u32[]{:S(2)}, u32[]{:S(2)}) %collective-permute-start.14) | collective-permute-done | bytes 262176 | tf_op jit(solution)/shard_map/ppermute | solution.py:344
  88.1 2.6 %collective-permute-start.15 = (bf16[256,256]{1,0:T(8,128)(2,1)S(1)}, bf16[256,256]{1,0:T(8,128)(2,1)S(1)}, u32[]{:S(2)}, u32[]{:S(2)}) collective-permute-start(bf16[256,256]{1,0:T(8,128)(2,1)S(1)} %dynamic-slice_bitcast_fusion.3), channel_id=1, source_target_pairs={{0,16},{2,18},{4,20},{6,22},{8,24},{10,26},{12,28},{14,30},{16,0},... | collective-permute-start | bytes 393224 | tf_op jit(solution)/shard_map/ppermute | solution.py:344
  92.4 4.6 %collective-permute-done.15 = bf16[256,256]{1,0:T(8,128)(2,1)S(1)} collective-permute-done((bf16[256,256]{1,0:T(8,128)(2,1)S(1)}, bf16[256,256]{1,0:T(8,128)(2,1)S(1)}, u32[]{:S(2)}, u32[]{:S(2)}) %collective-permute-start.15) | collective-permute-done | bytes 131104 | tf_op jit(solution)/shard_map/ppermute | solution.py:344
  97.9 3.5 %collective-permute-start.30 = (bf16[512,256]{1,0:T(8,128)(2,1)S(1)}, bf16[512,256]{1,0:T(8,128)(2,1)S(1)}, u32[]{:S(2)}, u32[]{:S(2)}) collective-permute-start(bf16[512,256]{1,0:T(8,128)(2,1)S(1)} %dynamic-slice_bitcast_fusion), channel_id=1, source_target_pairs={{0,16},{2,18},{4,20},{6,22},{8,24},{10,26},{12,28},{14,30},{16,0},... | collective-permute-start | bytes 786440 | tf_op jit(solution)/shard_map/ppermute | solution.py:344
  101.5 11.7 %collective-permute-done.30 = bf16[512,256]{1,0:T(8,128)(2,1)S(1)} collective-permute-done((bf16[512,256]{1,0:T(8,128)(2,1)S(1)}, bf16[512,256]{1,0:T(8,128)(2,1)S(1)}, u32[]{:S(2)}, u32[]{:S(2)}) %collective-permute-start.30) | collective-permute-done | bytes 262176 | tf_op jit(solution)/shard_map/ppermute | solution.py:344
  114.8 3.5 %collective-permute-done.31 = bf16[256,256]{1,0:T(8,128)(2,1)S(1)} collective-permute-done((bf16[256,256]{1,0:T(8,128)(2,1)S(1)}, bf16[256,256]{1,0:T(8,128)(2,1)S(1)}, u32[]{:S(2)}, u32[]{:S(2)}) %collective-permute-start.31) | collective-permute-done | bytes 131104 | tf_op jit(solution)/shard_map/ppermute | solution.py:344
  (123 shorter events, 19.4 us)
Async XLA Ops:
  0.6 9.1 %collective-permute-start = (bf16[128,2048]{1,0:T(8,128)(2,1)}, bf16[128,2048]{1,0:T(8,128)(2,1)}, u32[]{:S(2)}, u32[]{:S(2)}) collective-permute-start(bf16[128,2048]{1,0:T(8,128)(2,1)} %hidden.1), channel_id=1, source_target_pairs={{0,1},{1,0},{2,3},{3,2},{4,5},{5,4},{6,7},{7,6},{8,9},{9,8},{10,11... | collective-permute-start | bytes 1572872 | tf_op jit(solution)/shard_map/ppermute | solution.py:347
  5.1 15.4 %collective-permute-start.5 = (bf16[2048,128]{1,0:T(8,128)(2,1)}, bf16[2048,128]{1,0:T(8,128)(2,1)S(1)}, u32[]{:S(2)}, u32[]{:S(2)}) collective-permute-start(bf16[2048,128]{1,0:T(8,128)(2,1)} %get-tuple-element.38), channel_id=1, source_target_pairs={{0,2},{2,0},{4,6},{6,4},{8,10},{10,8},{12,14},{14,12},{16,18},{18,... | collective-permute-start | bytes 1572872 | tf_op jit(solution)/shard_map/ppermute | solution.py:344
  8.1 14.3 %collective-permute-start.7 = (bf16[2048,128]{1,0:T(8,128)(2,1)}, bf16[2048,128]{1,0:T(8,128)(2,1)S(1)}, u32[]{:S(2)}, u32[]{:S(2)}) collective-permute-start(bf16[2048,128]{1,0:T(8,128)(2,1)} %get-tuple-element.39), channel_id=1, source_target_pairs={{0,8},{2,10},{4,12},{6,14},{8,0},{10,2},{12,4},{14,6},{16,24},{18,... | collective-permute-start | bytes 1572872 | tf_op jit(solution)/shard_map/ppermute | solution.py:344
  9.7 14.1 %collective-permute-start.4 = (bf16[2048,128]{1,0:T(8,128)(2,1)}, bf16[2048,128]{1,0:T(8,128)(2,1)S(1)}, u32[]{:S(2)}, u32[]{:S(2)}) collective-permute-start(bf16[2048,128]{1,0:T(8,128)(2,1)} %get-tuple-element.37.refs_0_), channel_id=1, source_target_pairs={{0,1},{1,0},{2,3},{3,2},{4,5},{5,4},{6,7},{7,6},{8,9},{9,8},{10,11... | collective-permute-start | bytes 1572872 | tf_op jit(solution)/shard_map/ppermute | solution.py:347
  19.5 18.3 %collective-permute-start.24 = (bf16[512,256]{1,0:T(8,128)(2,1)}, bf16[512,256]{1,0:T(8,128)(2,1)S(1)}, u32[]{:S(2)}, u32[]{:S(2)}) collective-permute-start(bf16[512,256]{1,0:T(8,128)(2,1)} %get-tuple-element.28.rest_1_.refs_14_), channel_id=1, source_target_pairs={{0,8},{2,10},{4,12},{6,14},{8,0},{10,2},{12,4},{14,6},{16,24},{18,... | collective-permute-start | bytes 786440 | tf_op jit(solution)/shard_map/ppermute | solution.py:344
  20.0 17.9 %collective-permute-start.23 = (bf16[512,256]{1,0:T(8,128)(2,1)}, bf16[512,256]{1,0:T(8,128)(2,1)S(1)}, u32[]{:S(2)}, u32[]{:S(2)}) collective-permute-start(bf16[512,256]{1,0:T(8,128)(2,1)} %get-tuple-element.27.rest_0_.refs_8_), channel_id=1, source_target_pairs={{0,2},{2,0},{4,6},{6,4},{8,10},{10,8},{12,14},{14,12},{16,18},{18,... | collective-permute-start | bytes 786440 | tf_op jit(solution)/shard_map/ppermute | solution.py:344
  20.5 20.6 %collective-permute-start.9 = (bf16[1024,128]{1,0:T(8,128)(2,1)S(1)}, bf16[1024,128]{1,0:T(8,128)(2,1)S(1)}, u32[]{:S(2)}, u32[]{:S(2)}) collective-permute-start(bf16[1024,128]{1,0:T(8,128)(2,1)S(1)} %slice.56), channel_id=1, source_target_pairs={{0,8},{2,10},{4,12},{6,14},{8,0},{10,2},{12,4},{14,6},{16,24},{18,... | collective-permute-start | bytes 786440 | tf_op jit(solution)/shard_map/ppermute | solution.py:344
  22.4 14.8 %collective-permute-start.18 = (bf16[256,256]{1,0:T(8,128)(2,1)}, bf16[256,256]{1,0:T(8,128)(2,1)S(1)}, u32[]{:S(2)}, u32[]{:S(2)}) collective-permute-start(bf16[256,256]{1,0:T(8,128)(2,1)} %get-tuple-element.30.rest_3_), channel_id=1, source_target_pairs={{0,8},{2,10},{4,12},{6,14},{8,0},{10,2},{12,4},{14,6},{16,24},{18,... | collective-permute-start | bytes 393224 | tf_op jit(solution)/shard_map/ppermute | solution.py:344
  23.8 15.9 %collective-permute-start.12 = (bf16[256,256]{1,0:T(8,128)(2,1)}, bf16[256,256]{1,0:T(8,128)(2,1)S(1)}, u32[]{:S(2)}, u32[]{:S(2)}) collective-permute-start(bf16[256,256]{1,0:T(8,128)(2,1)} %get-tuple-element.32.rest_5_), channel_id=1, source_target_pairs={{0,8},{2,10},{4,12},{6,14},{8,0},{10,2},{12,4},{14,6},{16,24},{18,... | collective-permute-start | bytes 393224 | tf_op jit(solution)/shard_map/ppermute | solution.py:344
  37.3 12.0 %collective-permute-start.26 = (bf16[1024,128]{1,0:T(8,128)(2,1)}, bf16[1024,128]{1,0:T(8,128)(2,1)}, u32[]{:S(2)}, u32[]{:S(2)}) collective-permute-start(bf16[1024,128]{1,0:T(8,128)(2,1)} %slice.58), channel_id=1, source_target_pairs={{0,2},{2,0},{4,6},{6,4},{8,10},{10,8},{12,14},{14,12},{16,18},{18,... | collective-permute-start | bytes 786440 | tf_op jit(solution)/shard_map/ppermute | solution.py:344
  37.8 14.9 %collective-permute-start.6 = (bf16[2048,128]{1,0:T(8,128)(2,1)S(1)}, bf16[2048,128]{1,0:T(8,128)(2,1)}, u32[]{:S(2)}, u32[]{:S(2)}) collective-permute-start(bf16[2048,128]{1,0:T(8,128)(2,1)S(1)} %collective-permute-done.5.refs_2_), channel_id=1, source_target_pairs={{0,1},{1,0},{2,3},{3,2},{4,5},{5,4},{6,7},{7,6},{8,9},{9,8},{10,11... | collective-permute-start | bytes 1572872 | tf_op jit(solution)/shard_map/ppermute | solution.py:347
  37.8 16.2 %collective-permute-start.8 = (bf16[2048,128]{1,0:T(8,128)(2,1)S(1)}, bf16[2048,128]{1,0:T(8,128)(2,1)}, u32[]{:S(2)}, u32[]{:S(2)}) collective-permute-start(bf16[2048,128]{1,0:T(8,128)(2,1)S(1)} %collective-permute-done.7.refs_4_), channel_id=1, source_target_pairs={{0,1},{1,0},{2,3},{3,2},{4,5},{5,4},{6,7},{7,6},{8,9},{9,8},{10,11... | collective-permute-start | bytes 1572872 | tf_op jit(solution)/shard_map/ppermute | solution.py:347
  39.7 9.7 %collective-permute-start.25 = (bf16[256,256]{1,0:T(8,128)(2,1)}, bf16[256,256]{1,0:T(8,128)(2,1)}, u32[]{:S(2)}, u32[]{:S(2)}) collective-permute-start(bf16[256,256]{1,0:T(8,128)(2,1)} %slice.57), channel_id=1, source_target_pairs={{0,2},{2,0},{4,6},{6,4},{8,10},{10,8},{12,14},{14,12},{16,18},{18,... | collective-permute-start | bytes 393224 | tf_op jit(solution)/shard_map/ppermute | solution.py:344
  49.3 24.6 %collective-permute-start.3 = (bf16[128,2048]{1,0:T(8,128)(2,1)}, bf16[128,2048]{1,0:T(8,128)(2,1)}, u32[]{:S(2)}, u32[]{:S(2)}) collective-permute-start(bf16[128,2048]{1,0:T(8,128)(2,1)} %get-tuple-element.36), channel_id=1, source_target_pairs={{0,1},{1,0},{2,3},{3,2},{4,5},{5,4},{6,7},{7,6},{8,9},{9,8},{10,11... | collective-permute-start | bytes 1572872 | tf_op jit(solution)/shard_map/ppermute | solution.py:347
  52.0 10.1 %collective-permute-start.17 = (bf16[256,256]{1,0:T(8,128)(2,1)}, bf16[256,256]{1,0:T(8,128)(2,1)S(1)}, u32[]{:S(2)}, u32[]{:S(2)}) collective-permute-start(bf16[256,256]{1,0:T(8,128)(2,1)} %get-tuple-element.29.rest_2_.refs_8_), channel_id=1, source_target_pairs={{0,2},{2,0},{4,6},{6,4},{8,10},{10,8},{12,14},{14,12},{16,18},{18,... | collective-permute-start | bytes 393224 | tf_op jit(solution)/shard_map/ppermute | solution.py:344
  52.7 9.5 %collective-permute-start.19 = (bf16[256,256]{1,0:T(8,128)(2,1)}, bf16[256,256]{1,0:T(8,128)(2,1)S(1)}, u32[]{:S(2)}, u32[]{:S(2)}) collective-permute-start(bf16[256,256]{1,0:T(8,128)(2,1)} %copy-done.17), channel_id=1, source_target_pairs={{0,2},{2,0},{4,6},{6,4},{8,10},{10,8},{12,14},{14,12},{16,18},{18,... | collective-permute-start | bytes 393224 | tf_op jit(solution)/shard_map/ppermute | solution.py:344
  54.1 13.7 %collective-permute-start.11 = (bf16[256,256]{1,0:T(8,128)(2,1)S(1)}, bf16[256,256]{1,0:T(8,128)(2,1)S(1)}, u32[]{:S(2)}, u32[]{:S(2)}) collective-permute-start(bf16[256,256]{1,0:T(8,128)(2,1)S(1)} %copy-done.9), channel_id=1, source_target_pairs={{0,2},{2,0},{4,6},{6,4},{8,10},{10,8},{12,14},{14,12},{16,18},{18,... | collective-permute-start | bytes 393224 | tf_op jit(solution)/shard_map/ppermute | solution.py:344
  54.8 13.7 %collective-permute-start.13 = (bf16[256,256]{1,0:T(8,128)(2,1)}, bf16[256,256]{1,0:T(8,128)(2,1)}, u32[]{:S(2)}, u32[]{:S(2)}) collective-permute-start(bf16[256,256]{1,0:T(8,128)(2,1)} %copy-done.16), channel_id=1, source_target_pairs={{0,2},{2,0},{4,6},{6,4},{8,10},{10,8},{12,14},{14,12},{16,18},{18,... | collective-permute-start | bytes 393224 | tf_op jit(solution)/shard_map/ppermute | solution.py:344
  62.1 13.9 %collective-permute-start.2 = (bf16[128,2048]{1,0:T(8,128)(2,1)}, bf16[128,2048]{1,0:T(8,128)(2,1)}, u32[]{:S(2)}, u32[]{:S(2)}) collective-permute-start(bf16[128,2048]{1,0:T(8,128)(2,1)} %get-tuple-element.34), channel_id=1, source_target_pairs={{0,1},{1,0},{2,3},{3,2},{4,5},{5,4},{6,7},{7,6},{8,9},{9,8},{10,11... | collective-permute-start | bytes 1572872 | tf_op jit(solution)/shard_map/ppermute | solution.py:347
  62.2 35.5 %collective-permute-start.29 = (bf16[1024,256]{1,0:T(8,128)(2,1)}, bf16[1024,256]{1,0:T(8,128)(2,1)S(1)}, u32[]{:S(2)}, u32[]{:S(2)}) collective-permute-start(bf16[1024,256]{1,0:T(8,128)(2,1)} %get-tuple-element.45), channel_id=1, source_target_pairs={{0,4},{2,6},{4,0},{6,2},{8,12},{10,14},{12,8},{14,10},{16,20},{18,... | collective-permute-start | bytes 1572872 | tf_op jit(solution)/shard_map/ppermute | solution.py:344
  67.8 15.1 %collective-permute-start.20 = (bf16[512,256]{1,0:T(8,128)(2,1)}, bf16[512,256]{1,0:T(8,128)(2,1)S(1)}, u32[]{:S(2)}, u32[]{:S(2)}) collective-permute-start(bf16[512,256]{1,0:T(8,128)(2,1)} %get-tuple-element.43), channel_id=1, source_target_pairs={{0,4},{2,6},{4,0},{6,2},{8,12},{10,14},{12,8},{14,10},{16,20},{18,... | collective-permute-start | bytes 786440 | tf_op jit(solution)/shard_map/ppermute | solution.py:344
  72.4 15.6 %collective-permute-start.14 = (bf16[512,256]{1,0:T(8,128)(2,1)}, bf16[512,256]{1,0:T(8,128)(2,1)S(1)}, u32[]{:S(2)}, u32[]{:S(2)}) collective-permute-start(bf16[512,256]{1,0:T(8,128)(2,1)} %get-tuple-element.41), channel_id=1, source_target_pairs={{0,4},{2,6},{4,0},{6,2},{8,12},{10,14},{12,8},{14,10},{16,20},{18,... | collective-permute-start | bytes 786440 | tf_op jit(solution)/shard_map/ppermute | solution.py:344
  91.4 10.1 %collective-permute-start.22 = (bf16[128,256]{1,0:T(8,128)(2,1)S(1)}, bf16[128,256]{1,0:T(8,128)(2,1)S(1)}, u32[]{:S(2)}, u32[]{:S(2)}) collective-permute-start(bf16[128,256]{1,0:T(8,128)(2,1)S(1)} %dynamic-slice_bitcast_fusion.4), channel_id=1, source_target_pairs={{0,8},{2,10},{4,12},{6,14},{8,0},{10,2},{12,4},{14,6},{16,24},{18,... | collective-permute-start | bytes 196616 | tf_op jit(solution)/shard_map/ppermute | solution.py:344
  97.9 15.3 %collective-permute-start.30 = (bf16[512,256]{1,0:T(8,128)(2,1)S(1)}, bf16[512,256]{1,0:T(8,128)(2,1)S(1)}, u32[]{:S(2)}, u32[]{:S(2)}) collective-permute-start(bf16[512,256]{1,0:T(8,128)(2,1)S(1)} %dynamic-slice_bitcast_fusion), channel_id=1, source_target_pairs={{0,16},{2,18},{4,20},{6,22},{8,24},{10,26},{12,28},{14,30},{16,0},... | collective-permute-start | bytes 786440 | tf_op jit(solution)/shard_map/ppermute | solution.py:344
  (29 other events, 236.5 us)

commit v3 on v1

v3 whole, which is shorter than its diff:
```python
import functools
import math

import jax
import jax.numpy as jnp
from jax import lax
from jax.experimental import pallas as pl
from jax.experimental.pallas import tpu as pltpu
from jax.sharding import PartitionSpec as P

HDIM = 64
NORM_EPS = 1e-05
PAIR = 2 * HDIM
VMEM_BYTES = 62 * 1024 * 1024

ATTENTION_WORK = 11 * 10**9

F32 = jnp.float32
BF16 = jnp.bfloat16
NT = (((1,), (1,)), ((), ()))
TN = (((0,), (0,)), ((), ()))

PROJECTION_BITS = (0, 1)
OUT_BIT = 2

UNITS = ((0, 1), (2,))


def dot(left, right):
    return jnp.dot(left, right, preferred_element_type=F32)


def dot_nt(left, right):
    return lax.dot_general(left, right, NT, preferred_element_type=F32)


def dot_tn(left, right):
    return lax.dot_general(left, right, TN, preferred_element_type=F32)


def call(body, name, inputs, outs, scratch=(), work=0, scalars=0, far=0, after=()):
    near = len(inputs) - scalars - far
    count = len(inputs)
    specs = [pl.BlockSpec(memory_space=pltpu.SMEM)] * scalars
    specs += [pl.BlockSpec(memory_space=pltpu.VMEM)] * near
    specs += [pl.BlockSpec(memory_space=pltpu.HBM)] * (far + len(after))

    def run(*refs):
        body(*refs[:count], *refs[count + len(after) :])

    return pl.pallas_call(
        run,
        name=name,
        out_shape=outs,
        in_specs=specs,
        out_specs=[pl.BlockSpec(memory_space=pltpu.VMEM)] * len(outs),
        scratch_shapes=list(scratch),
        compiler_params=pltpu.CompilerParams(vmem_limit_bytes=VMEM_BYTES),
        cost_estimate=pl.CostEstimate(flops=work, bytes_accessed=0, transcendentals=0),
    )(*inputs, *after)


def fetch(pairs, sems):
    copies = [
        pltpu.make_async_copy(source, target, sems.at[place])
        for place, (source, target) in enumerate(pairs)
    ]
    for copy in copies:
        copy.start()
    return copies


def finish(copies):
    for copy in copies:
        copy.wait()


def spread(bits):
    found = [0]
    for bit in bits:
        found = [index | (value << bit) for index in found for value in (0, 1)]
    return found


def groups(bits, bit_count):
    others = [bit for bit in range(bit_count) if bit not in bits]
    return [[base | part for part in spread(bits)] for base in spread(others)]


def copy_chunks(source, target, chunks, size):
    for place, chunk in enumerate(chunks):
        target[place * size : (place + 1) * size, :] = source[chunk * size : (chunk + 1) * size, :]


def bit_here(bit):
    return (lax.axis_index("dp") >> bit) & 1


def prep_body(chunks, hidden, grad, x_blocks, g_send, x, turned, sems):
    columns = g_send.shape[1]
    away = pl.ds(pl.multiple_of((1 - bit_here(OUT_BIT)) * columns, columns), columns)
    x_copy, g_copy = fetch([(hidden, x), (grad.at[:, away], g_send)], sems)
    x_copy.wait()
    turned[...] = x[...].astype(F32).T.astype(BF16)
    for member in range(4):
        own = [chunk | (member % 2) << PROJECTION_BITS[0] for chunk in chunks]
        copy_chunks(turned, x_blocks.at[member], own, turned.shape[0] // (2 * len(own)))
    g_copy.wait()


def seen_mask(pattern, seq_len, blocks, slots):
    block_len = seq_len // blocks
    rows = lax.broadcasted_iota(jnp.int32, (seq_len, seq_len), 0)
    columns = lax.broadcasted_iota(jnp.int32, (seq_len, seq_len), 1)
    row_block, column_block = rows // block_len, columns // block_len
    seen = jnp.zeros((seq_len, seq_len), F32)
    for block in range(blocks):
        for slot in range(slots):
            hit = (row_block == block) & (column_block == pattern[block, slot])
            seen = jnp.where(hit, 1.0, seen)
    return jnp.where((row_block == column_block) & (columns > rows), 0.0, seen)


def scale_of(x):
    return lax.rsqrt(jnp.mean(x * x, axis=-1, keepdims=True) + NORM_EPS)


def attention_body(
    out_chunks,
    pattern,
    x_own,
    x_mirror,
    w_query,
    w_key,
    w_value,
    g_own,
    g_mirror,
    w_out,
    attended,
    att_turned,
    blocks,
    x_all,
    weights,
    weight_out,
    g_all,
    query,
    key,
    values,
    grad_att,
    turned,
    sems,
):
    seq_len = x_own.shape[0]
    tokens = 2 * seq_len
    half = w_query.shape[1]
    own, other = pl.ds(0, seq_len), pl.ds(seq_len, seq_len)
    copies = fetch(
        [
            (x_own, x_all.at[own]),
            (x_mirror, x_all.at[other]),
            (w_query, weights.at[0]),
            (w_key, weights.at[1]),
            (w_value, weights.at[2]),
            (g_own, g_all.at[own]),
            (g_mirror, g_all.at[other]),
            (w_out, weight_out),
        ],
        sems,
    )
    finish(copies[:2])
    x = x_all[...]
    factor = scale_of(x.astype(F32))
    for place, target in enumerate((query, key, values)):
        copies[2 + place].wait()
        target[...] = (dot(x, weights[place]) * factor).astype(BF16)
    finish(copies[5:])
    grad_att[...] = dot_nt(g_all[...], weight_out[...]).astype(BF16)

    seen = seen_mask(pattern, seq_len, pattern.shape[0], pattern.shape[1])
    seen = jnp.concatenate([seen, seen], axis=0) > 0.0
    low = lax.broadcasted_iota(jnp.int32, (seq_len, PAIR), 1) < HDIM
    inv_sqrt = 1.0 / math.sqrt(HDIM)
    zero = jnp.zeros((), BF16)

    def stacked(block):
        return jnp.concatenate([jnp.where(low, block, zero), jnp.where(low, zero, block)], axis=0)

    def merged(both):
        return jnp.where(low, both[:seq_len], both[seq_len:])

    width = half // 2
    def put(member, col, first, here, value):
        rounded = value.astype(BF16)
        first += member * tokens
        for row in range(2):
            blocks[2 * col + row, first : first + seq_len, here] = rounded

    for pair in range(half // PAIR):
        columns = slice(pair * PAIR, (pair + 1) * PAIR)
        col, start = pair * PAIR // width, pair * PAIR % width
        here = slice(start, start + PAIR)
        for seq in range(2):
            rows = slice(seq * seq_len, (seq + 1) * seq_len)
            q2 = stacked(query[rows, columns])
            k = key[rows, columns]
            v = values[rows, columns]
            ga2 = stacked(grad_att[rows, columns])
            r = factor[rows]

            expo = jnp.where(seen, jnp.exp(dot_nt(q2, k) * inv_sqrt), 0.0)
            prob = expo / jnp.sum(expo, axis=-1, keepdims=True)
            prob_bf = prob.astype(BF16)
            attended[rows, columns] = merged(dot(prob_bf, v)).astype(BF16)
            grad_prob = dot_nt(ga2, v)
            inner = jnp.sum(prob * grad_prob, axis=-1, keepdims=True)
            score = (prob * (grad_prob - inner) * inv_sqrt).astype(BF16)
            put(0, col, seq * seq_len, here, dot_tn(prob_bf, ga2) * r)
            put(1, col, seq * seq_len, here, dot_tn(score, q2) * r)
            put(2, col, seq * seq_len, here, merged(dot(score, k)) * r)

    turned[...] = attended[...].astype(F32).T.astype(BF16)
    copy_chunks(turned, att_turned, out_chunks, half // len(out_chunks))


def returned_body(
    x_own,
    x_mirror,
    attended,
    w_out,
    w_query,
    w_key,
    w_value,
    blocks,
    contrib_own,
    contrib_mirror,
    returned_own,
    returned_mirror,
    x_all,
    att,
    weight_out,
    weights,
    grads,
    sems,
):
    seq_len = x_own.shape[0]
    tokens, half = att.shape
    width = half // 2
    pairs = [
        (attended, att),
        (w_out, weight_out),
        (x_own, x_all.at[pl.ds(0, seq_len)]),
        (x_mirror, x_all.at[pl.ds(seq_len, seq_len)]),
    ]
    for member in range(3):
        for col in range(2):
            source = blocks.at[2 * col, pl.ds(member * tokens, tokens)]
            pairs.append((source, grads.at[member, :, pl.ds(col * width, width)]))
    pairs += [(w_value, weights.at[0]), (w_key, weights.at[1]), (w_query, weights.at[2])]
    copies = fetch(pairs, sems)
    finish(copies[:2])
    contrib = dot(att[...], weight_out[...]).astype(BF16)
    contrib_own[...] = contrib[:seq_len]
    contrib_mirror[...] = contrib[seq_len:]
    finish(copies[2:-3])
    grad = None
    for member in range(3):
        copies[member - 3].wait()
        term = dot_nt(grads[member], weights[member])
        grad = term if grad is None else grad + term
    x = x_all[...].astype(F32)
    factor = scale_of(x)
    mean_term = jnp.mean(x * grad, axis=-1, keepdims=True)
    returned = (grad - x * (factor * factor * mean_term)).astype(BF16)
    returned_own[...] = returned[:seq_len]
    returned_mirror[...] = returned[seq_len:]


def projection_grad_body(first_bit, x_pieces, x_mirrors, g_pieces, *rest):
    targets, (x_all, right, sems) = rest[: 2 * len(UNITS)], rest[2 * len(UNITS) :]
    seq_len = x_pieces.shape[2]
    tokens = 2 * seq_len
    width = g_pieces.shape[2]
    members = [member for unit in UNITS for member in unit]
    pairs = []
    for place in range(4):
        for at, source in enumerate((x_pieces, x_mirrors)):
            columns = pl.ds(place * tokens + at * seq_len, seq_len)
            pairs.append((source.at[place], x_all.at[:, columns]))
        for at, member in enumerate(members):
            target = right.at[pl.ds(place * tokens, tokens), pl.ds(at * width, width)]
            pairs.append((g_pieces.at[place, pl.ds(member * tokens, tokens)], target))
    finish(fetch(pairs, sems))
    bit = bit_here(first_bit)
    rows = x_all.shape[0] // 2
    for turn, side in ((0, 1 - bit), (1, bit)):
        part = pl.ds(pl.multiple_of(side * rows, rows), rows)
        column = 0
        for unit in range(len(UNITS)):
            target = targets[2 * unit + turn]
            columns = slice(column, column + target.shape[1])
            target[...] = dot(x_all[part, :], right[:, columns]).astype(BF16)
            column += target.shape[1]


def add_body(keep, arrived, total):
    total[...] = (keep[...].astype(F32) + arrived[...].astype(F32)).astype(BF16)


def out_grad_body(
    first_bit, grad, g_mirror, g_piece, g_piece_mirror, att_own, att_piece, send, keep, *scratch
):
    left, right, sems = scratch
    seq_len = grad.shape[0]
    tokens = 2 * seq_len
    columns = right.shape[1]
    here = pl.ds(pl.multiple_of(bit_here(OUT_BIT) * columns, columns), columns)
    pairs = [
        (att_own, left.at[:, pl.ds(0, tokens)]),
        (att_piece, left.at[:, pl.ds(tokens, tokens)]),
    ]
    for place, source in enumerate(
        (grad.at[:, here], g_mirror.at[:, here], g_piece, g_piece_mirror)
    ):
        pairs.append((source, right.at[pl.ds(place * seq_len, seq_len)]))
    finish(fetch(pairs, sems))
    bit = bit_here(first_bit)
    rows = left.shape[0] // 2
    for target, side in ((send, 1 - bit), (keep, bit)):
        part = pl.ds(pl.multiple_of(side * rows, rows), rows)
        target[...] = dot(left[part, :], right[...]).astype(BF16)


def final_body(count, pieces, *targets):
    width = pieces.shape[2] // count
    for at, target in enumerate(targets):
        here = slice(at * width, (at + 1) * width)
        for col in range(2):
            total = pieces[col, :, here].astype(F32)
            for place in range(1, pieces.shape[0] // 2):
                total += pieces[2 * place + col, :, here].astype(F32)
            target[:, col * width : (col + 1) * width] = total


def halve_body(bit, keep, arrived, send, next_keep):
    here = bit_here(bit)
    rows = send.shape[0]
    for target, side in ((send, 1 - here), (next_keep, here)):
        part = pl.ds(pl.multiple_of(side * rows, rows), rows)
        total = keep[part, :].astype(F32) + arrived[part, :].astype(F32)
        target[...] = total.astype(BF16)


def on_device(hidden_in, grad_out, w_query, w_key, w_value, w_out, pattern):
    replicas = lax.axis_size("dp")
    pipe = lax.axis_size("pipe")
    bit_count = replicas.bit_length() - 1
    row_bit, col_bit = PROJECTION_BITS
    halved_bits = [bit for bit in range(bit_count) if bit not in PROJECTION_BITS]
    out_bits = [col_bit, row_bit] + [bit for bit in halved_bits if bit != OUT_BIT]
    chunks = spread(halved_bits + [col_bit])
    out_chunks = spread(out_bits + [OUT_BIT])
    seq_len, features = hidden_in.shape
    half = w_query.shape[2]
    w_query, w_key, w_value, w_out = w_query[0], w_key[0], w_value[0], w_out[0]
    width, part, tokens = half // 2, features // 2, 2 * seq_len

    def swap(x, *bits):
        apart = sum(1 << bit for bit in bits)
        return lax.ppermute(x, "dp", [(i, i ^ apart) for i in range(replicas)])

    def mirror(x):
        return lax.ppermute(x, "pipe", [(i, pipe - 1 - i) for i in range(pipe)])

    def exchange(x, bits):
        members = groups(bits, bit_count)
        return lax.all_to_all(x, "dp", 0, 0, axis_index_groups=members, tiled=True)

    def follows(x, before):
        return lax.optimization_barrier((x, before))[0]

    def bf16(*shape):
        return jax.ShapeDtypeStruct(shape, BF16)

    x_mirror = mirror(hidden_in)
    g_mirror = mirror(grad_out)
    x_blocks, g_send = call(
        functools.partial(prep_body, chunks),
        "prep",
        (hidden_in, grad_out),
        [bf16(4, part, seq_len), bf16(seq_len, part)],
        [
            pltpu.VMEM((seq_len, features), BF16),
            pltpu.VMEM((features, seq_len), BF16),
            pltpu.SemaphoreType.DMA((2,)),
        ],
        far=2,
    )
    x_pieces = exchange(x_blocks, [col_bit, row_bit])
    g_piece = swap(g_send, OUT_BIT)

    attended, att_turned, g_blocks = call(
        functools.partial(attention_body, out_chunks),
        "attention",
        (pattern, hidden_in, x_mirror, w_query, w_key, w_value, grad_out, g_mirror, w_out),
        [bf16(tokens, half), bf16(half, tokens)]
        + [bf16(4, 3 * tokens, width)],
        [
            pltpu.VMEM((tokens, features), BF16),
            pltpu.VMEM((3, features, half), BF16),
            pltpu.VMEM((half, features), BF16),
            pltpu.VMEM((tokens, features), BF16),
        ]
        + [pltpu.VMEM((tokens, half), BF16)] * 4
        + [
            pltpu.VMEM((half, tokens), BF16),
            pltpu.SemaphoreType.DMA((8,)),
        ],
        work=ATTENTION_WORK,
        scalars=1,
        far=8,
        after=(x_blocks,),
    )
    g_pieces = exchange(follows(g_blocks, g_piece), [col_bit, row_bit])
    att_piece = swap(att_turned, OUT_BIT)
    x_mirrors = mirror(follows(x_pieces, attended))
    g_piece_mirror = mirror(follows(g_piece, attended))

    contrib, contrib_mirror, returned, returned_mirror = call(
        returned_body,
        "returned",
        (hidden_in, x_mirror, attended, w_out, w_query, w_key, w_value, g_blocks),
        [bf16(seq_len, features)] * 4,
        [
            pltpu.VMEM((tokens, features), BF16),
            pltpu.VMEM((tokens, half), BF16),
            pltpu.VMEM((half, features), BF16),
            pltpu.VMEM((3, features, half), BF16),
            pltpu.VMEM((3, tokens, half), BF16),
            pltpu.SemaphoreType.DMA((13,)),
        ],
        far=8,
    )

    out_send, out_keep = call(
        functools.partial(out_grad_body, out_bits[0]),
        "out_grad",
        (grad_out, g_mirror, g_piece, g_piece_mirror, att_turned, att_piece),
        [bf16(half // 2, part)] * 2,
        [
            pltpu.VMEM((half, 2 * tokens), BF16),
            pltpu.VMEM((2 * tokens, part), BF16),
            pltpu.SemaphoreType.DMA((6,)),
        ],
        far=6,
        after=(contrib,),
    )
    parts = call(
        functools.partial(projection_grad_body, halved_bits[0]),
        "projection_grad",
        (x_pieces, x_mirrors, g_pieces),
        [bf16(part // 2, len(unit) * width) for unit in UNITS for _ in range(2)],
        [
            pltpu.VMEM((part, 4 * tokens), BF16),
            pltpu.VMEM((4 * tokens, 3 * width), BF16),
            pltpu.SemaphoreType.DMA((20,)),
        ],
        far=3,
        after=(out_send,),
    )
    last_parts = parts[0]

    def halve(place, send, keep, after):
        return call(
            functools.partial(halve_body, (out_bits + [OUT_BIT])[place + 1]),
            "halve",
            (keep, swap(send, out_bits[place])),
            [bf16(keep.shape[0] // 2, part)] * 2,
            after=(after,),
        )

    def add(unit, after):
        send, keep = parts[2 * unit : 2 * unit + 2]
        return call(
            add_body,
            "add",
            (keep, swap(send, halved_bits[0])),
            [bf16(*keep.shape)],
            after=(after,),
        )[0]

    def finals(unit, total, after):
        pieces = exchange(total, halved_bits[1:] + [col_bit])
        members = UNITS[unit]
        return call(
            functools.partial(final_body, len(members)),
            "final",
            (pieces.reshape(2 << (len(halved_bits) - 1), -1, total.shape[1]),),
            [jax.ShapeDtypeStruct((features // replicas, half), F32)] * len(members),
            after=(after,),
        )

    totals = []
    last = parts[0]
    for unit in range(len(UNITS)):
        totals.append(add(unit, last))
        out_send, out_keep = halve(unit, out_send, out_keep, totals[-1])
        last = out_send
    found = {}
    for unit, members in enumerate(UNITS):
        grads = finals(unit, totals[unit], last)
        found |= {member: grad[None] for member, grad in zip(members, grads)}
        if len(UNITS) + unit < len(out_bits):
            out_send, out_keep = halve(len(UNITS) + unit, out_send, out_keep, grads[0])
            last = out_send
    for place in range(2 * len(UNITS), len(out_bits)):
        out_send, out_keep = halve(place, out_send, out_keep, last)
    out_other = swap(out_send, OUT_BIT)
    own_low = (lax.axis_index("dp") >> OUT_BIT) & 1 == 0
    low = jnp.where(own_low, out_keep, out_other)
    high = jnp.where(own_low, out_other, out_keep)
    grad_wout = jnp.concatenate([low, high], axis=1).astype(F32)[None]

    contrib_other = mirror(follows(contrib_mirror, parts[0]))
    returned_other = mirror(follows(returned_mirror, last_parts))
    hidden_out = (
        hidden_in.astype(F32) + contrib.astype(F32) + contrib_other.astype(F32)
    ).astype(BF16)
    grad_in = (
        grad_out.astype(F32) + returned.astype(F32) + returned_other.astype(F32)
    ).astype(BF16)
    return (hidden_out, grad_in, found[2], found[1], found[0], grad_wout)


def solution(mesh):
    in_specs = (
        P(("dp", "pipe"), None),
        P(("dp", "pipe"), None),
        P("pipe", None, None),
        P("pipe", None, None),
        P("pipe", None, None),
        P("pipe", None, None),
        P(),
    )
    out_specs = (
        P(("dp", "pipe"), None),
        P(("dp", "pipe"), None),
        P("pipe", "dp", None),
        P("pipe", "dp", None),
        P("pipe", "dp", None),
        P("pipe", "dp", None),
    )
    return jax.shard_map(
        on_device, mesh=mesh, in_specs=in_specs, out_specs=out_specs, check_vma=False
    )
```

time: 135 us -> 109 us (0.81)
  local copies, waits for them, and re-layouts: 42.9 us -> 7.33 us
  Pallas kernels: 18.2 us -> 39.7 us
  starting transfers between devices: 40.7 us -> 26.6 us
  waiting for transfers between devices: 26.1 us -> 28.2 us
    unnamed x108 -> x28, local copies, waits for them, and re-layouts: 42.8 us -> 7.33 us
    ppermute x30 -> x8, starting transfers between devices: 38.6 us -> 10.7 us  [swap(): return lax.ppermute(x, 'dp', [(i, i ^ apart) for i in range(replicas)])]
    pallas_call x7 -> x12, Pallas kernels: 18.2 us -> 39.7 us  [call(): pl.pallas_call(run, name=name, out_shape=outs, in_specs=specs, out_specs=...]
    all_to_all x0 -> x4, starting transfers between devices: none -> 14.7 us  [exchange(): return lax.all_to_all(x, 'dp', 0, 0, axis_index_groups=members, tiled=True)]
    all_to_all x0 -> x4, waiting for transfers between devices: none -> 9.53 us  [exchange(): return lax.all_to_all(x, 'dp', 0, 0, axis_index_groups=members, tiled=True)]
    ppermute x30 -> x8, waiting for transfers between devices: 26 us -> 18.7 us  [swap(): return lax.ppermute(x, 'dp', [(i, i ^ apart) for i in range(replicas)])]
    convert_element_type x12 -> x1, other arithmetic: 3.34 us -> 0.72 us  [on_device(): grad_wout = jnp.concatenate([low, high], axis=1).astype(F32)[None]]
  transfers between devices with their start and end apart: 42 -> 18, of which waited for: 11 -> 6; matrix products, arithmetic and copies ran while one was open for 4% -> 4% of each run, Pallas kernels for 13% -> 32%
where the time goes in v3:
time: 109 us; the launch traced here: 108 us
  Pallas kernels  39.7 us (36%)
  waiting for transfers between devices  28.2 us (26%)
  starting transfers between devices  26.6 us (24%)
  local copies, waits for them, and re-layouts  7.33 us (7%)
  other arithmetic  5.21 us (5%)
    pallas_call x12, Pallas kernels, call(): pl.pallas_call(run, name=name, out_shape=outs, in_specs=specs, out_specs=...  39.7 us
    ppermute x8, waiting for transfers between devices, swap(): return lax.ppermute(x, 'dp', [(i, i ^ apart) for i in range(replicas)])  18.7 us
    all_to_all x4, starting transfers between devices, exchange(): return lax.all_to_all(x, 'dp', 0, 0, axis_index_groups=members, tiled=True)  14.7 us
    ppermute x8, starting transfers between devices, swap(): return lax.ppermute(x, 'dp', [(i, i ^ apart) for i in range(replicas)])  10.7 us
    all_to_all x4, waiting for transfers between devices, exchange(): return lax.all_to_all(x, 'dp', 0, 0, axis_index_groups=members, tiled=True)  9.53 us
    unnamed x28, local copies, waits for them, and re-layouts  7.33 us
    convert_element_type x1, other arithmetic, on_device(): hidden_out = (hidden_in.astype(F32) + contrib.astype(F32) + contrib_other...  2.24 us
    convert_element_type x1, other arithmetic, on_device(): grad_in = (grad_out.astype(F32) + returned.astype(F32) + returned_other.a...  2.24 us
  transfers between devices with their start and end apart: 18, of which 6 were waited for; matrix products, arithmetic and copies ran while one was open for 4% of the time, Pallas kernels for 32%

profile of v3, /device:TPU:0, one launch (start us, length us, event | category | flops | bytes accessed | tf_op | source)
XLA Modules:
  0.0 107.8 jit_solution(16234205515093775607)
XLA Ops:
  1.2 2.4 %prep.1 = (bf16[4,1024,128]{2,1,0:T(8,128)(2,1)}, bf16[128,1024]{1,0:T(8,128)(2,1)}) custom-call(bf16[128,2048]{1,0:T(8,128)(2,1)} %refs_0_.6, bf16[128,2048]{1,0:T(8,128)(2,1)} %refs_0_.7), custom_call_target="tpu_custom_call" | custom-call | tf_op jit(solution)/shard_map/prep/pallas_call | solution.py:51
  3.7 3.1 %collective-permute-start.3 = (bf16[128,1024]{1,0:T(8,128)(2,1)}, bf16[128,1024]{1,0:T(8,128)(2,1)S(1)}, u32[]{:S(2)}, u32[]{:S(2)}) collective-permute-start(bf16[128,1024]{1,0:T(8,128)(2,1)} %get-tuple-element.40), channel_id=1, source_target_pairs={{0,8},{2,10},{4,12},{6,14},{8,0},{10,2},{12,4},{14,6},{16,24},{18,... | collective-permute-start | bytes 786440 | tf_op jit(solution)/shard_map/ppermute | solution.py:369
  6.7 3.7 %all-to-all-start = ((bf16[4,1024,128]{2,1,0:T(8,128)(2,1)}), bf16[4,1024,128]{2,1,0:T(8,128)(2,1)S(1)}, u32[]{:S(2)}, u32[]{:S(2)}) async-start(bf16[4,1024,128]{2,1,0:T(8,128)(2,1)} %get-tuple-element.34.refs_9_), calls=%async_computation | async-start | bytes 2097152 | tf_op jit(solution)/shard_map/all_to_all | solution.py:376
  11.3 10.0 %attention.1 = (bf16[256,512]{1,0:T(8,128)(2,1)}, bf16[512,256]{1,0:T(8,128)(2,1)}, bf16[4,768,256]{2,1,0:T(8,128)(2,1)}) custom-call(s32[4,3]{1,0:T(4,128)} %refs_0_.5, bf16[128,2048]{1,0:T(8,128)(2,1)} %refs_0_.6, bf16[128,2048]{1,0:T(8,128)(2,1)} %collective-permute-done.refs_2_.refs_1_, bf16[2048,512]{1,0:T(8,128)(2,1)} %bitcast.14, ...), custom_call_target="tpu_custom_call" | custom-call | flops 11000000512 | tf_op jit(solution)/shard_map/attention/pallas_call | solution.py:51
  21.3 2.8 %all-to-all-done.refs_0_ = bf16[4,1024,128]{2,1,0:T(8,128)(2,1)S(1)} async-done(((bf16[4,1024,128]{2,1,0:T(8,128)(2,1)}), bf16[4,1024,128]{2,1,0:T(8,128)(2,1)S(1)}, u32[]{:S(2)}, u32[]{:S(2)}) %all-to-all-start) | async-done | bytes 1048608 | tf_op jit(solution)/shard_map/all_to_all | solution.py:376
  25.1 3.6 %all-to-all-start.1 = ((bf16[4,768,256]{2,1,0:T(8,128)(2,1)}), bf16[4,768,256]{2,1,0:T(8,128)(2,1)S(1)}, u32[]{:S(2)}, u32[]{:S(2)}) async-start(bf16[4,768,256]{2,1,0:T(8,128)(2,1)} %get-tuple-element.41.refs_7_), calls=%async_computation.1 | async-start | bytes 3145728 | tf_op jit(solution)/shard_map/all_to_all | solution.py:376
  29.6 6.6 %returned.1 = (bf16[128,2048]{1,0:T(8,128)(2,1)}, bf16[128,2048]{1,0:T(8,128)(2,1)}, bf16[128,2048]{1,0:T(8,128)(2,1)}, bf16[128,2048]{1,0:T(8,128)(2,1)}) custom-call(bf16[128,2048]{1,0:T(8,128)(2,1)} %refs_0_.6, bf16[128,2048]{1,0:T(8,128)(2,1)} %collective-permute-done.refs_2_.refs_1_, bf16[256,512]{1,0:T(8,128)(2,1)} %get-tuple-element.35.refs_2_, ...), custom_call_target="tpu_custom_call" | custom-call | tf_op jit(solution)/shard_map/returned/pallas_call | solution.py:51
  37.8 2.9 %out_grad.1 = (bf16[256,1024]{1,0:T(8,128)(2,1)}, bf16[256,1024]{1,0:T(8,128)(2,1)}) custom-call(bf16[128,2048]{1,0:T(8,128)(2,1)} %refs_0_.7, bf16[128,2048]{1,0:T(8,128)(2,1)} %copy-done.6, bf16[128,1024]{1,0:T(8,128)(2,1)} %copy-done.9, bf16[128,1024]{1,0:T(8,128)(2,1)} %collective-permute-done.4.refs_3_, bf16[512,256]{1,0:T(8,128)(2,1)} %get-tuple-element.43.refs_4_, ...), custom_call_target="tpu_custom_call" | custom-call | tf_op jit(solution)/shard_map/out_grad/pallas_call | solution.py:51
  40.7 6.6 %all-to-all-done.1.refs_2_ = bf16[4,768,256]{2,1,0:T(8,128)(2,1)S(1)} async-done(((bf16[4,768,256]{2,1,0:T(8,128)(2,1)}), bf16[4,768,256]{2,1,0:T(8,128)(2,1)S(1)}, u32[]{:S(2)}, u32[]{:S(2)}) %all-to-all-start.1) | async-done | bytes 1572896 | tf_op jit(solution)/shard_map/all_to_all | solution.py:376
  48.5 4.9 %projection_grad.1 = (bf16[512,512]{1,0:T(8,128)(2,1)}, bf16[512,512]{1,0:T(8,128)(2,1)}, bf16[512,256]{1,0:T(8,128)(2,1)}, bf16[512,256]{1,0:T(8,128)(2,1)}) custom-call(bf16[4,1024,128]{2,1,0:T(8,128)(2,1)} %copy-done.3, bf16[4,1024,128]{2,1,0:T(8,128)(2,1)} %collective-permute-done.2.refs_1_, bf16[4,768,256]{2,1,0:T(8,128)(2,1)} %copy-done, ...), custom_call_target="tpu_custom_call" | custom-call | tf_op jit(solution)/shard_map/projection_grad/pallas_call | solution.py:51
  55.3 11.2 %collective-permute-done.10.refs_1_ = bf16[512,512]{1,0:T(8,128)(2,1)S(1)} collective-permute-done((bf16[512,512]{1,0:T(8,128)(2,1)}, bf16[512,512]{1,0:T(8,128)(2,1)S(1)}, u32[]{:S(2)}, u32[]{:S(2)}) %collective-permute-start.10) | collective-permute-done | bytes 524320 | tf_op jit(solution)/shard_map/ppermute | solution.py:369
  67.3 2.1 %add.22.refs_2_ = bf16[512,512]{1,0:T(8,128)(2,1)} custom-call(bf16[512,512]{1,0:T(8,128)(2,1)} %get-tuple-element.53.refs_0_, bf16[512,512]{1,0:T(8,128)(2,1)} %copy-done.8, bf16[512,512]{1,0:T(8,128)(2,1)} %get-tuple-element.45.refs_2_), custom_call_target="tpu_custom_call" | custom-call | tf_op jit(solution)/shard_map/add/pallas_call | solution.py:51
  69.5 4.0 %all-to-all-start.3 = ((bf16[4,128,512]{2,1,0:T(8,128)(2,1)}), bf16[4,128,512]{2,1,0:T(8,128)(2,1)S(1)}, u32[]{:S(2)}, u32[]{:S(2)}) async-start(bf16[4,128,512]{2,1,0:T(8,128)(2,1)} %bitcast.13), calls=%async_computation.3 | async-start | bytes 1048576 | tf_op jit(solution)/shard_map/all_to_all | solution.py:376
  74.7 2.1 %halve.3 = (bf16[128,1024]{1,0:T(8,128)(2,1)}, bf16[128,1024]{1,0:T(8,128)(2,1)}) custom-call(bf16[256,1024]{1,0:T(8,128)(2,1)} %get-tuple-element.52.refs_0_, bf16[256,1024]{1,0:T(8,128)(2,1)} %copy-done.7, bf16[512,512]{1,0:T(8,128)(2,1)} %add.22.refs_2_), custom_call_target="tpu_custom_call" | custom-call | tf_op jit(solution)/shard_map/halve/pallas_call | solution.py:51
  77.3 5.9 %collective-permute-done.8.refs_1_ = bf16[512,256]{1,0:T(8,128)(2,1)S(1)} collective-permute-done((bf16[512,256]{1,0:T(8,128)(2,1)}, bf16[512,256]{1,0:T(8,128)(2,1)S(1)}, u32[]{:S(2)}, u32[]{:S(2)}) %collective-permute-start.8) | collective-permute-done | bytes 262176 | tf_op jit(solution)/shard_map/ppermute | solution.py:369
  83.9 1.8 %add.23.refs_2_ = bf16[512,256]{1,0:T(8,128)(2,1)} custom-call(bf16[512,256]{1,0:T(8,128)(2,1)} %get-tuple-element.50.refs_0_, bf16[512,256]{1,0:T(8,128)(2,1)} %copy-done.11, bf16[128,1024]{1,0:T(8,128)(2,1)} %get-tuple-element.54.refs_2_), custom_call_target="tpu_custom_call" | custom-call | tf_op jit(solution)/shard_map/add/pallas_call | solution.py:51
  86.4 1.7 %halve.4 = (bf16[64,1024]{1,0:T(8,128)(2,1)}, bf16[64,1024]{1,0:T(8,128)(2,1)}) custom-call(bf16[128,1024]{1,0:T(8,128)(2,1)} %get-tuple-element.55.refs_0_, bf16[128,1024]{1,0:T(8,128)(2,1)} %copy-done.10, bf16[512,256]{1,0:T(8,128)(2,1)} %add.23.refs_2_), custom_call_target="tpu_custom_call" | custom-call | tf_op jit(solution)/shard_map/halve/pallas_call | solution.py:51
  88.2 3.4 %collective-permute-start.12 = (bf16[64,1024]{1,0:T(8,128)(2,1)}, bf16[64,1024]{1,0:T(8,128)(2,1)S(1)}, u32[]{:S(2)}, u32[]{:S(2)}) collective-permute-start(bf16[64,1024]{1,0:T(8,128)(2,1)} %get-tuple-element.57.refs_1_), channel_id=1, source_target_pairs={{0,16},{2,18},{4,20},{6,22},{8,24},{10,26},{12,28},{14,30},{16,0},... | collective-permute-start | bytes 393224 | tf_op jit(solution)/shard_map/ppermute | solution.py:369
  91.6 2.2 %add_convert_fusion.1 = bf16[128,2048]{1,0:T(8,128)(2,1)} fusion(bf16[128,2048]{1,0:T(8,128)(2,1)} %collective-permute-done.6, bf16[128,2048]{1,0:T(8,128)(2,1)} %get-tuple-element.37.refs_6_, bf16[128,2048]{1,0:T(8,128)(2,1)S(1)} %copy-done.1), kind=kLoop, calls=%fused_computation.1 | loop fusion | flops 1572864 | bytes 2097152 | tf_op jit(solution)/shard_map/convert_element_type | solution.py:527
  93.9 3.4 %all-to-all-start.2 = ((bf16[4,128,256]{2,1,0:T(8,128)(2,1)}), bf16[4,128,256]{2,1,0:T(8,128)(2,1)S(1)}, u32[]{:S(2)}, u32[]{:S(2)}) async-start(bf16[4,128,256]{2,1,0:T(8,128)(2,1)} %bitcast.4), calls=%async_computation.2 | async-start | bytes 524288 | tf_op jit(solution)/shard_map/all_to_all | solution.py:376
  97.3 1.9 %final.2 = (f32[128,512]{1,0:T(8,128)}, f32[128,512]{1,0:T(8,128)}) custom-call(bf16[4,128,512]{2,1,0:T(8,128)(2,1)} %copy-done.4, bf16[64,1024]{1,0:T(8,128)(2,1)} %get-tuple-element.57.refs_1_), custom_call_target="tpu_custom_call" | custom-call | tf_op jit(solution)/shard_map/final/pallas_call | solution.py:51
  99.8 1.6 %halve.5 = (bf16[32,1024]{1,0:T(8,128)(2,1)}, bf16[32,1024]{1,0:T(8,128)(2,1)}) custom-call(bf16[64,1024]{1,0:T(8,128)(2,1)} %get-tuple-element.56.refs_0_, bf16[64,1024]{1,0:T(8,128)(2,1)} %copy-done.12, f32[128,512]{1,0:T(8,128)} %get-tuple-element.58.refs_2_), custom_call_target="tpu_custom_call" | custom-call | tf_op jit(solution)/shard_map/halve/pallas_call | solution.py:51
  102.3 2.2 %add_convert_fusion = bf16[128,2048]{1,0:T(8,128)(2,1)} fusion(bf16[128,2048]{1,0:T(8,128)(2,1)} %collective-permute-done.7, bf16[128,2048]{1,0:T(8,128)(2,1)} %get-tuple-element.47, bf16[128,2048]{1,0:T(8,128)(2,1)S(1)} %copy-done.2), kind=kLoop, calls=%fused_computation | loop fusion | flops 1572864 | bytes 2097152 | tf_op jit(solution)/shard_map/convert_element_type | solution.py:530
  105.4 1.7 %final.3 = f32[128,512]{1,0:T(8,128)} custom-call(bf16[4,128,256]{2,1,0:T(8,128)(2,1)} %copy-done.5, bf16[32,1024]{1,0:T(8,128)(2,1)} %get-tuple-element.59.refs_1_), custom_call_target="tpu_custom_call" | custom-call | tf_op jit(solution)/shard_map/final/pallas_call | solution.py:51
  (56 shorter events, 15.2 us)
Async XLA Ops:
  0.6 9.8 %collective-permute-start = (bf16[128,2048]{1,0:T(8,128)(2,1)}, bf16[128,2048]{1,0:T(8,128)(2,1)}, u32[]{:S(2)}, u32[]{:S(2)}) collective-permute-start(bf16[128,2048]{1,0:T(8,128)(2,1)} %refs_0_.6), channel_id=1, source_target_pairs={{0,1},{1,0},{2,3},{3,2},{4,5},{5,4},{6,7},{7,6},{8,9},{9,8},{10,11... | collective-permute-start | bytes 1572872 | tf_op jit(solution)/shard_map/ppermute | solution.py:372
  1.1 9.3 %collective-permute-start.1 = (bf16[128,2048]{1,0:T(8,128)(2,1)}, bf16[128,2048]{1,0:T(8,128)(2,1)S(1)}, u32[]{:S(2)}, u32[]{:S(2)}) collective-permute-start(bf16[128,2048]{1,0:T(8,128)(2,1)} %refs_0_.7), channel_id=1, source_target_pairs={{0,1},{1,0},{2,3},{3,2},{4,5},{5,4},{6,7},{7,6},{8,9},{9,8},{10,11... | collective-permute-start | bytes 1572872 | tf_op jit(solution)/shard_map/ppermute | solution.py:372
  3.7 17.6 %collective-permute-start.3 = (bf16[128,1024]{1,0:T(8,128)(2,1)}, bf16[128,1024]{1,0:T(8,128)(2,1)S(1)}, u32[]{:S(2)}, u32[]{:S(2)}) collective-permute-start(bf16[128,1024]{1,0:T(8,128)(2,1)} %get-tuple-element.40), channel_id=1, source_target_pairs={{0,8},{2,10},{4,12},{6,14},{8,0},{10,2},{12,4},{14,6},{16,24},{18,... | collective-permute-start | bytes 786440 | tf_op jit(solution)/shard_map/ppermute | solution.py:369
  6.7 17.4 %all-to-all-start = ((bf16[4,1024,128]{2,1,0:T(8,128)(2,1)}), bf16[4,1024,128]{2,1,0:T(8,128)(2,1)S(1)}, u32[]{:S(2)}, u32[]{:S(2)}) async-start(bf16[4,1024,128]{2,1,0:T(8,128)(2,1)} %get-tuple-element.34.refs_9_), calls=%async_computation | async-start | bytes 2097152 | tf_op jit(solution)/shard_map/all_to_all | solution.py:376
  21.3 15.0 %copy-start.9 = (bf16[128,1024]{1,0:T(8,128)(2,1)}, bf16[128,1024]{1,0:T(8,128)(2,1)S(1)}, u32[]{:S(2)}) copy-start(bf16[128,1024]{1,0:T(8,128)(2,1)S(1)} %collective-permute-done.3.refs_2_) | copy-start | bytes 786436
  25.1 22.2 %all-to-all-start.1 = ((bf16[4,768,256]{2,1,0:T(8,128)(2,1)}), bf16[4,768,256]{2,1,0:T(8,128)(2,1)S(1)}, u32[]{:S(2)}, u32[]{:S(2)}) async-start(bf16[4,768,256]{2,1,0:T(8,128)(2,1)} %get-tuple-element.41.refs_7_), calls=%async_computation.1 | async-start | bytes 3145728 | tf_op jit(solution)/shard_map/all_to_all | solution.py:376
  28.6 18.7 %collective-permute-start.2 = (bf16[4,1024,128]{2,1,0:T(8,128)(2,1)}, bf16[4,1024,128]{2,1,0:T(8,128)(2,1)}, u32[]{:S(2)}, u32[]{:S(2)}) collective-permute-start(bf16[4,1024,128]{2,1,0:T(8,128)(2,1)} %copy-done.3), channel_id=1, source_target_pairs={{0,1},{1,0},{2,3},{3,2},{4,5},{5,4},{6,7},{7,6},{8,9},{9,8},{10,11... | collective-permute-start | bytes 3145736 | tf_op jit(solution)/shard_map/ppermute | solution.py:372
  28.7 7.5 %collective-permute-start.4 = (bf16[128,1024]{1,0:T(8,128)(2,1)S(1)}, bf16[128,1024]{1,0:T(8,128)(2,1)}, u32[]{:S(2)}, u32[]{:S(2)}) collective-permute-start(bf16[128,1024]{1,0:T(8,128)(2,1)S(1)} %collective-permute-done.3.refs_2_), channel_id=1, source_target_pairs={{0,1},{1,0},{2,3},{3,2},{4,5},{5,4},{6,7},{7,6},{8,9},{9,8},{10,11... | collective-permute-start | bytes 786440 | tf_op jit(solution)/shard_map/ppermute | solution.py:372
  29.2 8.6 %collective-permute-start.5 = (bf16[512,256]{1,0:T(8,128)(2,1)}, bf16[512,256]{1,0:T(8,128)(2,1)}, u32[]{:S(2)}, u32[]{:S(2)}) collective-permute-start(bf16[512,256]{1,0:T(8,128)(2,1)} %get-tuple-element.43.refs_4_), channel_id=1, source_target_pairs={{0,8},{2,10},{4,12},{6,14},{8,0},{10,2},{12,4},{14,6},{16,24},{18,... | collective-permute-start | bytes 786440 | tf_op jit(solution)/shard_map/ppermute | solution.py:369
  47.3 1.2 %copy-start = (bf16[4,768,256]{2,1,0:T(8,128)(2,1)}, bf16[4,768,256]{2,1,0:T(8,128)(2,1)S(1)}, u32[]{:S(2)}) copy-start(bf16[4,768,256]{2,1,0:T(8,128)(2,1)S(1)} %all-to-all-done.1.refs_2_) | copy-start | bytes 4718596
  53.4 13.1 %collective-permute-start.10 = (bf16[512,512]{1,0:T(8,128)(2,1)}, bf16[512,512]{1,0:T(8,128)(2,1)S(1)}, u32[]{:S(2)}, u32[]{:S(2)}) collective-permute-start(bf16[512,512]{1,0:T(8,128)(2,1)} %get-tuple-element.45.refs_2_), channel_id=1, source_target_pairs={{0,8},{2,10},{4,12},{6,14},{8,0},{10,2},{12,4},{14,6},{16,24},{18,... | collective-permute-start | bytes 1572872 | tf_op jit(solution)/shard_map/ppermute | solution.py:369
  53.9 20.1 %collective-permute-start.9 = (bf16[256,1024]{1,0:T(8,128)(2,1)}, bf16[256,1024]{1,0:T(8,128)(2,1)S(1)}, u32[]{:S(2)}, u32[]{:S(2)}) collective-permute-start(bf16[256,1024]{1,0:T(8,128)(2,1)} %get-tuple-element.44.refs_3_), channel_id=1, source_target_pairs={{0,4},{2,6},{4,0},{6,2},{8,12},{10,14},{12,8},{14,10},{16,20},{18,... | collective-permute-start | bytes 1572872 | tf_op jit(solution)/shard_map/ppermute | solution.py:369
  55.3 36.3 %collective-permute-start.6 = (bf16[128,2048]{1,0:T(8,128)(2,1)}, bf16[128,2048]{1,0:T(8,128)(2,1)}, u32[]{:S(2)}, u32[]{:S(2)}) collective-permute-start(bf16[128,2048]{1,0:T(8,128)(2,1)} %get-tuple-element.46), channel_id=1, source_target_pairs={{0,1},{1,0},{2,3},{3,2},{4,5},{5,4},{6,7},{7,6},{8,9},{9,8},{10,11... | collective-permute-start | bytes 1572872 | tf_op jit(solution)/shard_map/ppermute | solution.py:372
  69.4 22.2 %copy-start.1 = (bf16[128,2048]{1,0:T(8,128)(2,1)S(1)}, bf16[128,2048]{1,0:T(8,128)(2,1)}, u32[]{:S(2)}) copy-start(bf16[128,2048]{1,0:T(8,128)(2,1)} %refs_0_.6) | copy-start | bytes 1572868
  69.5 24.4 %all-to-all-start.3 = ((bf16[4,128,512]{2,1,0:T(8,128)(2,1)}), bf16[4,128,512]{2,1,0:T(8,128)(2,1)S(1)}, u32[]{:S(2)}, u32[]{:S(2)}) async-start(bf16[4,128,512]{2,1,0:T(8,128)(2,1)} %bitcast.13), calls=%async_computation.3 | async-start | bytes 1048576 | tf_op jit(solution)/shard_map/all_to_all | solution.py:376
  73.5 9.8 %collective-permute-start.8 = (bf16[512,256]{1,0:T(8,128)(2,1)}, bf16[512,256]{1,0:T(8,128)(2,1)S(1)}, u32[]{:S(2)}, u32[]{:S(2)}) collective-permute-start(bf16[512,256]{1,0:T(8,128)(2,1)} %get-tuple-element.51), channel_id=1, source_target_pairs={{0,8},{2,10},{4,12},{6,14},{8,0},{10,2},{12,4},{14,6},{16,24},{18,... | collective-permute-start | bytes 786440 | tf_op jit(solution)/shard_map/ppermute | solution.py:369
  76.8 8.9 %collective-permute-start.11 = (bf16[128,1024]{1,0:T(8,128)(2,1)}, bf16[128,1024]{1,0:T(8,128)(2,1)S(1)}, u32[]{:S(2)}, u32[]{:S(2)}) collective-permute-start(bf16[128,1024]{1,0:T(8,128)(2,1)} %get-tuple-element.54.refs_2_), channel_id=1, source_target_pairs={{0,2},{2,0},{4,6},{6,4},{8,10},{10,8},{12,14},{14,12},{16,18},{18,... | collective-permute-start | bytes 786440 | tf_op jit(solution)/shard_map/ppermute | solution.py:369
  77.3 25.0 %collective-permute-start.7 = (bf16[128,2048]{1,0:T(8,128)(2,1)}, bf16[128,2048]{1,0:T(8,128)(2,1)}, u32[]{:S(2)}, u32[]{:S(2)}) collective-permute-start(bf16[128,2048]{1,0:T(8,128)(2,1)} %get-tuple-element.49), channel_id=1, source_target_pairs={{0,1},{1,0},{2,3},{3,2},{4,5},{5,4},{6,7},{7,6},{8,9},{9,8},{10,11... | collective-permute-start | bytes 1572872 | tf_op jit(solution)/shard_map/ppermute | solution.py:372
  88.2 14.2 %copy-start.2 = (bf16[128,2048]{1,0:T(8,128)(2,1)S(1)}, bf16[128,2048]{1,0:T(8,128)(2,1)}, u32[]{:S(2)}) copy-start(bf16[128,2048]{1,0:T(8,128)(2,1)} %refs_0_.7) | copy-start | bytes 1572868
  88.2 11.0 %collective-permute-start.12 = (bf16[64,1024]{1,0:T(8,128)(2,1)}, bf16[64,1024]{1,0:T(8,128)(2,1)S(1)}, u32[]{:S(2)}, u32[]{:S(2)}) collective-permute-start(bf16[64,1024]{1,0:T(8,128)(2,1)} %get-tuple-element.57.refs_1_), channel_id=1, source_target_pairs={{0,16},{2,18},{4,20},{6,22},{8,24},{10,26},{12,28},{14,30},{16,0},... | collective-permute-start | bytes 393224 | tf_op jit(solution)/shard_map/ppermute | solution.py:369
  93.9 3.4 %copy-start.4 = (bf16[4,128,512]{2,1,0:T(8,128)(2,1)}, bf16[4,128,512]{2,1,0:T(8,128)(2,1)S(1)}, u32[]{:S(2)}) copy-start(bf16[4,128,512]{2,1,0:T(8,128)(2,1)S(1)} %all-to-all-done.3.refs_0_) | copy-start | bytes 1572868
  93.9 10.9 %all-to-all-start.2 = ((bf16[4,128,256]{2,1,0:T(8,128)(2,1)}), bf16[4,128,256]{2,1,0:T(8,128)(2,1)S(1)}, u32[]{:S(2)}, u32[]{:S(2)}) async-start(bf16[4,128,256]{2,1,0:T(8,128)(2,1)} %bitcast.4), calls=%async_computation.2 | async-start | bytes 524288 | tf_op jit(solution)/shard_map/all_to_all | solution.py:376
  101.4 5.7 %copy-start.13 = (bf16[32,1024]{1,0:T(8,128)(2,1)S(1)}, bf16[32,1024]{1,0:T(8,128)(2,1)}, u32[]{:S(2)}) copy-start(bf16[32,1024]{1,0:T(8,128)(2,1)} %get-tuple-element.61) | copy-start | bytes 196612
  101.4 5.7 %collective-permute-start.13 = (bf16[32,1024]{1,0:T(8,128)(2,1)}, bf16[32,1024]{1,0:T(8,128)(2,1)S(1)}, u32[]{:S(2)}, u32[]{:S(2)}) collective-permute-start(bf16[32,1024]{1,0:T(8,128)(2,1)} %get-tuple-element.59.refs_1_), channel_id=1, source_target_pairs={{0,8},{2,10},{4,12},{6,14},{8,0},{10,2},{12,4},{14,6},{16,24},{18,... | collective-permute-start | bytes 196616 | tf_op jit(solution)/shard_map/ppermute | solution.py:369
  (8 other events, 6.2 us)

commit v4 on v3

--- a/solution.py
+++ b/solution.py
@@ -11,20 +11,17 @@
 HDIM = 64
 NORM_EPS = 1e-05
 PAIR = 2 * HDIM
-VMEM_BYTES = 62 * 1024 * 1024
-
-ATTENTION_WORK = 11 * 10**9
+VMEM_BYTES = 64 * 1024 * 1024
+
+LONG_WORK = 11 * 10**9
 
 F32 = jnp.float32
 BF16 = jnp.bfloat16
 NT = (((1,), (1,)), ((), ()))
 TN = (((0,), (0,)), ((), ()))
 
-PROJECTION_BITS = (0, 1)
-OUT_BIT = 2
-
-UNITS = ((0, 1), (2,))
-
+PROJECTION_BITS = (2, 0)
+OUT_BIT = 1
 
 def dot(left, right):
     return jnp.dot(left, right, preferred_element_type=F32)
@@ -275,41 +272,35 @@
     returned_mirror[...] = returned[seq_len:]
 
 
-def projection_grad_body(first_bit, x_pieces, x_mirrors, g_pieces, *rest):
-    targets, (x_all, right, sems) = rest[: 2 * len(UNITS)], rest[2 * len(UNITS) :]
+def projection_grad_body(bits, x_pieces, x_mirrors, g_pieces, *rest):
+    pair_send, pair_keep, query_send, query_keep, x_all, right, sems = rest
     seq_len = x_pieces.shape[2]
     tokens = 2 * seq_len
     width = g_pieces.shape[2]
-    members = [member for unit in UNITS for member in unit]
     pairs = []
     for place in range(4):
         for at, source in enumerate((x_pieces, x_mirrors)):
             columns = pl.ds(place * tokens + at * seq_len, seq_len)
             pairs.append((source.at[place], x_all.at[:, columns]))
-        for at, member in enumerate(members):
-            target = right.at[pl.ds(place * tokens, tokens), pl.ds(at * width, width)]
+        for member in range(3):
+            target = right.at[pl.ds(place * tokens, tokens), pl.ds(member * width, width)]
             pairs.append((g_pieces.at[place, pl.ds(member * tokens, tokens)], target))
     finish(fetch(pairs, sems))
-    bit = bit_here(first_bit)
     rows = x_all.shape[0] // 2
-    for turn, side in ((0, 1 - bit), (1, bit)):
+    bit = bit_here(bits[0])
+    for target, side in ((pair_send, 1 - bit), (pair_keep, bit)):
         part = pl.ds(pl.multiple_of(side * rows, rows), rows)
-        column = 0
-        for unit in range(len(UNITS)):
-            target = targets[2 * unit + turn]
-            columns = slice(column, column + target.shape[1])
-            target[...] = dot(x_all[part, :], right[:, columns]).astype(BF16)
-            column += target.shape[1]
-
-
-def add_body(keep, arrived, total):
-    total[...] = (keep[...].astype(F32) + arrived[...].astype(F32)).astype(BF16)
-
-
-def out_grad_body(
-    first_bit, grad, g_mirror, g_piece, g_piece_mirror, att_own, att_piece, send, keep, *scratch
-):
-    left, right, sems = scratch
+        target[...] = dot(x_all[part, :], right[:, : 2 * width]).astype(BF16)
+    bit = bit_here(bits[1])
+    for target, side in ((query_send, 1 - bit), (query_keep, bit)):
+        for turn in range(2):
+            start = pl.multiple_of(turn * rows + side * (rows // 2), rows // 2)
+            grad = dot(x_all[pl.ds(start, rows // 2), :], right[:, 2 * width :]).astype(BF16)
+            target[turn * (rows // 2) : (turn + 1) * (rows // 2), :] = grad
+
+
+def out_grad_body(bits, grad, g_mirror, g_piece, g_piece_mirror, att_own, att_piece, *rest):
+    targets, (left, right, sems) = rest[:4], rest[4:]
     seq_len = grad.shape[0]
     tokens = 2 * seq_len
     columns = right.shape[1]
@@ -323,31 +314,51 @@
     ):
         pairs.append((source, right.at[pl.ds(place * seq_len, seq_len)]))
     finish(fetch(pairs, sems))
-    bit = bit_here(first_bit)
-    rows = left.shape[0] // 2
-    for target, side in ((send, 1 - bit), (keep, bit)):
-        part = pl.ds(pl.multiple_of(side * rows, rows), rows)
+    own = 2 * bit_here(bits[0]) + bit_here(bits[1])
+    rows = left.shape[0] // 4
+    for place, target in enumerate(targets):
+        part = pl.ds(pl.multiple_of((own ^ place) * rows, rows), rows)
         target[...] = dot(left[part, :], right[...]).astype(BF16)
 
 
-def final_body(count, pieces, *targets):
-    width = pieces.shape[2] // count
-    for at, target in enumerate(targets):
-        here = slice(at * width, (at + 1) * width)
-        for col in range(2):
-            total = pieces[col, :, here].astype(F32)
-            for place in range(1, pieces.shape[0] // 2):
-                total += pieces[2 * place + col, :, here].astype(F32)
-            target[:, col * width : (col + 1) * width] = total
-
-
-def halve_body(bit, keep, arrived, send, next_keep):
+def halve_body(bit, count, *refs):
+    sources, (send, keep, sides, sems) = refs[:count], refs[count:]
     here = bit_here(bit)
     rows = send.shape[0]
-    for target, side in ((send, 1 - here), (next_keep, here)):
+    pairs = []
+    for turn, side in ((0, 1 - here), (1, here)):
         part = pl.ds(pl.multiple_of(side * rows, rows), rows)
-        total = keep[part, :].astype(F32) + arrived[part, :].astype(F32)
+        pairs += [(ref.at[part], sides.at[turn, at]) for at, ref in enumerate(sources)]
+    copies = fetch(pairs, sems)
+    for turn, target in ((0, send), (1, keep)):
+        finish(copies[turn * count : (turn + 1) * count])
+        total = sides[turn, 0].astype(F32)
+        for at in range(1, count):
+            total += sides[turn, at].astype(F32)
         target[...] = total.astype(BF16)
+
+
+def out_final_body(keep, other, target):
+    columns = keep.shape[1]
+    here = bit_here(OUT_BIT)
+    for source, col in ((keep, here), (other, 1 - here)):
+        target[:, pl.ds(pl.multiple_of(col * columns, columns), columns)] = source[...].astype(F32)
+
+
+def final_body(pieces, query_keep, query_other, *targets):
+    columns = targets[0].shape[1] // 2
+    for col in range(2):
+        total = pieces[col].astype(F32)
+        for place in range(1, pieces.shape[0] // 2):
+            total += pieces[2 * place + col].astype(F32)
+        for member in range(2):
+            targets[member][:, col * columns : (col + 1) * columns] = total[
+                :, member * columns : (member + 1) * columns
+            ]
+    here = bit_here(PROJECTION_BITS[1])
+    for source, col in ((query_keep, here), (query_other, 1 - here)):
+        place = pl.ds(pl.multiple_of(col * columns, columns), columns)
+        targets[2][:, place] = source[...].astype(F32)
 
 
 def on_device(hidden_in, grad_out, w_query, w_key, w_value, w_out, pattern):
@@ -415,7 +426,7 @@
             pltpu.VMEM((half, tokens), BF16),
             pltpu.SemaphoreType.DMA((8,)),
         ],
-        work=ATTENTION_WORK,
+        work=LONG_WORK,
         scalars=1,
         far=8,
         after=(x_blocks,),
@@ -441,94 +452,95 @@
         far=8,
     )
 
-    out_send, out_keep = call(
-        functools.partial(out_grad_body, out_bits[0]),
+    out_keep, *out_sends = call(
+        functools.partial(out_grad_body, out_bits[:2]),
         "out_grad",
         (grad_out, g_mirror, g_piece, g_piece_mirror, att_turned, att_piece),
-        [bf16(half // 2, part)] * 2,
+        [bf16(half // 4, part)] * 4,
         [
             pltpu.VMEM((half, 2 * tokens), BF16),
             pltpu.VMEM((2 * tokens, part), BF16),
             pltpu.SemaphoreType.DMA((6,)),
         ],
         far=6,
-        after=(contrib,),
-    )
-    parts = call(
-        functools.partial(projection_grad_body, halved_bits[0]),
+        after=(contrib, x_mirrors),
+    )
+    out_arrived = [
+        swap(out_sends[0], out_bits[1]),
+        swap(out_sends[1], out_bits[0]),
+        swap(out_sends[2], *out_bits[:2]),
+    ]
+    pair_send, pair_keep, query_send, query_keep = call(
+        functools.partial(projection_grad_body, halved_bits),
         "projection_grad",
         (x_pieces, x_mirrors, g_pieces),
-        [bf16(part // 2, len(unit) * width) for unit in UNITS for _ in range(2)],
+        [bf16(part // 2, 2 * width)] * 2 + [bf16(part // 2, width)] * 2,
         [
             pltpu.VMEM((part, 4 * tokens), BF16),
             pltpu.VMEM((4 * tokens, 3 * width), BF16),
             pltpu.SemaphoreType.DMA((20,)),
         ],
         far=3,
-        after=(out_send,),
-    )
-    last_parts = parts[0]
-
-    def halve(place, send, keep, after):
+        after=(out_keep,),
+    )
+    pair_arrived = swap(pair_send, halved_bits[0])
+    query_arrived = swap(query_send, halved_bits[1])
+
+    def halve(arrays, next_bit, after, work=0):
+        count, shape = len(arrays), (arrays[0].shape[0] // 2, arrays[0].shape[1])
         return call(
-            functools.partial(halve_body, (out_bits + [OUT_BIT])[place + 1]),
+            functools.partial(halve_body, next_bit, count),
             "halve",
-            (keep, swap(send, out_bits[place])),
-            [bf16(keep.shape[0] // 2, part)] * 2,
+            arrays,
+            [bf16(*shape)] * 2,
+            [pltpu.VMEM((2, count, *shape), BF16), pltpu.SemaphoreType.DMA((2 * count,))],
+            work=work,
+            far=count,
             after=(after,),
         )
 
-    def add(unit, after):
-        send, keep = parts[2 * unit : 2 * unit + 2]
-        return call(
-            add_body,
-            "add",
-            (keep, swap(send, halved_bits[0])),
-            [bf16(*keep.shape)],
-            after=(after,),
-        )[0]
-
-    def finals(unit, total, after):
-        pieces = exchange(total, halved_bits[1:] + [col_bit])
-        members = UNITS[unit]
-        return call(
-            functools.partial(final_body, len(members)),
-            "final",
-            (pieces.reshape(2 << (len(halved_bits) - 1), -1, total.shape[1]),),
-            [jax.ShapeDtypeStruct((features // replicas, half), F32)] * len(members),
-            after=(after,),
-        )
-
-    totals = []
-    last = parts[0]
-    for unit in range(len(UNITS)):
-        totals.append(add(unit, last))
-        out_send, out_keep = halve(unit, out_send, out_keep, totals[-1])
-        last = out_send
-    found = {}
-    for unit, members in enumerate(UNITS):
-        grads = finals(unit, totals[unit], last)
-        found |= {member: grad[None] for member, grad in zip(members, grads)}
-        if len(UNITS) + unit < len(out_bits):
-            out_send, out_keep = halve(len(UNITS) + unit, out_send, out_keep, grads[0])
-            last = out_send
-    for place in range(2 * len(UNITS), len(out_bits)):
-        out_send, out_keep = halve(place, out_send, out_keep, last)
-    out_other = swap(out_send, OUT_BIT)
-    own_low = (lax.axis_index("dp") >> OUT_BIT) & 1 == 0
-    low = jnp.where(own_low, out_keep, out_other)
-    high = jnp.where(own_low, out_other, out_keep)
-    grad_wout = jnp.concatenate([low, high], axis=1).astype(F32)[None]
-
-    contrib_other = mirror(follows(contrib_mirror, parts[0]))
-    returned_other = mirror(follows(returned_mirror, last_parts))
+    def stepped(arrays, bits, after, work=0):
+        send, keep = halve(arrays, bits[0], after, work)
+        return [keep, swap(send, bits[0])], bits[1:], send
+
+    out, out_left, last = stepped(
+        [out_keep] + out_arrived, out_bits[2:] + [OUT_BIT], pair_send, LONG_WORK
+    )
+    contrib_other = mirror(follows(contrib_mirror, last))
+    returned_other = mirror(follows(returned_mirror, last))
     hidden_out = (
         hidden_in.astype(F32) + contrib.astype(F32) + contrib_other.astype(F32)
     ).astype(BF16)
     grad_in = (
         grad_out.astype(F32) + returned.astype(F32) + returned_other.astype(F32)
     ).astype(BF16)
-    return (hidden_out, grad_in, found[2], found[1], found[0], grad_wout)
+
+    pair_total = pair_keep.astype(F32) + follows(pair_arrived, (last, query_arrived)).astype(F32)
+    pair_total = pair_total.astype(BF16)
+    pieces = exchange(pair_total, halved_bits[1:] + [col_bit])
+    query, query_left = [query_keep, query_arrived], [halved_bits[0]] + halved_bits[2:] + [col_bit]
+    last = pair_total
+    while query_left or out_left:
+        if query_left:
+            query, query_left, last = stepped(query, query_left, last)
+        if out_left:
+            out, out_left, last = stepped(out, out_left, last)
+    (grad_wout,) = call(
+        out_final_body,
+        "out_final",
+        out,
+        [jax.ShapeDtypeStruct((half // replicas, features), F32)],
+        after=(last,),
+    )
+    grads = call(
+        final_body,
+        "final",
+        (pieces.reshape(1 << len(halved_bits), -1, 2 * width), *query),
+        [jax.ShapeDtypeStruct((features // replicas, half), F32)] * 3,
+        after=(grad_wout,),
+    )
+    grad_value, grad_key, grad_query = (grad[None] for grad in grads)
+    return (hidden_out, grad_in, grad_query, grad_key, grad_value, grad_wout[None])
 
 
 def solution(mesh):

time: 109 us -> 93.7 us (0.86)
  the two profiles are of different devices: /device:TPU:0 before, /device:TPU:8 now
where the time goes in v4:
time: 93.7 us; the launch traced here: 93 us
  starting transfers between devices  37.7 us (40%)
  Pallas kernels  37.3 us (40%)
  waiting for transfers between devices  9.56 us (10%)
  other arithmetic  6.92 us (7%)
    pallas_call x11, Pallas kernels, call(): pl.pallas_call(run, name=name, out_shape=outs, in_specs=specs, out_specs=...  37.3 us
    ppermute x11, starting transfers between devices, swap(): return lax.ppermute(x, 'dp', [(i, i ^ apart) for i in range(replicas)])  18.6 us
    all_to_all x3, starting transfers between devices, exchange(): return lax.all_to_all(x, 'dp', 0, 0, axis_index_groups=members, tiled=True)  17.7 us
    all_to_all x3, waiting for transfers between devices, exchange(): return lax.all_to_all(x, 'dp', 0, 0, axis_index_groups=members, tiled=True)  5.03 us
    ppermute x11, waiting for transfers between devices, swap(): return lax.ppermute(x, 'dp', [(i, i ^ apart) for i in range(replicas)])  4.24 us
    convert_element_type x1, other arithmetic, on_device(): grad_in = (grad_out.astype(F32) + returned.astype(F32) + returned_other.a...  2.39 us
    convert_element_type x1, other arithmetic, on_device(): hidden_out = (hidden_in.astype(F32) + contrib.astype(F32) + contrib_other...  2.39 us
    convert_element_type x1, other arithmetic, on_device(): pair_total = pair_total.astype(BF16)  2.13 us
  transfers between devices with their start and end apart: 20, of which 6 were waited for; matrix products, arithmetic and copies ran while one was open for 7% of the time, Pallas kernels for 35%

profile of v4, /device:TPU:8, one launch (start us, length us, event | category | flops | bytes accessed | tf_op | source)
XLA Modules:
  0.0 93.0 jit_solution(4687929652723838187)
XLA Ops:
  0.6 2.4 %prep.1 = (bf16[4,1024,128]{2,1,0:T(8,128)(2,1)}, bf16[128,1024]{1,0:T(8,128)(2,1)}) custom-call(bf16[128,2048]{1,0:T(8,128)(2,1)} %refs_0_.6, bf16[128,2048]{1,0:T(8,128)(2,1)} %refs_0_.7), custom_call_target="tpu_custom_call" | custom-call | tf_op jit(solution)/shard_map/prep/pallas_call | solution.py:48
  3.1 4.4 %all-to-all-start = ((bf16[4,1024,128]{2,1,0:T(8,128)(2,1)}), bf16[4,1024,128]{2,1,0:T(8,128)(2,1)}, u32[]{:S(2)}, u32[]{:S(2)}) async-start(bf16[4,1024,128]{2,1,0:T(8,128)(2,1)} %get-tuple-element.40.refs_9_), calls=%async_computation | async-start | bytes 2097152 | tf_op jit(solution)/shard_map/all_to_all | solution.py:387
  8.1 1.9 %collective-permute-start.2 = (bf16[128,1024]{1,0:T(8,128)(2,1)}, bf16[128,1024]{1,0:T(8,128)(2,1)}, u32[]{:S(2)}, u32[]{:S(2)}) collective-permute-start(bf16[128,1024]{1,0:T(8,128)(2,1)} %get-tuple-element.45), channel_id=1, source_target_pairs={{0,4},{2,6},{4,0},{6,2},{8,12},{10,14},{12,8},{14,10},{16,20},{18,... | collective-permute-start | bytes 786440 | tf_op jit(solution)/shard_map/ppermute | solution.py:380
  11.0 10.0 %attention.1 = (bf16[256,512]{1,0:T(8,128)(2,1)}, bf16[512,256]{1,0:T(8,128)(2,1)}, bf16[4,768,256]{2,1,0:T(8,128)(2,1)}) custom-call(s32[4,3]{1,0:T(4,128)} %refs_0_.5, bf16[128,2048]{1,0:T(8,128)(2,1)} %refs_0_.6, bf16[128,2048]{1,0:T(8,128)(2,1)} %copy-done.3, bf16[2048,512]{1,0:T(8,128)(2,1)} %bitcast.9, bf16[2048,512]{1,0:T(8,128)(2,1)} %bitcast.11, ...), custom_call_target="tpu_custom_call" | custom-call | flops 11000000512 | tf_op jit(solution)/shard_map/attention/pallas_call | solution.py:48
  21.2 4.8 %all-to-all-start.1 = ((bf16[4,768,256]{2,1,0:T(8,128)(2,1)}), bf16[4,768,256]{2,1,0:T(8,128)(2,1)}, u32[]{:S(2)}, u32[]{:S(2)}) async-start(bf16[4,768,256]{2,1,0:T(8,128)(2,1)} %get-tuple-element.53.refs_7_), calls=%async_computation.1 | async-start | bytes 3145728 | tf_op jit(solution)/shard_map/all_to_all | solution.py:387
  26.6 1.7 %collective-permute-start.4 = (bf16[512,256]{1,0:T(8,128)(2,1)}, bf16[512,256]{1,0:T(8,128)(2,1)}, u32[]{:S(2)}, u32[]{:S(2)}) collective-permute-start(bf16[512,256]{1,0:T(8,128)(2,1)} %get-tuple-element.47.refs_4_), channel_id=1, source_target_pairs={{0,4},{2,6},{4,0},{6,2},{8,12},{10,14},{12,8},{14,10},{16,20},{18,... | collective-permute-start | bytes 786440 | tf_op jit(solution)/shard_map/ppermute | solution.py:380
  28.2 6.7 %returned.1 = (bf16[128,2048]{1,0:T(8,128)(2,1)}, bf16[128,2048]{1,0:T(8,128)(2,1)}, bf16[128,2048]{1,0:T(8,128)(2,1)}, bf16[128,2048]{1,0:T(8,128)(2,1)}) custom-call(bf16[128,2048]{1,0:T(8,128)(2,1)} %refs_0_.6, bf16[128,2048]{1,0:T(8,128)(2,1)} %copy-done.3, bf16[256,512]{1,0:T(8,128)(2,1)} %get-tuple-element.41.refs_2_, bf16[512,2048]{1,0:T(8,128)(2,1)} %bitcast.16, ...), custom_call_target="tpu_custom_call" | custom-call | tf_op jit(solution)/shard_map/returned/pallas_call | solution.py:48
  35.1 2.8 %out_grad.1 = (bf16[128,1024]{1,0:T(8,128)(2,1)}, bf16[128,1024]{1,0:T(8,128)(2,1)}, bf16[128,1024]{1,0:T(8,128)(2,1)}, bf16[128,1024]{1,0:T(8,128)(2,1)}) custom-call(bf16[128,2048]{1,0:T(8,128)(2,1)} %refs_0_.7, bf16[128,2048]{1,0:T(8,128)(2,1)} %copy-done.2, bf16[128,1024]{1,0:T(8,128)(2,1)} %collective-permute-done.2.refs_2_, ...), custom_call_target="tpu_custom_call" | custom-call | tf_op jit(solution)/shard_map/out_grad/pallas_call | solution.py:48
  38.2 1.8 %collective-permute-start.7 = (bf16[128,1024]{1,0:T(8,128)(2,1)}, bf16[128,1024]{1,0:T(8,128)(2,1)}, u32[]{:S(2)}, u32[]{:S(2)}) collective-permute-start(bf16[128,1024]{1,0:T(8,128)(2,1)} %get-tuple-element.51), channel_id=1, source_target_pairs={{0,2},{2,0},{4,6},{6,4},{8,10},{10,8},{12,14},{14,12},{16,18},{18,... | collective-permute-start | bytes 786440 | tf_op jit(solution)/shard_map/ppermute | solution.py:380
  41.5 4.8 %all-to-all-done.1.refs_2_ = bf16[4,768,256]{2,1,0:T(8,128)(2,1)} async-done(((bf16[4,768,256]{2,1,0:T(8,128)(2,1)}), bf16[4,768,256]{2,1,0:T(8,128)(2,1)}, u32[]{:S(2)}, u32[]{:S(2)}) %all-to-all-start.1) | async-done | bytes 1572896 | tf_op jit(solution)/shard_map/all_to_all | solution.py:387
  46.3 4.6 %projection_grad.1 = (bf16[512,512]{1,0:T(8,128)(2,1)}, bf16[512,512]{1,0:T(8,128)(2,1)}, bf16[512,256]{1,0:T(8,128)(2,1)}, bf16[512,256]{1,0:T(8,128)(2,1)}) custom-call(bf16[4,1024,128]{2,1,0:T(8,128)(2,1)} %all-to-all-done.refs_0_, bf16[4,1024,128]{2,1,0:T(8,128)(2,1)} %collective-permute-done.5.refs_7_.refs_1_, ...), custom_call_target="tpu_custom_call" | custom-call | tf_op jit(solution)/shard_map/projection_grad/pallas_call | solution.py:48
  50.9 1.7 %collective-permute-start.11 = (bf16[512,512]{1,0:T(8,128)(2,1)}, bf16[512,512]{1,0:T(8,128)(2,1)}, u32[]{:S(2)}, u32[]{:S(2)}) collective-permute-start(bf16[512,512]{1,0:T(8,128)(2,1)} %get-tuple-element.54.refs_4_), channel_id=1, source_target_pairs={{0,4},{2,6},{4,0},{6,2},{8,12},{10,14},{12,8},{14,10},{16,20},{18,... | collective-permute-start | bytes 1572872 | tf_op jit(solution)/shard_map/ppermute | solution.py:380
  52.6 2.6 %collective-permute-start.12 = (bf16[512,256]{1,0:T(8,128)(2,1)}, bf16[512,256]{1,0:T(8,128)(2,1)}, u32[]{:S(2)}, u32[]{:S(2)}) collective-permute-start(bf16[512,256]{1,0:T(8,128)(2,1)} %get-tuple-element.61), channel_id=1, source_target_pairs={{0,16},{2,18},{4,20},{6,22},{8,24},{10,26},{12,28},{14,30},{16,0},... | collective-permute-start | bytes 786440 | tf_op jit(solution)/shard_map/ppermute | solution.py:380
  55.2 3.2 %collective-permute-done.8.refs_3_ = bf16[128,1024]{1,0:T(8,128)(2,1)} collective-permute-done((bf16[128,1024]{1,0:T(8,128)(2,1)}, bf16[128,1024]{1,0:T(8,128)(2,1)}, u32[]{:S(2)}, u32[]{:S(2)}) %collective-permute-start.8) | collective-permute-done | bytes 262176 | tf_op jit(solution)/shard_map/ppermute | solution.py:380
  58.5 2.1 %halve.4 = (bf16[64,1024]{1,0:T(8,128)(2,1)}, bf16[64,1024]{1,0:T(8,128)(2,1)}) custom-call(bf16[128,1024]{1,0:T(8,128)(2,1)} %get-tuple-element.49.refs_3_.refs_0_, bf16[128,1024]{1,0:T(8,128)(2,1)} %collective-permute-done.6.refs_1_, bf16[128,1024]{1,0:T(8,128)(2,1)} %collective-permute-done.7.refs_2_, bf16[128,1024]{1,0:T(8,128)(2,1)} %collective-permute-done.8.refs_3_, ...), custom_call_target="tpu_custom_call" | custom-call | flops 11000000512 | tf_op jit(solution)/shard_map/halve/pallas_call | solution.py:48
  60.6 3.0 %collective-permute-start.14 = (bf16[64,1024]{1,0:T(8,128)(2,1)}, bf16[64,1024]{1,0:T(8,128)(2,1)}, u32[]{:S(2)}, u32[]{:S(2)}) collective-permute-start(bf16[64,1024]{1,0:T(8,128)(2,1)} %get-tuple-element.55), channel_id=1, source_target_pairs={{0,16},{2,18},{4,20},{6,22},{8,24},{10,26},{12,28},{14,30},{16,0},... | collective-permute-start | bytes 393224 | tf_op jit(solution)/shard_map/ppermute | solution.py:380
  64.6 2.1 %add_convert_fusion.refs_2_ = bf16[512,512]{1,0:T(8,128)(2,1)} fusion(bf16[512,512]{1,0:T(8,128)(2,1)} %collective-permute-done.11, bf16[512,512]{1,0:T(8,128)(2,1)} %get-tuple-element.60), kind=kLoop, calls=%fused_computation | loop fusion | flops 1048576 | bytes 1572864 | tf_op jit(solution)/shard_map/convert_element_type | solution.py:519
  66.8 8.5 %all-to-all-start.2 = ((bf16[4,128,512]{2,1,0:T(8,128)(2,1)}), bf16[4,128,512]{2,1,0:T(8,128)(2,1)}, u32[]{:S(2)}, u32[]{:S(2)}) async-start(bf16[4,128,512]{2,1,0:T(8,128)(2,1)} %bitcast.4), calls=%async_computation.2 | async-start | bytes 1048576 | tf_op jit(solution)/shard_map/all_to_all | solution.py:387
  75.3 1.8 %halve.5 = (bf16[256,256]{1,0:T(8,128)(2,1)}, bf16[256,256]{1,0:T(8,128)(2,1)}) custom-call(bf16[512,256]{1,0:T(8,128)(2,1)} %get-tuple-element.63.refs_0_, bf16[512,256]{1,0:T(8,128)(2,1)} %collective-permute-done.12.refs_1_, bf16[512,512]{1,0:T(8,128)(2,1)} %add_convert_fusion.refs_2_), custom_call_target="tpu_custom_call" | custom-call | tf_op jit(solution)/shard_map/halve/pallas_call | solution.py:48
  78.9 2.1 %collective-permute-start.16 = (bf16[32,1024]{1,0:T(8,128)(2,1)}, bf16[32,1024]{1,0:T(8,128)(2,1)}, u32[]{:S(2)}, u32[]{:S(2)}) collective-permute-start(bf16[32,1024]{1,0:T(8,128)(2,1)} %get-tuple-element.67.refs_2_), channel_id=1, source_target_pairs={{0,4},{2,6},{4,0},{6,2},{8,12},{10,14},{12,8},{14,10},{16,20},{18,... | collective-permute-start | bytes 196616 | tf_op jit(solution)/shard_map/ppermute | solution.py:380
  80.9 2.4 %add_convert_fusion.2 = bf16[128,2048]{1,0:T(8,128)(2,1)} fusion(bf16[128,2048]{1,0:T(8,128)(2,1)} %collective-permute-done.9, bf16[128,2048]{1,0:T(8,128)(2,1)} %get-tuple-element.43.refs_6_, bf16[128,2048]{1,0:T(8,128)(2,1)} %refs_0_.6), kind=kLoop, calls=%fused_computation.2 | loop fusion | flops 1572864 | bytes 2097152 | tf_op jit(solution)/shard_map/convert_element_type | solution.py:513
  84.9 2.1 %collective-permute-start.15 = (bf16[128,256]{1,0:T(8,128)(2,1)}, bf16[128,256]{1,0:T(8,128)(2,1)}, u32[]{:S(2)}, u32[]{:S(2)}) collective-permute-start(bf16[128,256]{1,0:T(8,128)(2,1)} %get-tuple-element.69.refs_2_), channel_id=1, source_target_pairs={{0,2},{2,0},{4,6},{6,4},{8,10},{10,8},{12,14},{14,12},{16,18},{18,... | collective-permute-start | bytes 196616 | tf_op jit(solution)/shard_map/ppermute | solution.py:380
  87.0 2.4 %add_convert_fusion.1 = bf16[128,2048]{1,0:T(8,128)(2,1)} fusion(bf16[128,2048]{1,0:T(8,128)(2,1)} %collective-permute-done.10, bf16[128,2048]{1,0:T(8,128)(2,1)} %get-tuple-element.57, bf16[128,2048]{1,0:T(8,128)(2,1)} %refs_0_.7), kind=kLoop, calls=%fused_computation.1 | loop fusion | flops 1572864 | bytes 2097152 | tf_op jit(solution)/shard_map/convert_element_type | solution.py:516
  91.0 2.0 %final.1 = (f32[128,512]{1,0:T(8,128)}, f32[128,512]{1,0:T(8,128)}, f32[128,512]{1,0:T(8,128)}) custom-call(bf16[4,128,512]{2,1,0:T(8,128)(2,1)} %all-to-all-done.2.refs_0_, bf16[128,256]{1,0:T(8,128)(2,1)} %get-tuple-element.68.refs_1_, bf16[128,256]{1,0:T(8,128)(2,1)} %collective-permute-done.15.refs_2_, f32[32,2048]{1,0:T(8,128)} %out_final.1.refs_3_), custom_call_target="tpu_custom_call" | custom-call | tf_op jit(solution)/shard_map/final/pallas_call | solution.py:48
  (38 shorter events, 10.3 us)
Async XLA Ops:
  3.1 4.4 %copy-start = (bf16[128,2048]{1,0:T(8,128)(2,1)S(1)}, bf16[128,2048]{1,0:T(8,128)(2,1)}, u32[]{:S(2)}) copy-start(bf16[128,2048]{1,0:T(8,128)(2,1)} %refs_0_.6) | copy-start | bytes 1572868
  3.1 4.5 %copy-start.1 = (bf16[128,2048]{1,0:T(8,128)(2,1)S(1)}, bf16[128,2048]{1,0:T(8,128)(2,1)}, u32[]{:S(2)}) copy-start(bf16[128,2048]{1,0:T(8,128)(2,1)} %refs_0_.7) | copy-start | bytes 1572868
  3.1 18.1 %all-to-all-start = ((bf16[4,1024,128]{2,1,0:T(8,128)(2,1)}), bf16[4,1024,128]{2,1,0:T(8,128)(2,1)}, u32[]{:S(2)}, u32[]{:S(2)}) async-start(bf16[4,1024,128]{2,1,0:T(8,128)(2,1)} %get-tuple-element.40.refs_9_), calls=%async_computation | async-start | bytes 2097152 | tf_op jit(solution)/shard_map/all_to_all | solution.py:387
  7.5 2.4 %collective-permute-start = (bf16[128,2048]{1,0:T(8,128)(2,1)S(1)}, bf16[128,2048]{1,0:T(8,128)(2,1)S(1)}, u32[]{:S(2)}, u32[]{:S(2)}) collective-permute-start(bf16[128,2048]{1,0:T(8,128)(2,1)S(1)} %copy-done), channel_id=1, source_target_pairs={{0,1},{1,0},{2,3},{3,2},{4,5},{5,4},{6,7},{7,6},{8,9},{9,8},{10,11... | collective-permute-start | bytes 1572872 | tf_op jit(solution)/shard_map/ppermute | solution.py:383
  7.6 2.6 %collective-permute-start.1 = (bf16[128,2048]{1,0:T(8,128)(2,1)S(1)}, bf16[128,2048]{1,0:T(8,128)(2,1)S(1)}, u32[]{:S(2)}, u32[]{:S(2)}) collective-permute-start(bf16[128,2048]{1,0:T(8,128)(2,1)S(1)} %copy-done.1), channel_id=1, source_target_pairs={{0,1},{1,0},{2,3},{3,2},{4,5},{5,4},{6,7},{7,6},{8,9},{9,8},{10,11... | collective-permute-start | bytes 1572872 | tf_op jit(solution)/shard_map/ppermute | solution.py:383
  8.1 12.9 %collective-permute-start.2 = (bf16[128,1024]{1,0:T(8,128)(2,1)}, bf16[128,1024]{1,0:T(8,128)(2,1)}, u32[]{:S(2)}, u32[]{:S(2)}) collective-permute-start(bf16[128,1024]{1,0:T(8,128)(2,1)} %get-tuple-element.45), channel_id=1, source_target_pairs={{0,4},{2,6},{4,0},{6,2},{8,12},{10,14},{12,8},{14,10},{16,20},{18,... | collective-permute-start | bytes 786440 | tf_op jit(solution)/shard_map/ppermute | solution.py:380
  9.9 1.1 %copy-start.3 = (bf16[128,2048]{1,0:T(8,128)(2,1)}, bf16[128,2048]{1,0:T(8,128)(2,1)S(1)}, u32[]{:S(2)}) copy-start(bf16[128,2048]{1,0:T(8,128)(2,1)S(1)} %collective-permute-done.refs_2_.refs_1_) | copy-start | bytes 1572868
  10.2 0.8 copy-start.2
  21.2 25.1 %all-to-all-start.1 = ((bf16[4,768,256]{2,1,0:T(8,128)(2,1)}), bf16[4,768,256]{2,1,0:T(8,128)(2,1)}, u32[]{:S(2)}, u32[]{:S(2)}) async-start(bf16[4,768,256]{2,1,0:T(8,128)(2,1)} %get-tuple-element.53.refs_7_), calls=%async_computation.1 | async-start | bytes 3145728 | tf_op jit(solution)/shard_map/all_to_all | solution.py:387
  26.0 9.0 %collective-permute-start.5 = (bf16[4,1024,128]{2,1,0:T(8,128)(2,1)}, bf16[4,1024,128]{2,1,0:T(8,128)(2,1)}, u32[]{:S(2)}, u32[]{:S(2)}) collective-permute-start(bf16[4,1024,128]{2,1,0:T(8,128)(2,1)} %all-to-all-done.refs_0_), channel_id=1, source_target_pairs={{0,1},{1,0},{2,3},{3,2},{4,5},{5,4},{6,7},{7,6},{8,9},{9,8},{10,11... | collective-permute-start | bytes 3145736 | tf_op jit(solution)/shard_map/ppermute | solution.py:383
  26.0 8.9 %collective-permute-start.3 = (bf16[128,1024]{1,0:T(8,128)(2,1)}, bf16[128,1024]{1,0:T(8,128)(2,1)}, u32[]{:S(2)}, u32[]{:S(2)}) collective-permute-start(bf16[128,1024]{1,0:T(8,128)(2,1)} %collective-permute-done.2.refs_2_), channel_id=1, source_target_pairs={{0,1},{1,0},{2,3},{3,2},{4,5},{5,4},{6,7},{7,6},{8,9},{9,8},{10,11... | collective-permute-start | bytes 786440 | tf_op jit(solution)/shard_map/ppermute | solution.py:383
  26.6 8.5 %collective-permute-start.4 = (bf16[512,256]{1,0:T(8,128)(2,1)}, bf16[512,256]{1,0:T(8,128)(2,1)}, u32[]{:S(2)}, u32[]{:S(2)}) collective-permute-start(bf16[512,256]{1,0:T(8,128)(2,1)} %get-tuple-element.47.refs_4_), channel_id=1, source_target_pairs={{0,4},{2,6},{4,0},{6,2},{8,12},{10,14},{12,8},{14,10},{16,20},{18,... | collective-permute-start | bytes 786440 | tf_op jit(solution)/shard_map/ppermute | solution.py:380
  37.9 17.3 %collective-permute-start.6 = (bf16[128,1024]{1,0:T(8,128)(2,1)}, bf16[128,1024]{1,0:T(8,128)(2,1)}, u32[]{:S(2)}, u32[]{:S(2)}) collective-permute-start(bf16[128,1024]{1,0:T(8,128)(2,1)} %get-tuple-element.50), channel_id=1, source_target_pairs={{0,8},{2,10},{4,12},{6,14},{8,0},{10,2},{12,4},{14,6},{16,24},{18,... | collective-permute-start | bytes 786440 | tf_op jit(solution)/shard_map/ppermute | solution.py:380
  38.2 17.1 %collective-permute-start.7 = (bf16[128,1024]{1,0:T(8,128)(2,1)}, bf16[128,1024]{1,0:T(8,128)(2,1)}, u32[]{:S(2)}, u32[]{:S(2)}) collective-permute-start(bf16[128,1024]{1,0:T(8,128)(2,1)} %get-tuple-element.51), channel_id=1, source_target_pairs={{0,2},{2,0},{4,6},{6,4},{8,10},{10,8},{12,14},{14,12},{16,18},{18,... | collective-permute-start | bytes 786440 | tf_op jit(solution)/shard_map/ppermute | solution.py:380
  40.0 18.4 %collective-permute-start.8 = (bf16[128,1024]{1,0:T(8,128)(2,1)}, bf16[128,1024]{1,0:T(8,128)(2,1)}, u32[]{:S(2)}, u32[]{:S(2)}) collective-permute-start(bf16[128,1024]{1,0:T(8,128)(2,1)} %get-tuple-element.52), channel_id=1, source_target_pairs={{0,10},{2,8},{4,14},{6,12},{8,2},{10,0},{12,6},{14,4},{16,26},{18,... | collective-permute-start | bytes 786440 | tf_op jit(solution)/shard_map/ppermute | solution.py:380
  50.9 13.7 %collective-permute-start.11 = (bf16[512,512]{1,0:T(8,128)(2,1)}, bf16[512,512]{1,0:T(8,128)(2,1)}, u32[]{:S(2)}, u32[]{:S(2)}) collective-permute-start(bf16[512,512]{1,0:T(8,128)(2,1)} %get-tuple-element.54.refs_4_), channel_id=1, source_target_pairs={{0,4},{2,6},{4,0},{6,2},{8,12},{10,14},{12,8},{14,10},{16,20},{18,... | collective-permute-start | bytes 1572872 | tf_op jit(solution)/shard_map/ppermute | solution.py:380
  52.6 12.0 %collective-permute-start.12 = (bf16[512,256]{1,0:T(8,128)(2,1)}, bf16[512,256]{1,0:T(8,128)(2,1)}, u32[]{:S(2)}, u32[]{:S(2)}) collective-permute-start(bf16[512,256]{1,0:T(8,128)(2,1)} %get-tuple-element.61), channel_id=1, source_target_pairs={{0,16},{2,18},{4,20},{6,22},{8,24},{10,26},{12,28},{14,30},{16,0},... | collective-permute-start | bytes 786440 | tf_op jit(solution)/shard_map/ppermute | solution.py:380
  60.5 20.4 %collective-permute-start.9 = (bf16[128,2048]{1,0:T(8,128)(2,1)}, bf16[128,2048]{1,0:T(8,128)(2,1)}, u32[]{:S(2)}, u32[]{:S(2)}) collective-permute-start(bf16[128,2048]{1,0:T(8,128)(2,1)} %get-tuple-element.56), channel_id=1, source_target_pairs={{0,1},{1,0},{2,3},{3,2},{4,5},{5,4},{6,7},{7,6},{8,9},{9,8},{10,11... | collective-permute-start | bytes 1572872 | tf_op jit(solution)/shard_map/ppermute | solution.py:383
  60.6 16.6 %collective-permute-start.14 = (bf16[64,1024]{1,0:T(8,128)(2,1)}, bf16[64,1024]{1,0:T(8,128)(2,1)}, u32[]{:S(2)}, u32[]{:S(2)}) collective-permute-start(bf16[64,1024]{1,0:T(8,128)(2,1)} %get-tuple-element.55), channel_id=1, source_target_pairs={{0,16},{2,18},{4,20},{6,22},{8,24},{10,26},{12,28},{14,30},{16,0},... | collective-permute-start | bytes 393224 | tf_op jit(solution)/shard_map/ppermute | solution.py:380
  63.6 23.4 %collective-permute-start.10 = (bf16[128,2048]{1,0:T(8,128)(2,1)}, bf16[128,2048]{1,0:T(8,128)(2,1)}, u32[]{:S(2)}, u32[]{:S(2)}) collective-permute-start(bf16[128,2048]{1,0:T(8,128)(2,1)} %get-tuple-element.59), channel_id=1, source_target_pairs={{0,1},{1,0},{2,3},{3,2},{4,5},{5,4},{6,7},{7,6},{8,9},{9,8},{10,11... | collective-permute-start | bytes 1572872 | tf_op jit(solution)/shard_map/ppermute | solution.py:383
  66.8 24.3 %all-to-all-start.2 = ((bf16[4,128,512]{2,1,0:T(8,128)(2,1)}), bf16[4,128,512]{2,1,0:T(8,128)(2,1)}, u32[]{:S(2)}, u32[]{:S(2)}) async-start(bf16[4,128,512]{2,1,0:T(8,128)(2,1)} %bitcast.4), calls=%async_computation.2 | async-start | bytes 1048576 | tf_op jit(solution)/shard_map/all_to_all | solution.py:387
  77.1 6.2 %collective-permute-start.13 = (bf16[256,256]{1,0:T(8,128)(2,1)}, bf16[256,256]{1,0:T(8,128)(2,1)}, u32[]{:S(2)}, u32[]{:S(2)}) collective-permute-start(bf16[256,256]{1,0:T(8,128)(2,1)} %get-tuple-element.65.refs_2_), channel_id=1, source_target_pairs={{0,4},{2,6},{4,0},{6,2},{8,12},{10,14},{12,8},{14,10},{16,20},{18,... | collective-permute-start | bytes 393224 | tf_op jit(solution)/shard_map/ppermute | solution.py:380
  78.9 10.6 %collective-permute-start.16 = (bf16[32,1024]{1,0:T(8,128)(2,1)}, bf16[32,1024]{1,0:T(8,128)(2,1)}, u32[]{:S(2)}, u32[]{:S(2)}) collective-permute-start(bf16[32,1024]{1,0:T(8,128)(2,1)} %get-tuple-element.67.refs_2_), channel_id=1, source_target_pairs={{0,4},{2,6},{4,0},{6,2},{8,12},{10,14},{12,8},{14,10},{16,20},{18,... | collective-permute-start | bytes 196616 | tf_op jit(solution)/shard_map/ppermute | solution.py:380
  84.9 6.1 %collective-permute-start.15 = (bf16[128,256]{1,0:T(8,128)(2,1)}, bf16[128,256]{1,0:T(8,128)(2,1)}, u32[]{:S(2)}, u32[]{:S(2)}) collective-permute-start(bf16[128,256]{1,0:T(8,128)(2,1)} %get-tuple-element.69.refs_2_), channel_id=1, source_target_pairs={{0,2},{2,0},{4,6},{6,4},{8,10},{10,8},{12,14},{14,12},{16,18},{18,... | collective-permute-start | bytes 196616 | tf_op jit(solution)/shard_map/ppermute | solution.py:380

commit v5 on v4

--- a/solution.py
+++ b/solution.py
@@ -292,11 +292,16 @@
         part = pl.ds(pl.multiple_of(side * rows, rows), rows)
         target[...] = dot(x_all[part, :], right[:, : 2 * width]).astype(BF16)
     bit = bit_here(bits[1])
+    count = 1 << (len(bits) - 2)
+    size = rows // 2 // count
     for target, side in ((query_send, 1 - bit), (query_keep, bit)):
         for turn in range(2):
-            start = pl.multiple_of(turn * rows + side * (rows // 2), rows // 2)
-            grad = dot(x_all[pl.ds(start, rows // 2), :], right[:, 2 * width :]).astype(BF16)
-            target[turn * (rows // 2) : (turn + 1) * (rows // 2), :] = grad
+            for place in range(count):
+                start = turn * rows + side * (rows // 2) + place * size
+                part = pl.ds(pl.multiple_of(start, size), size)
+                grad = dot(x_all[part, :], right[:, 2 * width :]).astype(BF16)
+                first = (2 * place + turn) * size
+                target[first : first + size, :] = grad
 
 
 def out_grad_body(bits, grad, g_mirror, g_piece, g_piece_mirror, att_own, att_piece, *rest):
@@ -338,14 +343,41 @@
         target[...] = total.astype(BF16)
 
 
-def out_final_body(keep, other, target):
-    columns = keep.shape[1]
+def meet_body(
+    col_bit, query_keep, query_arrived, out_keep, out_arrived, own, send_out, send_col, send_both, *rest
+):
+    next_out, query, out, sems = rest
     here = bit_here(OUT_BIT)
-    for source, col in ((keep, here), (other, 1 - here)):
-        target[:, pl.ds(pl.multiple_of(col * columns, columns), columns)] = source[...].astype(F32)
-
-
-def final_body(pieces, query_keep, query_other, *targets):
+    col = bit_here(col_bit)
+    rows, out_rows, width = own.shape[0], next_out.shape[0], own.shape[1]
+    copies = fetch(
+        [
+            (query_keep, query.at[0]),
+            (query_arrived, query.at[1]),
+            (out_keep, out.at[0]),
+            (out_arrived, out.at[1]),
+        ],
+        sems,
+    )
+
+    def total(both, block, extent):
+        part = pl.ds(pl.multiple_of(block * extent, extent), extent)
+        return (both[0, part, :].astype(F32) + both[1, part, :].astype(F32)).astype(BF16)
+
+    finish(copies[:2])
+    own[...] = total(query, 2 * here + col, rows)
+    send_out[:rows, :] = total(query, 2 * (1 - here) + col, rows)
+    send_col[...] = total(query, 2 * here + 1 - col, rows)
+    send_both[...] = total(query, 2 * (1 - here) + 1 - col, rows)
+    finish(copies[2:])
+    away = total(out, 1 - here, out_rows)
+    for place in range(next_out.shape[1] // width):
+        first = rows + place * out_rows
+        send_out[first : first + out_rows, :] = away[:, place * width : (place + 1) * width]
+    next_out[...] = total(out, here, out_rows)
+
+
+def final_body(pieces, own, from_out, from_col, from_both, out_own, *targets):
     columns = targets[0].shape[1] // 2
     for col in range(2):
         total = pieces[col].astype(F32)
@@ -356,9 +388,19 @@
                 :, member * columns : (member + 1) * columns
             ]
     here = bit_here(PROJECTION_BITS[1])
-    for source, col in ((query_keep, here), (query_other, 1 - here)):
+    rows = own.shape[0]
+    for one, two, col in ((own, from_out, here), (from_col, from_both, 1 - here)):
         place = pl.ds(pl.multiple_of(col * columns, columns), columns)
-        targets[2][:, place] = source[...].astype(F32)
+        targets[2][:, place] = one[...].astype(F32) + two[:rows, :].astype(F32)
+    here = bit_here(OUT_BIT)
+    out_rows, out_columns = out_own.shape
+    place = pl.ds(pl.multiple_of(here * out_columns, out_columns), out_columns)
+    targets[3][:, place] = out_own[...].astype(F32)
+    for at in range(out_columns // columns):
+        start = (1 - here) * out_columns + at * columns
+        first = rows + at * out_rows
+        block = from_out[first : first + out_rows, :].astype(F32)
+        targets[3][:, pl.ds(pl.multiple_of(start, columns), columns)] = block
 
 
 def on_device(hidden_in, grad_out, w_query, w_key, w_value, w_out, pattern):
@@ -518,29 +560,44 @@
     pair_total = pair_keep.astype(F32) + follows(pair_arrived, (last, query_arrived)).astype(F32)
     pair_total = pair_total.astype(BF16)
     pieces = exchange(pair_total, halved_bits[1:] + [col_bit])
-    query, query_left = [query_keep, query_arrived], [halved_bits[0]] + halved_bits[2:] + [col_bit]
     last = pair_total
-    while query_left or out_left:
-        if query_left:
-            query, query_left, last = stepped(query, query_left, last)
-        if out_left:
-            out, out_left, last = stepped(out, out_left, last)
-    (grad_wout,) = call(
-        out_final_body,
-        "out_final",
-        out,
-        [jax.ShapeDtypeStruct((half // replicas, features), F32)],
+    while out_left[1:]:
+        out, out_left, last = stepped(out, out_left, last)
+    query = [query_keep, query_arrived]
+    for bit in halved_bits[2:]:
+        query, _, last = stepped(query, [bit], last)
+    rows, out_rows = features // replicas, half // replicas
+    own, send_out, send_col, send_both, out_own = call(
+        functools.partial(meet_body, col_bit),
+        "meet",
+        (*query, *out),
+        [bf16(rows, width), bf16(rows + out_rows * (part // width), width)]
+        + [bf16(rows, width)] * 2
+        + [bf16(out_rows, part)],
+        [
+            pltpu.VMEM((2, 4 * rows, width), BF16),
+            pltpu.VMEM((2, 2 * out_rows, part), BF16),
+            pltpu.SemaphoreType.DMA((4,)),
+        ],
+        far=4,
         after=(last,),
     )
+    blocks = [
+        own,
+        swap(send_out, OUT_BIT),
+        swap(send_col, col_bit),
+        swap(send_both, OUT_BIT, col_bit),
+        out_own,
+    ]
     grads = call(
         final_body,
         "final",
-        (pieces.reshape(1 << len(halved_bits), -1, 2 * width), *query),
-        [jax.ShapeDtypeStruct((features // replicas, half), F32)] * 3,
-        after=(grad_wout,),
-    )
-    grad_value, grad_key, grad_query = (grad[None] for grad in grads)
-    return (hidden_out, grad_in, grad_query, grad_key, grad_value, grad_wout[None])
+        (pieces.reshape(1 << len(halved_bits), -1, 2 * width), *blocks),
+        [jax.ShapeDtypeStruct((rows, half), F32)] * 3
+        + [jax.ShapeDtypeStruct((out_rows, features), F32)],
+    )
+    grad_value, grad_key, grad_query, grad_wout = (grad[None] for grad in grads)
+    return (hidden_out, grad_in, grad_query, grad_key, grad_value, grad_wout)
 
 
 def solution(mesh):

time: 93.7 us -> 89.9 us (0.959)
  the two profiles are of different devices: /device:TPU:8 before, /device:TPU:0 now
where the time goes in v5:
time: 89.9 us; the launch traced here: 89.4 us
  Pallas kernels  32.6 us (36%)
  starting transfers between devices  31.2 us (35%)
  waiting for transfers between devices  17.2 us (19%)
  other arithmetic  6.61 us (7%)
  local copies, waits for them, and re-layouts  0.91 us (1%)
    pallas_call x8, Pallas kernels, call(): pl.pallas_call(run, name=name, out_shape=outs, in_specs=specs, out_specs=...  32.6 us
    ppermute x11, starting transfers between devices, swap(): return lax.ppermute(x, 'dp', [(i, i ^ apart) for i in range(replicas)])  15.8 us
    all_to_all x3, starting transfers between devices, exchange(): return lax.all_to_all(x, 'dp', 0, 0, axis_index_groups=members, tiled=True)  13.8 us
    ppermute x11, waiting for transfers between devices, swap(): return lax.ppermute(x, 'dp', [(i, i ^ apart) for i in range(replicas)])  8.93 us
    all_to_all x3, waiting for transfers between devices, exchange(): return lax.all_to_all(x, 'dp', 0, 0, axis_index_groups=members, tiled=True)  8.14 us
    convert_element_type x1, other arithmetic, on_device(): hidden_out = (hidden_in.astype(F32) + contrib.astype(F32) + contrib_other...  2.39 us
    convert_element_type x1, other arithmetic, on_device(): pair_total = pair_total.astype(BF16)  2.14 us
    convert_element_type x1, other arithmetic, on_device(): grad_in = (grad_out.astype(F32) + returned.astype(F32) + returned_other.a...  2.08 us
  transfers between devices with their start and end apart: 20, of which 8 were waited for; matrix products, arithmetic and copies ran while one was open for 7% of the time, Pallas kernels for 31%

profile of v5, /device:TPU:0, one launch (start us, length us, event | category | flops | bytes accessed | tf_op | source)
XLA Modules:
  0.0 89.4 jit_solution(14716643912884518215)
XLA Ops:
  0.6 2.4 %prep.1 = (bf16[4,1024,128]{2,1,0:T(8,128)(2,1)}, bf16[128,1024]{1,0:T(8,128)(2,1)}) custom-call(bf16[128,2048]{1,0:T(8,128)(2,1)} %refs_0_.6, bf16[128,2048]{1,0:T(8,128)(2,1)} %refs_0_.7), custom_call_target="tpu_custom_call" | custom-call | tf_op jit(solution)/shard_map/prep/pallas_call | solution.py:48
  3.1 5.4 %all-to-all-start = ((bf16[4,1024,128]{2,1,0:T(8,128)(2,1)}), bf16[4,1024,128]{2,1,0:T(8,128)(2,1)}, u32[]{:S(2)}, u32[]{:S(2)}) async-start(bf16[4,1024,128]{2,1,0:T(8,128)(2,1)} %get-tuple-element.40.refs_9_), calls=%async_computation | async-start | bytes 2097152 | tf_op jit(solution)/shard_map/all_to_all | solution.py:429
  9.0 2.1 %collective-permute-start.2 = (bf16[128,1024]{1,0:T(8,128)(2,1)}, bf16[128,1024]{1,0:T(8,128)(2,1)}, u32[]{:S(2)}, u32[]{:S(2)}) collective-permute-start(bf16[128,1024]{1,0:T(8,128)(2,1)} %get-tuple-element.45), channel_id=1, source_target_pairs={{0,4},{2,6},{4,0},{6,2},{8,12},{10,14},{12,8},{14,10},{16,20},{18,... | collective-permute-start | bytes 786440 | tf_op jit(solution)/shard_map/ppermute | solution.py:422
  12.0 10.0 %attention.1 = (bf16[256,512]{1,0:T(8,128)(2,1)}, bf16[512,256]{1,0:T(8,128)(2,1)}, bf16[4,768,256]{2,1,0:T(8,128)(2,1)}) custom-call(s32[4,3]{1,0:T(4,128)} %refs_0_.5, bf16[128,2048]{1,0:T(8,128)(2,1)} %refs_0_.6, bf16[128,2048]{1,0:T(8,128)(2,1)} %copy-done.4, bf16[2048,512]{1,0:T(8,128)(2,1)} %bitcast.9, bf16[2048,512]{1,0:T(8,128)(2,1)} %bitcast.11, ...), custom_call_target="tpu_custom_call" | custom-call | flops 11000000512 | tf_op jit(solution)/shard_map/attention/pallas_call | solution.py:48
  22.7 4.3 %all-to-all-start.1 = ((bf16[4,768,256]{2,1,0:T(8,128)(2,1)}), bf16[4,768,256]{2,1,0:T(8,128)(2,1)}, u32[]{:S(2)}, u32[]{:S(2)}) async-start(bf16[4,768,256]{2,1,0:T(8,128)(2,1)} %get-tuple-element.53.refs_7_), calls=%async_computation.1 | async-start | bytes 3145728 | tf_op jit(solution)/shard_map/all_to_all | solution.py:429
  27.7 1.7 %collective-permute-start.4 = (bf16[512,256]{1,0:T(8,128)(2,1)}, bf16[512,256]{1,0:T(8,128)(2,1)}, u32[]{:S(2)}, u32[]{:S(2)}) collective-permute-start(bf16[512,256]{1,0:T(8,128)(2,1)} %get-tuple-element.47.refs_4_), channel_id=1, source_target_pairs={{0,4},{2,6},{4,0},{6,2},{8,12},{10,14},{12,8},{14,10},{16,20},{18,... | collective-permute-start | bytes 786440 | tf_op jit(solution)/shard_map/ppermute | solution.py:422
  29.3 6.7 %returned.1 = (bf16[128,2048]{1,0:T(8,128)(2,1)}, bf16[128,2048]{1,0:T(8,128)(2,1)}, bf16[128,2048]{1,0:T(8,128)(2,1)}, bf16[128,2048]{1,0:T(8,128)(2,1)}) custom-call(bf16[128,2048]{1,0:T(8,128)(2,1)} %refs_0_.6, bf16[128,2048]{1,0:T(8,128)(2,1)} %copy-done.4, bf16[256,512]{1,0:T(8,128)(2,1)} %get-tuple-element.41.refs_2_, bf16[512,2048]{1,0:T(8,128)(2,1)} %bitcast.16, ...), custom_call_target="tpu_custom_call" | custom-call | tf_op jit(solution)/shard_map/returned/pallas_call | solution.py:48
  36.3 2.8 %out_grad.1 = (bf16[128,1024]{1,0:T(8,128)(2,1)}, bf16[128,1024]{1,0:T(8,128)(2,1)}, bf16[128,1024]{1,0:T(8,128)(2,1)}, bf16[128,1024]{1,0:T(8,128)(2,1)}) custom-call(bf16[128,2048]{1,0:T(8,128)(2,1)} %refs_0_.7, bf16[128,2048]{1,0:T(8,128)(2,1)} %copy-done.3, bf16[128,1024]{1,0:T(8,128)(2,1)} %collective-permute-done.2.refs_2_, ...), custom_call_target="tpu_custom_call" | custom-call | tf_op jit(solution)/shard_map/out_grad/pallas_call | solution.py:48
  39.1 1.9 %collective-permute-start.6 = (bf16[128,1024]{1,0:T(8,128)(2,1)}, bf16[128,1024]{1,0:T(8,128)(2,1)}, u32[]{:S(2)}, u32[]{:S(2)}) collective-permute-start(bf16[128,1024]{1,0:T(8,128)(2,1)} %get-tuple-element.50), channel_id=1, source_target_pairs={{0,8},{2,10},{4,12},{6,14},{8,0},{10,2},{12,4},{14,6},{16,24},{18,... | collective-permute-start | bytes 786440 | tf_op jit(solution)/shard_map/ppermute | solution.py:422
  42.7 5.1 %all-to-all-done.1.refs_2_ = bf16[4,768,256]{2,1,0:T(8,128)(2,1)} async-done(((bf16[4,768,256]{2,1,0:T(8,128)(2,1)}), bf16[4,768,256]{2,1,0:T(8,128)(2,1)}, u32[]{:S(2)}, u32[]{:S(2)}) %all-to-all-start.1) | async-done | bytes 1572896 | tf_op jit(solution)/shard_map/all_to_all | solution.py:429
  47.8 4.6 %projection_grad.1 = (bf16[512,512]{1,0:T(8,128)(2,1)}, bf16[512,512]{1,0:T(8,128)(2,1)}, bf16[512,256]{1,0:T(8,128)(2,1)}, bf16[512,256]{1,0:T(8,128)(2,1)}) custom-call(bf16[4,1024,128]{2,1,0:T(8,128)(2,1)} %all-to-all-done.refs_0_, bf16[4,1024,128]{2,1,0:T(8,128)(2,1)} %collective-permute-done.5.refs_7_.refs_1_, ...), custom_call_target="tpu_custom_call" | custom-call | tf_op jit(solution)/shard_map/projection_grad/pallas_call | solution.py:48
  52.4 1.7 %collective-permute-start.11 = (bf16[512,512]{1,0:T(8,128)(2,1)}, bf16[512,512]{1,0:T(8,128)(2,1)}, u32[]{:S(2)}, u32[]{:S(2)}) collective-permute-start(bf16[512,512]{1,0:T(8,128)(2,1)} %get-tuple-element.54.refs_4_), channel_id=1, source_target_pairs={{0,4},{2,6},{4,0},{6,2},{8,12},{10,14},{12,8},{14,10},{16,20},{18,... | collective-permute-start | bytes 1572872 | tf_op jit(solution)/shard_map/ppermute | solution.py:422
  54.2 2.6 %collective-permute-start.12 = (bf16[512,256]{1,0:T(8,128)(2,1)}, bf16[512,256]{1,0:T(8,128)(2,1)}, u32[]{:S(2)}, u32[]{:S(2)}) collective-permute-start(bf16[512,256]{1,0:T(8,128)(2,1)} %get-tuple-element.61), channel_id=1, source_target_pairs={{0,16},{2,18},{4,20},{6,22},{8,24},{10,26},{12,28},{14,30},{16,0},... | collective-permute-start | bytes 786440 | tf_op jit(solution)/shard_map/ppermute | solution.py:422
  56.8 6.1 %collective-permute-done.8.refs_3_ = bf16[128,1024]{1,0:T(8,128)(2,1)} collective-permute-done((bf16[128,1024]{1,0:T(8,128)(2,1)}, bf16[128,1024]{1,0:T(8,128)(2,1)}, u32[]{:S(2)}, u32[]{:S(2)}) %collective-permute-start.8) | collective-permute-done | bytes 262176 | tf_op jit(solution)/shard_map/ppermute | solution.py:422
  62.9 2.1 %halve.1 = (bf16[64,1024]{1,0:T(8,128)(2,1)}, bf16[64,1024]{1,0:T(8,128)(2,1)}) custom-call(bf16[128,1024]{1,0:T(8,128)(2,1)} %get-tuple-element.49.refs_3_.refs_0_, bf16[128,1024]{1,0:T(8,128)(2,1)} %collective-permute-done.6.refs_1_, bf16[128,1024]{1,0:T(8,128)(2,1)} %collective-permute-done.7.refs_2_, bf16[128,1024]{1,0:T(8,128)(2,1)} %collective-permute-done.8.refs_3_, ...), custom_call_target="tpu_custom_call" | custom-call | flops 11000000512 | tf_op jit(solution)/shard_map/halve/pallas_call | solution.py:48
  65.5 1.8 %collective-permute-done.12.refs_1_ = bf16[512,256]{1,0:T(8,128)(2,1)} collective-permute-done((bf16[512,256]{1,0:T(8,128)(2,1)}, bf16[512,256]{1,0:T(8,128)(2,1)}, u32[]{:S(2)}, u32[]{:S(2)}) %collective-permute-start.12) | collective-permute-done | bytes 262176 | tf_op jit(solution)/shard_map/ppermute | solution.py:422
  67.4 2.1 %add_convert_fusion.refs_4_ = bf16[512,512]{1,0:T(8,128)(2,1)} fusion(bf16[512,512]{1,0:T(8,128)(2,1)} %collective-permute-done.11, bf16[512,512]{1,0:T(8,128)(2,1)} %get-tuple-element.60), kind=kLoop, calls=%fused_computation | loop fusion | flops 1048576 | bytes 1572864 | tf_op jit(solution)/shard_map/convert_element_type | solution.py:561
  69.5 4.1 %all-to-all-start.2 = ((bf16[4,128,512]{2,1,0:T(8,128)(2,1)}), bf16[4,128,512]{2,1,0:T(8,128)(2,1)}, u32[]{:S(2)}, u32[]{:S(2)}) async-start(bf16[4,128,512]{2,1,0:T(8,128)(2,1)} %bitcast.4), calls=%async_computation.2 | async-start | bytes 1048576 | tf_op jit(solution)/shard_map/all_to_all | solution.py:429
  73.7 1.9 %meet.1 = (bf16[128,256]{1,0:T(8,128)(2,1)}, bf16[256,256]{1,0:T(8,128)(2,1)}, bf16[128,256]{1,0:T(8,128)(2,1)}, bf16[128,256]{1,0:T(8,128)(2,1)}, bf16[32,1024]{1,0:T(8,128)(2,1)}) custom-call(bf16[512,256]{1,0:T(8,128)(2,1)} %get-tuple-element.63.refs_0_, bf16[512,256]{1,0:T(8,128)(2,1)} %collective-permute-done.12.refs_1_, ...), custom_call_target="tpu_custom_call" | custom-call | tf_op jit(solution)/shard_map/meet/pallas_call | solution.py:48
  75.6 2.6 %collective-permute-start.14 = (bf16[256,256]{1,0:T(8,128)(2,1)}, bf16[256,256]{1,0:T(8,128)(2,1)}, u32[]{:S(2)}, u32[]{:S(2)}) collective-permute-start(bf16[256,256]{1,0:T(8,128)(2,1)} %get-tuple-element.66), channel_id=1, source_target_pairs={{0,4},{2,6},{4,0},{6,2},{8,12},{10,14},{12,8},{14,10},{16,20},{18,... | collective-permute-start | bytes 393224 | tf_op jit(solution)/shard_map/ppermute | solution.py:422
  79.7 2.4 %add_convert_fusion.2 = bf16[128,2048]{1,0:T(8,128)(2,1)} fusion(bf16[128,2048]{1,0:T(8,128)(2,1)} %collective-permute-done.9, bf16[128,2048]{1,0:T(8,128)(2,1)} %get-tuple-element.43.refs_6_, bf16[128,2048]{1,0:T(8,128)(2,1)} %refs_0_.6), kind=kLoop, calls=%fused_computation.2 | loop fusion | flops 1572864 | bytes 2097152 | tf_op jit(solution)/shard_map/convert_element_type | solution.py:555
  82.1 2.1 %add_convert_fusion.1 = bf16[128,2048]{1,0:T(8,128)(2,1)} fusion(bf16[128,2048]{1,0:T(8,128)(2,1)} %collective-permute-done.10, bf16[128,2048]{1,0:T(8,128)(2,1)S(1)} %copy-done.5, bf16[128,2048]{1,0:T(8,128)(2,1)S(1)} %copy-done.2), kind=kLoop, calls=%fused_computation.1 | loop fusion | flops 1572864 | bytes 2097152 | tf_op jit(solution)/shard_map/convert_element_type | solution.py:558
  84.9 2.3 %all-to-all-done.2.refs_0_ = bf16[4,128,512]{2,1,0:T(8,128)(2,1)} async-done(((bf16[4,128,512]{2,1,0:T(8,128)(2,1)}), bf16[4,128,512]{2,1,0:T(8,128)(2,1)}, u32[]{:S(2)}, u32[]{:S(2)}) %all-to-all-start.2) | async-done | bytes 524320 | tf_op jit(solution)/shard_map/all_to_all | solution.py:429
  87.2 2.1 %final.1 = (f32[128,512]{1,0:T(8,128)}, f32[128,512]{1,0:T(8,128)}, f32[128,512]{1,0:T(8,128)}, f32[32,2048]{1,0:T(8,128)}) custom-call(bf16[4,128,512]{2,1,0:T(8,128)(2,1)} %all-to-all-done.2.refs_0_, bf16[128,256]{1,0:T(8,128)(2,1)} %get-tuple-element.65.refs_1_, bf16[256,256]{1,0:T(8,128)(2,1)} %collective-permute-done.14.refs_2_, ...), custom_call_target="tpu_custom_call" | custom-call | tf_op jit(solution)/shard_map/final/pallas_call | solution.py:48
  (39 shorter events, 7.5 us)
Async XLA Ops:
  3.1 5.4 %copy-start = (bf16[128,2048]{1,0:T(8,128)(2,1)S(1)}, bf16[128,2048]{1,0:T(8,128)(2,1)}, u32[]{:S(2)}) copy-start(bf16[128,2048]{1,0:T(8,128)(2,1)} %refs_0_.6) | copy-start | bytes 1572868
  3.1 5.4 %copy-start.1 = (bf16[128,2048]{1,0:T(8,128)(2,1)S(1)}, bf16[128,2048]{1,0:T(8,128)(2,1)}, u32[]{:S(2)}) copy-start(bf16[128,2048]{1,0:T(8,128)(2,1)} %refs_0_.7) | copy-start | bytes 1572868
  3.1 19.7 %all-to-all-start = ((bf16[4,1024,128]{2,1,0:T(8,128)(2,1)}), bf16[4,1024,128]{2,1,0:T(8,128)(2,1)}, u32[]{:S(2)}, u32[]{:S(2)}) async-start(bf16[4,1024,128]{2,1,0:T(8,128)(2,1)} %get-tuple-element.40.refs_9_), calls=%async_computation | async-start | bytes 2097152 | tf_op jit(solution)/shard_map/all_to_all | solution.py:429
  8.5 2.6 %collective-permute-start = (bf16[128,2048]{1,0:T(8,128)(2,1)S(1)}, bf16[128,2048]{1,0:T(8,128)(2,1)S(1)}, u32[]{:S(2)}, u32[]{:S(2)}) collective-permute-start(bf16[128,2048]{1,0:T(8,128)(2,1)S(1)} %copy-done), channel_id=1, source_target_pairs={{0,1},{1,0},{2,3},{3,2},{4,5},{5,4},{6,7},{7,6},{8,9},{9,8},{10,11... | collective-permute-start | bytes 1572872 | tf_op jit(solution)/shard_map/ppermute | solution.py:425
  8.5 2.6 %collective-permute-start.1 = (bf16[128,2048]{1,0:T(8,128)(2,1)S(1)}, bf16[128,2048]{1,0:T(8,128)(2,1)S(1)}, u32[]{:S(2)}, u32[]{:S(2)}) collective-permute-start(bf16[128,2048]{1,0:T(8,128)(2,1)S(1)} %copy-done.1), channel_id=1, source_target_pairs={{0,1},{1,0},{2,3},{3,2},{4,5},{5,4},{6,7},{7,6},{8,9},{9,8},{10,11... | collective-permute-start | bytes 1572872 | tf_op jit(solution)/shard_map/ppermute | solution.py:425
  9.0 13.0 %collective-permute-start.2 = (bf16[128,1024]{1,0:T(8,128)(2,1)}, bf16[128,1024]{1,0:T(8,128)(2,1)}, u32[]{:S(2)}, u32[]{:S(2)}) collective-permute-start(bf16[128,1024]{1,0:T(8,128)(2,1)} %get-tuple-element.45), channel_id=1, source_target_pairs={{0,4},{2,6},{4,0},{6,2},{8,12},{10,14},{12,8},{14,10},{16,20},{18,... | collective-permute-start | bytes 786440 | tf_op jit(solution)/shard_map/ppermute | solution.py:422
  22.7 25.1 %all-to-all-start.1 = ((bf16[4,768,256]{2,1,0:T(8,128)(2,1)}), bf16[4,768,256]{2,1,0:T(8,128)(2,1)}, u32[]{:S(2)}, u32[]{:S(2)}) async-start(bf16[4,768,256]{2,1,0:T(8,128)(2,1)} %get-tuple-element.53.refs_7_), calls=%async_computation.1 | async-start | bytes 3145728 | tf_op jit(solution)/shard_map/all_to_all | solution.py:429
  27.1 9.2 %collective-permute-start.5 = (bf16[4,1024,128]{2,1,0:T(8,128)(2,1)}, bf16[4,1024,128]{2,1,0:T(8,128)(2,1)}, u32[]{:S(2)}, u32[]{:S(2)}) collective-permute-start(bf16[4,1024,128]{2,1,0:T(8,128)(2,1)} %all-to-all-done.refs_0_), channel_id=1, source_target_pairs={{0,1},{1,0},{2,3},{3,2},{4,5},{5,4},{6,7},{7,6},{8,9},{9,8},{10,11... | collective-permute-start | bytes 3145736 | tf_op jit(solution)/shard_map/ppermute | solution.py:425
  27.2 8.8 %collective-permute-start.3 = (bf16[128,1024]{1,0:T(8,128)(2,1)}, bf16[128,1024]{1,0:T(8,128)(2,1)}, u32[]{:S(2)}, u32[]{:S(2)}) collective-permute-start(bf16[128,1024]{1,0:T(8,128)(2,1)} %collective-permute-done.2.refs_2_), channel_id=1, source_target_pairs={{0,1},{1,0},{2,3},{3,2},{4,5},{5,4},{6,7},{7,6},{8,9},{9,8},{10,11... | collective-permute-start | bytes 786440 | tf_op jit(solution)/shard_map/ppermute | solution.py:425
  27.7 8.6 %collective-permute-start.4 = (bf16[512,256]{1,0:T(8,128)(2,1)}, bf16[512,256]{1,0:T(8,128)(2,1)}, u32[]{:S(2)}, u32[]{:S(2)}) collective-permute-start(bf16[512,256]{1,0:T(8,128)(2,1)} %get-tuple-element.47.refs_4_), channel_id=1, source_target_pairs={{0,4},{2,6},{4,0},{6,2},{8,12},{10,14},{12,8},{14,10},{16,20},{18,... | collective-permute-start | bytes 786440 | tf_op jit(solution)/shard_map/ppermute | solution.py:422
  39.1 17.6 %collective-permute-start.6 = (bf16[128,1024]{1,0:T(8,128)(2,1)}, bf16[128,1024]{1,0:T(8,128)(2,1)}, u32[]{:S(2)}, u32[]{:S(2)}) collective-permute-start(bf16[128,1024]{1,0:T(8,128)(2,1)} %get-tuple-element.50), channel_id=1, source_target_pairs={{0,8},{2,10},{4,12},{6,14},{8,0},{10,2},{12,4},{14,6},{16,24},{18,... | collective-permute-start | bytes 786440 | tf_op jit(solution)/shard_map/ppermute | solution.py:422
  41.0 15.7 %collective-permute-start.7 = (bf16[128,1024]{1,0:T(8,128)(2,1)}, bf16[128,1024]{1,0:T(8,128)(2,1)}, u32[]{:S(2)}, u32[]{:S(2)}) collective-permute-start(bf16[128,1024]{1,0:T(8,128)(2,1)} %get-tuple-element.51), channel_id=1, source_target_pairs={{0,2},{2,0},{4,6},{6,4},{8,10},{10,8},{12,14},{14,12},{16,18},{18,... | collective-permute-start | bytes 786440 | tf_op jit(solution)/shard_map/ppermute | solution.py:422
  42.5 20.4 %collective-permute-start.8 = (bf16[128,1024]{1,0:T(8,128)(2,1)}, bf16[128,1024]{1,0:T(8,128)(2,1)}, u32[]{:S(2)}, u32[]{:S(2)}) collective-permute-start(bf16[128,1024]{1,0:T(8,128)(2,1)} %get-tuple-element.52), channel_id=1, source_target_pairs={{0,10},{2,8},{4,14},{6,12},{8,2},{10,0},{12,6},{14,4},{16,26},{18,... | collective-permute-start | bytes 786440 | tf_op jit(solution)/shard_map/ppermute | solution.py:422
  52.4 14.9 %collective-permute-start.11 = (bf16[512,512]{1,0:T(8,128)(2,1)}, bf16[512,512]{1,0:T(8,128)(2,1)}, u32[]{:S(2)}, u32[]{:S(2)}) collective-permute-start(bf16[512,512]{1,0:T(8,128)(2,1)} %get-tuple-element.54.refs_4_), channel_id=1, source_target_pairs={{0,4},{2,6},{4,0},{6,2},{8,12},{10,14},{12,8},{14,10},{16,20},{18,... | collective-permute-start | bytes 1572872 | tf_op jit(solution)/shard_map/ppermute | solution.py:422
  54.2 13.2 %collective-permute-start.12 = (bf16[512,256]{1,0:T(8,128)(2,1)}, bf16[512,256]{1,0:T(8,128)(2,1)}, u32[]{:S(2)}, u32[]{:S(2)}) collective-permute-start(bf16[512,256]{1,0:T(8,128)(2,1)} %get-tuple-element.61), channel_id=1, source_target_pairs={{0,16},{2,18},{4,20},{6,22},{8,24},{10,26},{12,28},{14,30},{16,0},... | collective-permute-start | bytes 786440 | tf_op jit(solution)/shard_map/ppermute | solution.py:422
  65.0 14.8 %collective-permute-start.9 = (bf16[128,2048]{1,0:T(8,128)(2,1)}, bf16[128,2048]{1,0:T(8,128)(2,1)}, u32[]{:S(2)}, u32[]{:S(2)}) collective-permute-start(bf16[128,2048]{1,0:T(8,128)(2,1)} %get-tuple-element.56), channel_id=1, source_target_pairs={{0,1},{1,0},{2,3},{3,2},{4,5},{5,4},{6,7},{7,6},{8,9},{9,8},{10,11... | collective-permute-start | bytes 1572872 | tf_op jit(solution)/shard_map/ppermute | solution.py:425
  65.0 8.6 %collective-permute-start.13 = (bf16[64,1024]{1,0:T(8,128)(2,1)}, bf16[64,1024]{1,0:T(8,128)(2,1)}, u32[]{:S(2)}, u32[]{:S(2)}) collective-permute-start(bf16[64,1024]{1,0:T(8,128)(2,1)} %get-tuple-element.55), channel_id=1, source_target_pairs={{0,16},{2,18},{4,20},{6,22},{8,24},{10,26},{12,28},{14,30},{16,0},... | collective-permute-start | bytes 393224 | tf_op jit(solution)/shard_map/ppermute | solution.py:422
  65.1 17.0 %collective-permute-start.10 = (bf16[128,2048]{1,0:T(8,128)(2,1)}, bf16[128,2048]{1,0:T(8,128)(2,1)}, u32[]{:S(2)}, u32[]{:S(2)}) collective-permute-start(bf16[128,2048]{1,0:T(8,128)(2,1)} %get-tuple-element.59), channel_id=1, source_target_pairs={{0,1},{1,0},{2,3},{3,2},{4,5},{5,4},{6,7},{7,6},{8,9},{9,8},{10,11... | collective-permute-start | bytes 1572872 | tf_op jit(solution)/shard_map/ppermute | solution.py:425
  69.5 17.7 %all-to-all-start.2 = ((bf16[4,128,512]{2,1,0:T(8,128)(2,1)}), bf16[4,128,512]{2,1,0:T(8,128)(2,1)}, u32[]{:S(2)}, u32[]{:S(2)}) async-start(bf16[4,128,512]{2,1,0:T(8,128)(2,1)} %bitcast.4), calls=%async_computation.2 | async-start | bytes 1048576 | tf_op jit(solution)/shard_map/all_to_all | solution.py:429
  75.6 6.6 %copy-start.2 = (bf16[128,2048]{1,0:T(8,128)(2,1)S(1)}, bf16[128,2048]{1,0:T(8,128)(2,1)}, u32[]{:S(2)}) copy-start(bf16[128,2048]{1,0:T(8,128)(2,1)} %refs_0_.7) | copy-start | bytes 1572868
  75.6 6.6 %copy-start.5 = (bf16[128,2048]{1,0:T(8,128)(2,1)S(1)}, bf16[128,2048]{1,0:T(8,128)(2,1)}, u32[]{:S(2)}) copy-start(bf16[128,2048]{1,0:T(8,128)(2,1)} %get-tuple-element.57) | copy-start | bytes 1572868
  75.6 9.3 %collective-permute-start.14 = (bf16[256,256]{1,0:T(8,128)(2,1)}, bf16[256,256]{1,0:T(8,128)(2,1)}, u32[]{:S(2)}, u32[]{:S(2)}) collective-permute-start(bf16[256,256]{1,0:T(8,128)(2,1)} %get-tuple-element.66), channel_id=1, source_target_pairs={{0,4},{2,6},{4,0},{6,2},{8,12},{10,14},{12,8},{14,10},{16,20},{18,... | collective-permute-start | bytes 393224 | tf_op jit(solution)/shard_map/ppermute | solution.py:422
  78.2 6.0 %collective-permute-start.15 = (bf16[128,256]{1,0:T(8,128)(2,1)}, bf16[128,256]{1,0:T(8,128)(2,1)}, u32[]{:S(2)}, u32[]{:S(2)}) collective-permute-start(bf16[128,256]{1,0:T(8,128)(2,1)} %get-tuple-element.67), channel_id=1, source_target_pairs={{0,2},{2,0},{4,6},{6,4},{8,10},{10,8},{12,14},{14,12},{16,18},{18,... | collective-permute-start | bytes 196616 | tf_op jit(solution)/shard_map/ppermute | solution.py:422
  79.5 5.5 %collective-permute-start.16 = (bf16[128,256]{1,0:T(8,128)(2,1)}, bf16[128,256]{1,0:T(8,128)(2,1)}, u32[]{:S(2)}, u32[]{:S(2)}) collective-permute-start(bf16[128,256]{1,0:T(8,128)(2,1)} %get-tuple-element.68), channel_id=1, source_target_pairs={{0,6},{2,4},{4,2},{6,0},{8,14},{10,12},{12,10},{14,8},{16,22},{18,... | collective-permute-start | bytes 196616 | tf_op jit(solution)/shard_map/ppermute | solution.py:422
  (2 other events, 1.8 us)

commit v6 on v5

--- a/solution.py
+++ b/solution.py
@@ -13,6 +13,8 @@
 PAIR = 2 * HDIM
 VMEM_BYTES = 64 * 1024 * 1024
 
+LATE_VMEM_BYTES = 16 * 1024 * 1024
+
 LONG_WORK = 11 * 10**9
 
 F32 = jnp.float32
@@ -35,7 +37,19 @@
     return lax.dot_general(left, right, TN, preferred_element_type=F32)
 
 
-def call(body, name, inputs, outs, scratch=(), work=0, scalars=0, far=0, after=()):
+def call(
+    body,
+    name,
+    inputs,
+    outs,
+    scratch=(),
+    work=0,
+    scalars=0,
+    far=0,
+    far_outs=0,
+    after=(),
+    vmem=VMEM_BYTES,
+):
     near = len(inputs) - scalars - far
     count = len(inputs)
     specs = [pl.BlockSpec(memory_space=pltpu.SMEM)] * scalars
@@ -50,16 +64,17 @@
         name=name,
         out_shape=outs,
         in_specs=specs,
-        out_specs=[pl.BlockSpec(memory_space=pltpu.VMEM)] * len(outs),
+        out_specs=[pl.BlockSpec(memory_space=pltpu.VMEM)] * (len(outs) - far_outs)
+        + [pl.BlockSpec(memory_space=pltpu.HBM)] * far_outs,
         scratch_shapes=list(scratch),
-        compiler_params=pltpu.CompilerParams(vmem_limit_bytes=VMEM_BYTES),
+        compiler_params=pltpu.CompilerParams(vmem_limit_bytes=vmem),
         cost_estimate=pl.CostEstimate(flops=work, bytes_accessed=0, transcendentals=0),
     )(*inputs, *after)
 
 
-def fetch(pairs, sems):
+def fetch(pairs, sems, first=0):
     copies = [
-        pltpu.make_async_copy(source, target, sems.at[place])
+        pltpu.make_async_copy(source, target, sems.at[first + place])
         for place, (source, target) in enumerate(pairs)
     ]
     for copy in copies:
@@ -93,16 +108,21 @@
     return (lax.axis_index("dp") >> bit) & 1
 
 
-def prep_body(chunks, hidden, grad, x_blocks, g_send, x, turned, sems):
+def prep_body(chunks, hidden, grad, x_blocks, g_send, x, g, turned, sides, sems):
     columns = g_send.shape[1]
     away = pl.ds(pl.multiple_of((1 - bit_here(OUT_BIT)) * columns, columns), columns)
-    x_copy, g_copy = fetch([(hidden, x), (grad.at[:, away], g_send)], sems)
+    x_copy, g_copy = fetch([(hidden, x), (grad.at[:, away], g)], sems)
     x_copy.wait()
     turned[...] = x[...].astype(F32).T.astype(BF16)
-    for member in range(4):
-        own = [chunk | (member % 2) << PROJECTION_BITS[0] for chunk in chunks]
-        copy_chunks(turned, x_blocks.at[member], own, turned.shape[0] // (2 * len(own)))
+    sends = []
+    for row in range(2):
+        own = [chunk | row << PROJECTION_BITS[0] for chunk in chunks]
+        copy_chunks(turned, sides.at[row], own, turned.shape[0] // (2 * len(own)))
+        pairs = [(sides.at[row], x_blocks.at[2 * col + row]) for col in range(2)]
+        sends += fetch(pairs, sems, 2 + 2 * row)
     g_copy.wait()
+    sends += fetch([(g, g_send)], sems, 6)
+    finish(sends)
 
 
 def seen_mask(pattern, seq_len, blocks, slots):
@@ -273,7 +293,7 @@
 
 
 def projection_grad_body(bits, x_pieces, x_mirrors, g_pieces, *rest):
-    pair_send, pair_keep, query_send, query_keep, x_all, right, sems = rest
+    pair_send, pair_keep, query_send, query_keep, x_all, right, pair_sums, query_sums, sems = rest
     seq_len = x_pieces.shape[2]
     tokens = 2 * seq_len
     width = g_pieces.shape[2]
@@ -285,23 +305,32 @@
         for member in range(3):
             target = right.at[pl.ds(place * tokens, tokens), pl.ds(member * width, width)]
             pairs.append((g_pieces.at[place, pl.ds(member * tokens, tokens)], target))
-    finish(fetch(pairs, sems))
+    copies = fetch(pairs, sems)
     rows = x_all.shape[0] // 2
-    bit = bit_here(bits[0])
-    for target, side in ((pair_send, 1 - bit), (pair_keep, bit)):
-        part = pl.ds(pl.multiple_of(side * rows, rows), rows)
-        target[...] = dot(x_all[part, :], right[:, : 2 * width]).astype(BF16)
-    bit = bit_here(bits[1])
+    pair_bit, query_bit = bit_here(bits[0]), bit_here(bits[1])
     count = 1 << (len(bits) - 2)
     size = rows // 2 // count
-    for target, side in ((query_send, 1 - bit), (query_keep, bit)):
-        for turn in range(2):
-            for place in range(count):
-                start = turn * rows + side * (rows // 2) + place * size
-                part = pl.ds(pl.multiple_of(start, size), size)
-                grad = dot(x_all[part, :], right[:, 2 * width :]).astype(BF16)
-                first = (2 * place + turn) * size
-                target[first : first + size, :] = grad
+    middle = 2 * tokens
+    for half_at, depth in enumerate((slice(0, middle), slice(middle, 2 * middle))):
+        finish(copies[10 * half_at : 10 * (half_at + 1)])
+        for at, (target, side) in enumerate(((pair_send, 1 - pair_bit), (pair_keep, pair_bit))):
+            part = pl.ds(pl.multiple_of(side * rows, rows), rows)
+            grad = dot(x_all[part, depth], right[depth, : 2 * width])
+            if half_at == 0:
+                pair_sums[at] = grad
+            else:
+                target[...] = (pair_sums[at] + grad).astype(BF16)
+        for at, (target, side) in enumerate(((query_send, 1 - query_bit), (query_keep, query_bit))):
+            for turn in range(2):
+                for place in range(count):
+                    start = turn * rows + side * (rows // 2) + place * size
+                    part = pl.ds(pl.multiple_of(start, size), size)
+                    grad = dot(x_all[part, depth], right[depth, 2 * width :])
+                    here = slice((2 * place + turn) * size, (2 * place + turn + 1) * size)
+                    if half_at == 0:
+                        query_sums[at, here, :] = grad
+                    else:
+                        target[here, :] = (query_sums[at, here, :] + grad).astype(BF16)
 
 
 def out_grad_body(bits, grad, g_mirror, g_piece, g_piece_mirror, att_own, att_piece, *rest):
@@ -443,10 +472,13 @@
         [bf16(4, part, seq_len), bf16(seq_len, part)],
         [
             pltpu.VMEM((seq_len, features), BF16),
+            pltpu.VMEM((seq_len, part), BF16),
             pltpu.VMEM((features, seq_len), BF16),
-            pltpu.SemaphoreType.DMA((2,)),
+            pltpu.VMEM((2, part, seq_len), BF16),
+            pltpu.SemaphoreType.DMA((7,)),
         ],
         far=2,
+        far_outs=2,
     )
     x_pieces = exchange(x_blocks, [col_bit, row_bit])
     g_piece = swap(g_send, OUT_BIT)
@@ -520,10 +552,13 @@
         [
             pltpu.VMEM((part, 4 * tokens), BF16),
             pltpu.VMEM((4 * tokens, 3 * width), BF16),
+            pltpu.VMEM((2, part // 2, 2 * width), F32),
+            pltpu.VMEM((2, part // 2, width), F32),
             pltpu.SemaphoreType.DMA((20,)),
         ],
         far=3,
         after=(out_keep,),
+        vmem=LATE_VMEM_BYTES,
     )
     pair_arrived = swap(pair_send, halved_bits[0])
     query_arrived = swap(query_send, halved_bits[1])
@@ -538,6 +573,7 @@
             [pltpu.VMEM((2, count, *shape), BF16), pltpu.SemaphoreType.DMA((2 * count,))],
             work=work,
             far=count,
+            vmem=LATE_VMEM_BYTES,
             after=(after,),
         )
 
@@ -581,6 +617,7 @@
         ],
         far=4,
         after=(last,),
+        vmem=LATE_VMEM_BYTES,
     )
     blocks = [
         own,
@@ -595,6 +632,7 @@
         (pieces.reshape(1 << len(halved_bits), -1, 2 * width), *blocks),
         [jax.ShapeDtypeStruct((rows, half), F32)] * 3
         + [jax.ShapeDtypeStruct((out_rows, features), F32)],
+        vmem=LATE_VMEM_BYTES,
     )
     grad_value, grad_key, grad_query, grad_wout = (grad[None] for grad in grads)
     return (hidden_out, grad_in, grad_query, grad_key, grad_value, grad_wout)

time: 89.9 us -> 87.3 us (0.971)
  Pallas kernels: 32.6 us -> 28.4 us
  waiting for transfers between devices: 17.2 us -> 19.2 us
  other arithmetic: 6.61 us -> 5.1 us
  local copies, waits for them, and re-layouts: 0.91 us -> 1.88 us
    pallas_call x8, Pallas kernels: 32.6 us -> 28.4 us  [call(): pl.pallas_call(run, name=name, out_shape=outs, in_specs=specs, out_specs=...]
    ppermute x11, waiting for transfers between devices: 8.93 us -> 10.6 us  [swap(): return lax.ppermute(x, 'dp', [(i, i ^ apart) for i in range(replicas)])]
    convert_element_type x1, other arithmetic: 2.14 us -> 0.94 us  [on_device(): pair_total = pair_total.astype(BF16)]
    unnamed x12 -> x20, local copies, waits for them, and re-layouts: 0.91 us -> 1.88 us
  transfers between devices with their start and end apart: 20 -> 20, of which waited for: 8 -> 10; matrix products, arithmetic and copies ran while one was open for 7% -> 6% of each run, Pallas kernels for 31% -> 29%
where the time goes in v6:
time: 87.3 us; the launch traced here: 86.3 us
  starting transfers between devices  30.9 us (35%)
  Pallas kernels  28.4 us (33%)
  waiting for transfers between devices  19.2 us (22%)
  other arithmetic  5.1 us (6%)
  local copies, waits for them, and re-layouts  1.88 us (2%)
    pallas_call x8, Pallas kernels, call(): pl.pallas_call(run, name=name, out_shape=outs, in_specs=specs, out_specs=...  28.4 us
    ppermute x11, starting transfers between devices, swap(): return lax.ppermute(x, 'dp', [(i, i ^ apart) for i in range(replicas)])  16.1 us
    all_to_all x3, starting transfers between devices, exchange(): return lax.all_to_all(x, 'dp', 0, 0, axis_index_groups=members, tiled=True)  13.3 us
    ppermute x11, waiting for transfers between devices, swap(): return lax.ppermute(x, 'dp', [(i, i ^ apart) for i in range(replicas)])  10.6 us
    all_to_all x3, waiting for transfers between devices, exchange(): return lax.all_to_all(x, 'dp', 0, 0, axis_index_groups=members, tiled=True)  8.46 us
    convert_element_type x1, other arithmetic, on_device(): hidden_out = (hidden_in.astype(F32) + contrib.astype(F32) + contrib_other...  2.08 us
    convert_element_type x1, other arithmetic, on_device(): grad_in = (grad_out.astype(F32) + returned.astype(F32) + returned_other.a...  2.08 us
    unnamed x20, local copies, waits for them, and re-layouts  1.88 us
  transfers between devices with their start and end apart: 20, of which 10 were waited for; matrix products, arithmetic and copies ran while one was open for 6% of the time, Pallas kernels for 29%

profile of v6, /device:TPU:0, one launch (start us, length us, event | category | flops | bytes accessed | tf_op | source)
XLA Modules:
  0.0 86.3 jit_solution(13770496110611289765)
XLA Ops:
  0.6 2.4 %prep.1 = (bf16[4,1024,128]{2,1,0:T(8,128)(2,1)}, bf16[128,1024]{1,0:T(8,128)(2,1)}) custom-call(bf16[128,2048]{1,0:T(8,128)(2,1)} %refs_0_.6, bf16[128,2048]{1,0:T(8,128)(2,1)} %refs_0_.7), custom_call_target="tpu_custom_call" | custom-call | tf_op jit(solution)/shard_map/prep/pallas_call | solution.py:62
  3.0 5.4 %all-to-all-start = ((bf16[4,1024,128]{2,1,0:T(8,128)(2,1)}), bf16[4,1024,128]{2,1,0:T(8,128)(2,1)}, u32[]{:S(2)}, u32[]{:S(2)}) async-start(bf16[4,1024,128]{2,1,0:T(8,128)(2,1)} %get-tuple-element.40.refs_9_), calls=%async_computation | async-start | bytes 2097152 | tf_op jit(solution)/shard_map/all_to_all | solution.py:458
  8.9 2.1 %collective-permute-start.2 = (bf16[128,1024]{1,0:T(8,128)(2,1)}, bf16[128,1024]{1,0:T(8,128)(2,1)}, u32[]{:S(2)}, u32[]{:S(2)}) collective-permute-start(bf16[128,1024]{1,0:T(8,128)(2,1)} %get-tuple-element.45), channel_id=1, source_target_pairs={{0,4},{2,6},{4,0},{6,2},{8,12},{10,14},{12,8},{14,10},{16,20},{18,... | collective-permute-start | bytes 786440 | tf_op jit(solution)/shard_map/ppermute | solution.py:451
  11.9 10.0 %attention.1 = (bf16[256,512]{1,0:T(8,128)(2,1)}, bf16[512,256]{1,0:T(8,128)(2,1)}, bf16[4,768,256]{2,1,0:T(8,128)(2,1)}) custom-call(s32[4,3]{1,0:T(4,128)} %refs_0_.5, bf16[128,2048]{1,0:T(8,128)(2,1)} %refs_0_.6, bf16[128,2048]{1,0:T(8,128)(2,1)} %copy-done.8, bf16[2048,512]{1,0:T(8,128)(2,1)} %bitcast.9, bf16[2048,512]{1,0:T(8,128)(2,1)} %bitcast.11, ...), custom_call_target="tpu_custom_call" | custom-call | flops 11000000512 | tf_op jit(solution)/shard_map/attention/pallas_call | solution.py:62
  22.7 4.3 %all-to-all-start.1 = ((bf16[4,768,256]{2,1,0:T(8,128)(2,1)}), bf16[4,768,256]{2,1,0:T(8,128)(2,1)}, u32[]{:S(2)}, u32[]{:S(2)}) async-start(bf16[4,768,256]{2,1,0:T(8,128)(2,1)} %get-tuple-element.53.refs_7_), calls=%async_computation.1 | async-start | bytes 3145728 | tf_op jit(solution)/shard_map/all_to_all | solution.py:458
  27.6 1.7 %collective-permute-start.4 = (bf16[512,256]{1,0:T(8,128)(2,1)}, bf16[512,256]{1,0:T(8,128)(2,1)}, u32[]{:S(2)}, u32[]{:S(2)}) collective-permute-start(bf16[512,256]{1,0:T(8,128)(2,1)} %get-tuple-element.47.refs_4_), channel_id=1, source_target_pairs={{0,4},{2,6},{4,0},{6,2},{8,12},{10,14},{12,8},{14,10},{16,20},{18,... | collective-permute-start | bytes 786440 | tf_op jit(solution)/shard_map/ppermute | solution.py:451
  29.3 6.7 %returned.1 = (bf16[128,2048]{1,0:T(8,128)(2,1)}, bf16[128,2048]{1,0:T(8,128)(2,1)}, bf16[128,2048]{1,0:T(8,128)(2,1)}, bf16[128,2048]{1,0:T(8,128)(2,1)}) custom-call(bf16[128,2048]{1,0:T(8,128)(2,1)} %refs_0_.6, bf16[128,2048]{1,0:T(8,128)(2,1)} %copy-done.8, bf16[256,512]{1,0:T(8,128)(2,1)} %get-tuple-element.41.refs_2_, bf16[512,2048]{1,0:T(8,128)(2,1)} %bitcast.16, ...), custom_call_target="tpu_custom_call" | custom-call | tf_op jit(solution)/shard_map/returned/pallas_call | solution.py:62
  36.2 2.8 %out_grad.1 = (bf16[128,1024]{1,0:T(8,128)(2,1)}, bf16[128,1024]{1,0:T(8,128)(2,1)}, bf16[128,1024]{1,0:T(8,128)(2,1)}, bf16[128,1024]{1,0:T(8,128)(2,1)}) custom-call(bf16[128,2048]{1,0:T(8,128)(2,1)} %refs_0_.7, bf16[128,2048]{1,0:T(8,128)(2,1)} %copy-done.7, bf16[128,1024]{1,0:T(8,128)(2,1)} %collective-permute-done.2.refs_2_, ...), custom_call_target="tpu_custom_call" | custom-call | tf_op jit(solution)/shard_map/out_grad/pallas_call | solution.py:62
  39.0 1.9 %collective-permute-start.6 = (bf16[128,1024]{1,0:T(8,128)(2,1)}, bf16[128,1024]{1,0:T(8,128)(2,1)S(1)}, u32[]{:S(2)}, u32[]{:S(2)}) collective-permute-start(bf16[128,1024]{1,0:T(8,128)(2,1)} %get-tuple-element.50), channel_id=1, source_target_pairs={{0,8},{2,10},{4,12},{6,14},{8,0},{10,2},{12,4},{14,6},{16,24},{18,... | collective-permute-start | bytes 786440 | tf_op jit(solution)/shard_map/ppermute | solution.py:451
  41.0 1.5 %collective-permute-start.7 = (bf16[128,1024]{1,0:T(8,128)(2,1)}, bf16[128,1024]{1,0:T(8,128)(2,1)S(1)}, u32[]{:S(2)}, u32[]{:S(2)}) collective-permute-start(bf16[128,1024]{1,0:T(8,128)(2,1)} %get-tuple-element.51), channel_id=1, source_target_pairs={{0,2},{2,0},{4,6},{6,4},{8,10},{10,8},{12,14},{14,12},{16,18},{18,... | collective-permute-start | bytes 786440 | tf_op jit(solution)/shard_map/ppermute | solution.py:451
  42.6 5.1 %all-to-all-done.1.refs_2_ = bf16[4,768,256]{2,1,0:T(8,128)(2,1)} async-done(((bf16[4,768,256]{2,1,0:T(8,128)(2,1)}), bf16[4,768,256]{2,1,0:T(8,128)(2,1)}, u32[]{:S(2)}, u32[]{:S(2)}) %all-to-all-start.1) | async-done | bytes 1572896 | tf_op jit(solution)/shard_map/all_to_all | solution.py:458
  48.7 3.5 %projection_grad.1 = (bf16[512,512]{1,0:T(8,128)(2,1)S(1)}, bf16[512,512]{1,0:T(8,128)(2,1)S(1)}, bf16[512,256]{1,0:T(8,128)(2,1)S(1)}, bf16[512,256]{1,0:T(8,128)(2,1)S(1)}) custom-call(bf16[4,1024,128]{2,1,0:T(8,128)(2,1)} %all-to-all-done.refs_0_, bf16[4,1024,128]{2,1,0:T(8,128)(2,1)} %collective-permute-done.5.refs_7_.refs_1_, ...), custom_call_target="tpu_custom_call" | custom-call | tf_op jit(solution)/shard_map/projection_grad/pallas_call | solution.py:62
  52.2 1.7 %collective-permute-start.11 = (bf16[512,512]{1,0:T(8,128)(2,1)S(1)}, bf16[512,512]{1,0:T(8,128)(2,1)S(1)}, u32[]{:S(2)}, u32[]{:S(2)}) collective-permute-start(bf16[512,512]{1,0:T(8,128)(2,1)S(1)} %get-tuple-element.54.refs_4_), channel_id=1, source_target_pairs={{0,4},{2,6},{4,0},{6,2},{8,12},{10,14},{12,8},{14,10},{16,20},{18,... | collective-permute-start | bytes 1572872 | tf_op jit(solution)/shard_map/ppermute | solution.py:451
  53.9 2.6 %collective-permute-start.12 = (bf16[512,256]{1,0:T(8,128)(2,1)S(1)}, bf16[512,256]{1,0:T(8,128)(2,1)S(1)}, u32[]{:S(2)}, u32[]{:S(2)}) collective-permute-start(bf16[512,256]{1,0:T(8,128)(2,1)S(1)} %get-tuple-element.61), channel_id=1, source_target_pairs={{0,16},{2,18},{4,20},{6,22},{8,24},{10,26},{12,28},{14,30},{16,0},... | collective-permute-start | bytes 786440 | tf_op jit(solution)/shard_map/ppermute | solution.py:451
  56.5 6.6 %collective-permute-done.8.refs_3_ = bf16[128,1024]{1,0:T(8,128)(2,1)S(1)} collective-permute-done((bf16[128,1024]{1,0:T(8,128)(2,1)}, bf16[128,1024]{1,0:T(8,128)(2,1)S(1)}, u32[]{:S(2)}, u32[]{:S(2)}) %collective-permute-start.8) | collective-permute-done | bytes 262176 | tf_op jit(solution)/shard_map/ppermute | solution.py:451
  63.1 1.5 %halve.1 = (bf16[64,1024]{1,0:T(8,128)(2,1)S(1)}, bf16[64,1024]{1,0:T(8,128)(2,1)S(1)}) custom-call(bf16[128,1024]{1,0:T(8,128)(2,1)S(1)} %copy-done.1, bf16[128,1024]{1,0:T(8,128)(2,1)S(1)} %collective-permute-done.6.refs_1_, bf16[128,1024]{1,0:T(8,128)(2,1)S(1)} %collective-permute-done.7.refs_2_, bf16[128,1024]{1,0:T(8,128)(2,1)S(1)} %collective-permute-done.8.refs_3_, ...), custom_call_target="tpu_custom_call" | custom-call | flops 11000000512 | tf_op jit(solution)/shard_map/halve/pallas_call | solution.py:62
  65.3 1.5 %collective-permute-done.12.refs_1_ = bf16[512,256]{1,0:T(8,128)(2,1)S(1)} collective-permute-done((bf16[512,256]{1,0:T(8,128)(2,1)S(1)}, bf16[512,256]{1,0:T(8,128)(2,1)S(1)}, u32[]{:S(2)}, u32[]{:S(2)}) %collective-permute-start.12) | collective-permute-done | bytes 262176 | tf_op jit(solution)/shard_map/ppermute | solution.py:451
  67.7 3.6 %all-to-all-start.2 = ((bf16[4,128,512]{2,1,0:T(8,128)(2,1)}), bf16[4,128,512]{2,1,0:T(8,128)(2,1)S(1)}, u32[]{:S(2)}, u32[]{:S(2)}) async-start(bf16[4,128,512]{2,1,0:T(8,128)(2,1)} %bitcast.4), calls=%async_computation.2 | async-start | bytes 1048576 | tf_op jit(solution)/shard_map/all_to_all | solution.py:458
  71.4 1.3 %collective-permute-done.13.refs_3_ = bf16[64,1024]{1,0:T(8,128)(2,1)S(1)} collective-permute-done((bf16[64,1024]{1,0:T(8,128)(2,1)S(1)}, bf16[64,1024]{1,0:T(8,128)(2,1)S(1)}, u32[]{:S(2)}, u32[]{:S(2)}) %collective-permute-start.13) | collective-permute-done | bytes 131104 | tf_op jit(solution)/shard_map/ppermute | solution.py:451
  73.2 2.9 %collective-permute-start.14 = (bf16[256,256]{1,0:T(8,128)(2,1)S(1)}, bf16[256,256]{1,0:T(8,128)(2,1)S(1)}, u32[]{:S(2)}, u32[]{:S(2)}) collective-permute-start(bf16[256,256]{1,0:T(8,128)(2,1)S(1)} %get-tuple-element.66), channel_id=1, source_target_pairs={{0,4},{2,6},{4,0},{6,2},{8,12},{10,14},{12,8},{14,10},{16,20},{18,... | collective-permute-start | bytes 393224 | tf_op jit(solution)/shard_map/ppermute | solution.py:451
  76.1 1.4 %collective-permute-start.15 = (bf16[128,256]{1,0:T(8,128)(2,1)S(1)}, bf16[128,256]{1,0:T(8,128)(2,1)S(1)}, u32[]{:S(2)}, u32[]{:S(2)}) collective-permute-start(bf16[128,256]{1,0:T(8,128)(2,1)S(1)} %get-tuple-element.67), channel_id=1, source_target_pairs={{0,2},{2,0},{4,6},{6,4},{8,10},{10,8},{12,14},{14,12},{16,18},{18,... | collective-permute-start | bytes 196616 | tf_op jit(solution)/shard_map/ppermute | solution.py:451
  77.6 2.1 %add_convert_fusion.2 = bf16[128,2048]{1,0:T(8,128)(2,1)} fusion(bf16[128,2048]{1,0:T(8,128)(2,1)} %collective-permute-done.9, bf16[128,2048]{1,0:T(8,128)(2,1)S(1)} %copy-done.6, bf16[128,2048]{1,0:T(8,128)(2,1)S(1)} %copy-done.3), kind=kLoop, calls=%fused_computation.2 | loop fusion | flops 1572864 | bytes 2097152 | tf_op jit(solution)/shard_map/convert_element_type | solution.py:591
  79.7 2.1 %add_convert_fusion.1 = bf16[128,2048]{1,0:T(8,128)(2,1)} fusion(bf16[128,2048]{1,0:T(8,128)(2,1)} %collective-permute-done.10, bf16[128,2048]{1,0:T(8,128)(2,1)S(1)} %copy-done.9, bf16[128,2048]{1,0:T(8,128)(2,1)S(1)} %copy-done.5), kind=kLoop, calls=%fused_computation.1 | loop fusion | flops 1572864 | bytes 2097152 | tf_op jit(solution)/shard_map/convert_element_type | solution.py:594
  82.7 2.6 %all-to-all-done.2.refs_0_ = bf16[4,128,512]{2,1,0:T(8,128)(2,1)S(1)} async-done(((bf16[4,128,512]{2,1,0:T(8,128)(2,1)}), bf16[4,128,512]{2,1,0:T(8,128)(2,1)S(1)}, u32[]{:S(2)}, u32[]{:S(2)}) %all-to-all-start.2) | async-done | bytes 524320 | tf_op jit(solution)/shard_map/all_to_all | solution.py:458
  (47 shorter events, 8.2 us)
Async XLA Ops:
  3.0 19.6 %all-to-all-start = ((bf16[4,1024,128]{2,1,0:T(8,128)(2,1)}), bf16[4,1024,128]{2,1,0:T(8,128)(2,1)}, u32[]{:S(2)}, u32[]{:S(2)}) async-start(bf16[4,1024,128]{2,1,0:T(8,128)(2,1)} %get-tuple-element.40.refs_9_), calls=%async_computation | async-start | bytes 2097152 | tf_op jit(solution)/shard_map/all_to_all | solution.py:458
  8.4 2.6 %collective-permute-start = (bf16[128,2048]{1,0:T(8,128)(2,1)S(1)}, bf16[128,2048]{1,0:T(8,128)(2,1)S(1)}, u32[]{:S(2)}, u32[]{:S(2)}) collective-permute-start(bf16[128,2048]{1,0:T(8,128)(2,1)S(1)} %copy-done.2), channel_id=1, source_target_pairs={{0,1},{1,0},{2,3},{3,2},{4,5},{5,4},{6,7},{7,6},{8,9},{9,8},{10,11... | collective-permute-start | bytes 1572872 | tf_op jit(solution)/shard_map/ppermute | solution.py:454
  8.4 2.6 %collective-permute-start.1 = (bf16[128,2048]{1,0:T(8,128)(2,1)S(1)}, bf16[128,2048]{1,0:T(8,128)(2,1)S(1)}, u32[]{:S(2)}, u32[]{:S(2)}) collective-permute-start(bf16[128,2048]{1,0:T(8,128)(2,1)S(1)} %copy-done.4), channel_id=1, source_target_pairs={{0,1},{1,0},{2,3},{3,2},{4,5},{5,4},{6,7},{7,6},{8,9},{9,8},{10,11... | collective-permute-start | bytes 1572872 | tf_op jit(solution)/shard_map/ppermute | solution.py:454
  8.9 13.0 %collective-permute-start.2 = (bf16[128,1024]{1,0:T(8,128)(2,1)}, bf16[128,1024]{1,0:T(8,128)(2,1)}, u32[]{:S(2)}, u32[]{:S(2)}) collective-permute-start(bf16[128,1024]{1,0:T(8,128)(2,1)} %get-tuple-element.45), channel_id=1, source_target_pairs={{0,4},{2,6},{4,0},{6,2},{8,12},{10,14},{12,8},{14,10},{16,20},{18,... | collective-permute-start | bytes 786440 | tf_op jit(solution)/shard_map/ppermute | solution.py:451
  22.7 25.1 %all-to-all-start.1 = ((bf16[4,768,256]{2,1,0:T(8,128)(2,1)}), bf16[4,768,256]{2,1,0:T(8,128)(2,1)}, u32[]{:S(2)}, u32[]{:S(2)}) async-start(bf16[4,768,256]{2,1,0:T(8,128)(2,1)} %get-tuple-element.53.refs_7_), calls=%async_computation.1 | async-start | bytes 3145728 | tf_op jit(solution)/shard_map/all_to_all | solution.py:458
  27.0 9.2 %collective-permute-start.5 = (bf16[4,1024,128]{2,1,0:T(8,128)(2,1)}, bf16[4,1024,128]{2,1,0:T(8,128)(2,1)}, u32[]{:S(2)}, u32[]{:S(2)}) collective-permute-start(bf16[4,1024,128]{2,1,0:T(8,128)(2,1)} %all-to-all-done.refs_0_), channel_id=1, source_target_pairs={{0,1},{1,0},{2,3},{3,2},{4,5},{5,4},{6,7},{7,6},{8,9},{9,8},{10,11... | collective-permute-start | bytes 3145736 | tf_op jit(solution)/shard_map/ppermute | solution.py:454
  27.1 8.8 %collective-permute-start.3 = (bf16[128,1024]{1,0:T(8,128)(2,1)}, bf16[128,1024]{1,0:T(8,128)(2,1)}, u32[]{:S(2)}, u32[]{:S(2)}) collective-permute-start(bf16[128,1024]{1,0:T(8,128)(2,1)} %collective-permute-done.2.refs_2_), channel_id=1, source_target_pairs={{0,1},{1,0},{2,3},{3,2},{4,5},{5,4},{6,7},{7,6},{8,9},{9,8},{10,11... | collective-permute-start | bytes 786440 | tf_op jit(solution)/shard_map/ppermute | solution.py:454
  27.6 8.6 %collective-permute-start.4 = (bf16[512,256]{1,0:T(8,128)(2,1)}, bf16[512,256]{1,0:T(8,128)(2,1)}, u32[]{:S(2)}, u32[]{:S(2)}) collective-permute-start(bf16[512,256]{1,0:T(8,128)(2,1)} %get-tuple-element.47.refs_4_), channel_id=1, source_target_pairs={{0,4},{2,6},{4,0},{6,2},{8,12},{10,14},{12,8},{14,10},{16,20},{18,... | collective-permute-start | bytes 786440 | tf_op jit(solution)/shard_map/ppermute | solution.py:451
  39.0 17.5 %collective-permute-start.6 = (bf16[128,1024]{1,0:T(8,128)(2,1)}, bf16[128,1024]{1,0:T(8,128)(2,1)S(1)}, u32[]{:S(2)}, u32[]{:S(2)}) collective-permute-start(bf16[128,1024]{1,0:T(8,128)(2,1)} %get-tuple-element.50), channel_id=1, source_target_pairs={{0,8},{2,10},{4,12},{6,14},{8,0},{10,2},{12,4},{14,6},{16,24},{18,... | collective-permute-start | bytes 786440 | tf_op jit(solution)/shard_map/ppermute | solution.py:451
  41.0 15.6 %collective-permute-start.7 = (bf16[128,1024]{1,0:T(8,128)(2,1)}, bf16[128,1024]{1,0:T(8,128)(2,1)S(1)}, u32[]{:S(2)}, u32[]{:S(2)}) collective-permute-start(bf16[128,1024]{1,0:T(8,128)(2,1)} %get-tuple-element.51), channel_id=1, source_target_pairs={{0,2},{2,0},{4,6},{6,4},{8,10},{10,8},{12,14},{14,12},{16,18},{18,... | collective-permute-start | bytes 786440 | tf_op jit(solution)/shard_map/ppermute | solution.py:451
  42.4 20.7 %collective-permute-start.8 = (bf16[128,1024]{1,0:T(8,128)(2,1)}, bf16[128,1024]{1,0:T(8,128)(2,1)S(1)}, u32[]{:S(2)}, u32[]{:S(2)}) collective-permute-start(bf16[128,1024]{1,0:T(8,128)(2,1)} %get-tuple-element.52), channel_id=1, source_target_pairs={{0,10},{2,8},{4,14},{6,12},{8,2},{10,0},{12,6},{14,4},{16,26},{18,... | collective-permute-start | bytes 786440 | tf_op jit(solution)/shard_map/ppermute | solution.py:451
  48.7 14.4 %copy-start.1 = (bf16[128,1024]{1,0:T(8,128)(2,1)S(1)}, bf16[128,1024]{1,0:T(8,128)(2,1)}, u32[]{:S(2)}) copy-start(bf16[128,1024]{1,0:T(8,128)(2,1)} %get-tuple-element.49.refs_3_.refs_0_) | copy-start | bytes 786436
  52.2 14.6 %collective-permute-start.11 = (bf16[512,512]{1,0:T(8,128)(2,1)S(1)}, bf16[512,512]{1,0:T(8,128)(2,1)S(1)}, u32[]{:S(2)}, u32[]{:S(2)}) collective-permute-start(bf16[512,512]{1,0:T(8,128)(2,1)S(1)} %get-tuple-element.54.refs_4_), channel_id=1, source_target_pairs={{0,4},{2,6},{4,0},{6,2},{8,12},{10,14},{12,8},{14,10},{16,20},{18,... | collective-permute-start | bytes 1572872 | tf_op jit(solution)/shard_map/ppermute | solution.py:451
  53.9 12.9 %collective-permute-start.12 = (bf16[512,256]{1,0:T(8,128)(2,1)S(1)}, bf16[512,256]{1,0:T(8,128)(2,1)S(1)}, u32[]{:S(2)}, u32[]{:S(2)}) collective-permute-start(bf16[512,256]{1,0:T(8,128)(2,1)S(1)} %get-tuple-element.61), channel_id=1, source_target_pairs={{0,16},{2,18},{4,20},{6,22},{8,24},{10,26},{12,28},{14,30},{16,0},... | collective-permute-start | bytes 786440 | tf_op jit(solution)/shard_map/ppermute | solution.py:451
  64.7 13.0 %copy-start.3 = (bf16[128,2048]{1,0:T(8,128)(2,1)S(1)}, bf16[128,2048]{1,0:T(8,128)(2,1)}, u32[]{:S(2)}) copy-start(bf16[128,2048]{1,0:T(8,128)(2,1)} %refs_0_.6) | copy-start | bytes 1572868
  64.7 12.9 %copy-start.6 = (bf16[128,2048]{1,0:T(8,128)(2,1)S(1)}, bf16[128,2048]{1,0:T(8,128)(2,1)}, u32[]{:S(2)}) copy-start(bf16[128,2048]{1,0:T(8,128)(2,1)} %get-tuple-element.43.refs_6_) | copy-start | bytes 1572868
  64.7 12.9 %collective-permute-start.9 = (bf16[128,2048]{1,0:T(8,128)(2,1)}, bf16[128,2048]{1,0:T(8,128)(2,1)}, u32[]{:S(2)}, u32[]{:S(2)}) collective-permute-start(bf16[128,2048]{1,0:T(8,128)(2,1)} %get-tuple-element.56), channel_id=1, source_target_pairs={{0,1},{1,0},{2,3},{3,2},{4,5},{5,4},{6,7},{7,6},{8,9},{9,8},{10,11... | collective-permute-start | bytes 1572872 | tf_op jit(solution)/shard_map/ppermute | solution.py:454
  64.8 7.9 %collective-permute-start.13 = (bf16[64,1024]{1,0:T(8,128)(2,1)S(1)}, bf16[64,1024]{1,0:T(8,128)(2,1)S(1)}, u32[]{:S(2)}, u32[]{:S(2)}) collective-permute-start(bf16[64,1024]{1,0:T(8,128)(2,1)S(1)} %get-tuple-element.55), channel_id=1, source_target_pairs={{0,16},{2,18},{4,20},{6,22},{8,24},{10,26},{12,28},{14,30},{16,0},... | collective-permute-start | bytes 393224 | tf_op jit(solution)/shard_map/ppermute | solution.py:451
  64.8 14.9 %collective-permute-start.10 = (bf16[128,2048]{1,0:T(8,128)(2,1)}, bf16[128,2048]{1,0:T(8,128)(2,1)}, u32[]{:S(2)}, u32[]{:S(2)}) collective-permute-start(bf16[128,2048]{1,0:T(8,128)(2,1)} %get-tuple-element.59), channel_id=1, source_target_pairs={{0,1},{1,0},{2,3},{3,2},{4,5},{5,4},{6,7},{7,6},{8,9},{9,8},{10,11... | collective-permute-start | bytes 1572872 | tf_op jit(solution)/shard_map/ppermute | solution.py:454
  67.7 12.0 %copy-start.9 = (bf16[128,2048]{1,0:T(8,128)(2,1)S(1)}, bf16[128,2048]{1,0:T(8,128)(2,1)}, u32[]{:S(2)}) copy-start(bf16[128,2048]{1,0:T(8,128)(2,1)} %get-tuple-element.57) | copy-start | bytes 1572868
  67.7 17.5 %all-to-all-start.2 = ((bf16[4,128,512]{2,1,0:T(8,128)(2,1)}), bf16[4,128,512]{2,1,0:T(8,128)(2,1)S(1)}, u32[]{:S(2)}, u32[]{:S(2)}) async-start(bf16[4,128,512]{2,1,0:T(8,128)(2,1)} %bitcast.4), calls=%async_computation.2 | async-start | bytes 1048576 | tf_op jit(solution)/shard_map/all_to_all | solution.py:458
  73.2 9.5 %collective-permute-start.14 = (bf16[256,256]{1,0:T(8,128)(2,1)S(1)}, bf16[256,256]{1,0:T(8,128)(2,1)S(1)}, u32[]{:S(2)}, u32[]{:S(2)}) collective-permute-start(bf16[256,256]{1,0:T(8,128)(2,1)S(1)} %get-tuple-element.66), channel_id=1, source_target_pairs={{0,4},{2,6},{4,0},{6,2},{8,12},{10,14},{12,8},{14,10},{16,20},{18,... | collective-permute-start | bytes 393224 | tf_op jit(solution)/shard_map/ppermute | solution.py:451
  76.1 6.0 %collective-permute-start.15 = (bf16[128,256]{1,0:T(8,128)(2,1)S(1)}, bf16[128,256]{1,0:T(8,128)(2,1)S(1)}, u32[]{:S(2)}, u32[]{:S(2)}) collective-permute-start(bf16[128,256]{1,0:T(8,128)(2,1)S(1)} %get-tuple-element.67), channel_id=1, source_target_pairs={{0,2},{2,0},{4,6},{6,4},{8,10},{10,8},{12,14},{14,12},{16,18},{18,... | collective-permute-start | bytes 196616 | tf_op jit(solution)/shard_map/ppermute | solution.py:451
  77.5 5.2 %collective-permute-start.16 = (bf16[128,256]{1,0:T(8,128)(2,1)S(1)}, bf16[128,256]{1,0:T(8,128)(2,1)S(1)}, u32[]{:S(2)}, u32[]{:S(2)}) collective-permute-start(bf16[128,256]{1,0:T(8,128)(2,1)S(1)} %get-tuple-element.68), channel_id=1, source_target_pairs={{0,6},{2,4},{4,2},{6,0},{8,14},{10,12},{12,10},{14,8},{16,22},{18,... | collective-permute-start | bytes 196616 | tf_op jit(solution)/shard_map/ppermute | solution.py:451
  (6 other events, 25.6 us)

commit v7 on v6

--- a/solution.py
+++ b/solution.py
@@ -113,7 +113,7 @@
     away = pl.ds(pl.multiple_of((1 - bit_here(OUT_BIT)) * columns, columns), columns)
     x_copy, g_copy = fetch([(hidden, x), (grad.at[:, away], g)], sems)
     x_copy.wait()
-    turned[...] = x[...].astype(F32).T.astype(BF16)
+    turned[...] = x[...].T
     sends = []
     for row in range(2):
         own = [chunk | row << PROJECTION_BITS[0] for chunk in chunks]
@@ -235,7 +235,7 @@
             put(1, col, seq * seq_len, here, dot_tn(score, q2) * r)
             put(2, col, seq * seq_len, here, merged(dot(score, k)) * r)
 
-    turned[...] = attended[...].astype(F32).T.astype(BF16)
+    turned[...] = attended[...].T
     copy_chunks(turned, att_turned, out_chunks, half // len(out_chunks))
 
 
@@ -582,7 +582,7 @@
         return [keep, swap(send, bits[0])], bits[1:], send
 
     out, out_left, last = stepped(
-        [out_keep] + out_arrived, out_bits[2:] + [OUT_BIT], pair_send, LONG_WORK
+        [out_keep] + out_arrived, out_bits[2:] + [OUT_BIT], pair_send, LONG_WORK // 2
     )
     contrib_other = mirror(follows(contrib_mirror, last))
     returned_other = mirror(follows(returned_mirror, last))

time: 87.3 us -> 87.3 us (level)
  no operation moved by 1% of the time
where the time goes in v7:
time: 87.3 us; the launch traced here: 86.2 us
  starting transfers between devices  30.9 us (35%)
  Pallas kernels  28.3 us (32%)
  waiting for transfers between devices  19.2 us (22%)
  other arithmetic  5.1 us (6%)
  local copies, waits for them, and re-layouts  1.88 us (2%)
    pallas_call x8, Pallas kernels, call(): pl.pallas_call(run, name=name, out_shape=outs, in_specs=specs, out_specs=...  28.3 us
    ppermute x11, starting transfers between devices, swap(): return lax.ppermute(x, 'dp', [(i, i ^ apart) for i in range(replicas)])  16.1 us
    all_to_all x3, starting transfers between devices, exchange(): return lax.all_to_all(x, 'dp', 0, 0, axis_index_groups=members, tiled=True)  13.3 us
    ppermute x11, waiting for transfers between devices, swap(): return lax.ppermute(x, 'dp', [(i, i ^ apart) for i in range(replicas)])  10.6 us
    all_to_all x3, waiting for transfers between devices, exchange(): return lax.all_to_all(x, 'dp', 0, 0, axis_index_groups=members, tiled=True)  8.45 us
    convert_element_type x1, other arithmetic, on_device(): grad_in = (grad_out.astype(F32) + returned.astype(F32) + returned_other.a...  2.08 us
    convert_element_type x1, other arithmetic, on_device(): hidden_out = (hidden_in.astype(F32) + contrib.astype(F32) + contrib_other...  2.08 us
    unnamed x20, local copies, waits for them, and re-layouts  1.88 us
  transfers between devices with their start and end apart: 20, of which 10 were waited for; matrix products, arithmetic and copies ran while one was open for 6% of the time, Pallas kernels for 29%

profile of v7, /device:TPU:0, one launch (start us, length us, event | category | flops | bytes accessed | tf_op | source)
XLA Modules:
  0.0 86.2 jit_solution(1309092207568138380)
XLA Ops:
  0.6 2.3 %prep.1 = (bf16[4,1024,128]{2,1,0:T(8,128)(2,1)}, bf16[128,1024]{1,0:T(8,128)(2,1)}) custom-call(bf16[128,2048]{1,0:T(8,128)(2,1)} %refs_0_.6, bf16[128,2048]{1,0:T(8,128)(2,1)} %refs_0_.7), custom_call_target="tpu_custom_call" | custom-call | tf_op jit(solution)/shard_map/prep/pallas_call | solution.py:62
  3.0 5.4 %all-to-all-start = ((bf16[4,1024,128]{2,1,0:T(8,128)(2,1)}), bf16[4,1024,128]{2,1,0:T(8,128)(2,1)}, u32[]{:S(2)}, u32[]{:S(2)}) async-start(bf16[4,1024,128]{2,1,0:T(8,128)(2,1)} %get-tuple-element.40.refs_9_), calls=%async_computation | async-start | bytes 2097152 | tf_op jit(solution)/shard_map/all_to_all | solution.py:458
  8.9 2.1 %collective-permute-start.2 = (bf16[128,1024]{1,0:T(8,128)(2,1)}, bf16[128,1024]{1,0:T(8,128)(2,1)}, u32[]{:S(2)}, u32[]{:S(2)}) collective-permute-start(bf16[128,1024]{1,0:T(8,128)(2,1)} %get-tuple-element.45), channel_id=1, source_target_pairs={{0,4},{2,6},{4,0},{6,2},{8,12},{10,14},{12,8},{14,10},{16,20},{18,... | collective-permute-start | bytes 786440 | tf_op jit(solution)/shard_map/ppermute | solution.py:451
  11.9 10.0 %attention.1 = (bf16[256,512]{1,0:T(8,128)(2,1)}, bf16[512,256]{1,0:T(8,128)(2,1)}, bf16[4,768,256]{2,1,0:T(8,128)(2,1)}) custom-call(s32[4,3]{1,0:T(4,128)} %refs_0_.5, bf16[128,2048]{1,0:T(8,128)(2,1)} %refs_0_.6, bf16[128,2048]{1,0:T(8,128)(2,1)} %copy-done.8, bf16[2048,512]{1,0:T(8,128)(2,1)} %bitcast.9, bf16[2048,512]{1,0:T(8,128)(2,1)} %bitcast.11, ...), custom_call_target="tpu_custom_call" | custom-call | flops 11000000512 | tf_op jit(solution)/shard_map/attention/pallas_call | solution.py:62
  22.7 4.3 %all-to-all-start.1 = ((bf16[4,768,256]{2,1,0:T(8,128)(2,1)}), bf16[4,768,256]{2,1,0:T(8,128)(2,1)}, u32[]{:S(2)}, u32[]{:S(2)}) async-start(bf16[4,768,256]{2,1,0:T(8,128)(2,1)} %get-tuple-element.53.refs_7_), calls=%async_computation.1 | async-start | bytes 3145728 | tf_op jit(solution)/shard_map/all_to_all | solution.py:458
  27.6 1.7 %collective-permute-start.4 = (bf16[512,256]{1,0:T(8,128)(2,1)}, bf16[512,256]{1,0:T(8,128)(2,1)}, u32[]{:S(2)}, u32[]{:S(2)}) collective-permute-start(bf16[512,256]{1,0:T(8,128)(2,1)} %get-tuple-element.47.refs_4_), channel_id=1, source_target_pairs={{0,4},{2,6},{4,0},{6,2},{8,12},{10,14},{12,8},{14,10},{16,20},{18,... | collective-permute-start | bytes 786440 | tf_op jit(solution)/shard_map/ppermute | solution.py:451
  29.3 6.7 %returned.1 = (bf16[128,2048]{1,0:T(8,128)(2,1)}, bf16[128,2048]{1,0:T(8,128)(2,1)}, bf16[128,2048]{1,0:T(8,128)(2,1)}, bf16[128,2048]{1,0:T(8,128)(2,1)}) custom-call(bf16[128,2048]{1,0:T(8,128)(2,1)} %refs_0_.6, bf16[128,2048]{1,0:T(8,128)(2,1)} %copy-done.8, bf16[256,512]{1,0:T(8,128)(2,1)} %get-tuple-element.41.refs_2_, bf16[512,2048]{1,0:T(8,128)(2,1)} %bitcast.16, ...), custom_call_target="tpu_custom_call" | custom-call | tf_op jit(solution)/shard_map/returned/pallas_call | solution.py:62
  36.2 2.8 %out_grad.1 = (bf16[128,1024]{1,0:T(8,128)(2,1)}, bf16[128,1024]{1,0:T(8,128)(2,1)}, bf16[128,1024]{1,0:T(8,128)(2,1)}, bf16[128,1024]{1,0:T(8,128)(2,1)}) custom-call(bf16[128,2048]{1,0:T(8,128)(2,1)} %refs_0_.7, bf16[128,2048]{1,0:T(8,128)(2,1)} %copy-done.7, bf16[128,1024]{1,0:T(8,128)(2,1)} %collective-permute-done.2.refs_2_, ...), custom_call_target="tpu_custom_call" | custom-call | tf_op jit(solution)/shard_map/out_grad/pallas_call | solution.py:62
  39.0 1.9 %collective-permute-start.6 = (bf16[128,1024]{1,0:T(8,128)(2,1)}, bf16[128,1024]{1,0:T(8,128)(2,1)S(1)}, u32[]{:S(2)}, u32[]{:S(2)}) collective-permute-start(bf16[128,1024]{1,0:T(8,128)(2,1)} %get-tuple-element.50), channel_id=1, source_target_pairs={{0,8},{2,10},{4,12},{6,14},{8,0},{10,2},{12,4},{14,6},{16,24},{18,... | collective-permute-start | bytes 786440 | tf_op jit(solution)/shard_map/ppermute | solution.py:451
  40.9 1.5 %collective-permute-start.7 = (bf16[128,1024]{1,0:T(8,128)(2,1)}, bf16[128,1024]{1,0:T(8,128)(2,1)S(1)}, u32[]{:S(2)}, u32[]{:S(2)}) collective-permute-start(bf16[128,1024]{1,0:T(8,128)(2,1)} %get-tuple-element.51), channel_id=1, source_target_pairs={{0,2},{2,0},{4,6},{6,4},{8,10},{10,8},{12,14},{14,12},{16,18},{18,... | collective-permute-start | bytes 786440 | tf_op jit(solution)/shard_map/ppermute | solution.py:451
  42.6 5.1 %all-to-all-done.1.refs_2_ = bf16[4,768,256]{2,1,0:T(8,128)(2,1)} async-done(((bf16[4,768,256]{2,1,0:T(8,128)(2,1)}), bf16[4,768,256]{2,1,0:T(8,128)(2,1)}, u32[]{:S(2)}, u32[]{:S(2)}) %all-to-all-start.1) | async-done | bytes 1572896 | tf_op jit(solution)/shard_map/all_to_all | solution.py:458
  48.7 3.5 %projection_grad.1 = (bf16[512,512]{1,0:T(8,128)(2,1)S(1)}, bf16[512,512]{1,0:T(8,128)(2,1)S(1)}, bf16[512,256]{1,0:T(8,128)(2,1)S(1)}, bf16[512,256]{1,0:T(8,128)(2,1)S(1)}) custom-call(bf16[4,1024,128]{2,1,0:T(8,128)(2,1)} %all-to-all-done.refs_0_, bf16[4,1024,128]{2,1,0:T(8,128)(2,1)} %collective-permute-done.5.refs_7_.refs_1_, ...), custom_call_target="tpu_custom_call" | custom-call | tf_op jit(solution)/shard_map/projection_grad/pallas_call | solution.py:62
  52.2 1.7 %collective-permute-start.11 = (bf16[512,512]{1,0:T(8,128)(2,1)S(1)}, bf16[512,512]{1,0:T(8,128)(2,1)S(1)}, u32[]{:S(2)}, u32[]{:S(2)}) collective-permute-start(bf16[512,512]{1,0:T(8,128)(2,1)S(1)} %get-tuple-element.54.refs_4_), channel_id=1, source_target_pairs={{0,4},{2,6},{4,0},{6,2},{8,12},{10,14},{12,8},{14,10},{16,20},{18,... | collective-permute-start | bytes 1572872 | tf_op jit(solution)/shard_map/ppermute | solution.py:451
  53.9 2.6 %collective-permute-start.12 = (bf16[512,256]{1,0:T(8,128)(2,1)S(1)}, bf16[512,256]{1,0:T(8,128)(2,1)S(1)}, u32[]{:S(2)}, u32[]{:S(2)}) collective-permute-start(bf16[512,256]{1,0:T(8,128)(2,1)S(1)} %get-tuple-element.61), channel_id=1, source_target_pairs={{0,16},{2,18},{4,20},{6,22},{8,24},{10,26},{12,28},{14,30},{16,0},... | collective-permute-start | bytes 786440 | tf_op jit(solution)/shard_map/ppermute | solution.py:451
  56.5 6.6 %collective-permute-done.8.refs_3_ = bf16[128,1024]{1,0:T(8,128)(2,1)S(1)} collective-permute-done((bf16[128,1024]{1,0:T(8,128)(2,1)}, bf16[128,1024]{1,0:T(8,128)(2,1)S(1)}, u32[]{:S(2)}, u32[]{:S(2)}) %collective-permute-start.8) | collective-permute-done | bytes 262176 | tf_op jit(solution)/shard_map/ppermute | solution.py:451
  63.0 1.5 %halve.1 = (bf16[64,1024]{1,0:T(8,128)(2,1)S(1)}, bf16[64,1024]{1,0:T(8,128)(2,1)S(1)}) custom-call(bf16[128,1024]{1,0:T(8,128)(2,1)S(1)} %copy-done.1, bf16[128,1024]{1,0:T(8,128)(2,1)S(1)} %collective-permute-done.6.refs_1_, bf16[128,1024]{1,0:T(8,128)(2,1)S(1)} %collective-permute-done.7.refs_2_, bf16[128,1024]{1,0:T(8,128)(2,1)S(1)} %collective-permute-done.8.refs_3_, ...), custom_call_target="tpu_custom_call" | custom-call | flops 5500000256 | tf_op jit(solution)/shard_map/halve/pallas_call | solution.py:62
  65.2 1.6 %collective-permute-done.12.refs_1_ = bf16[512,256]{1,0:T(8,128)(2,1)S(1)} collective-permute-done((bf16[512,256]{1,0:T(8,128)(2,1)S(1)}, bf16[512,256]{1,0:T(8,128)(2,1)S(1)}, u32[]{:S(2)}, u32[]{:S(2)}) %collective-permute-start.12) | collective-permute-done | bytes 262176 | tf_op jit(solution)/shard_map/ppermute | solution.py:451
  67.7 3.6 %all-to-all-start.2 = ((bf16[4,128,512]{2,1,0:T(8,128)(2,1)}), bf16[4,128,512]{2,1,0:T(8,128)(2,1)S(1)}, u32[]{:S(2)}, u32[]{:S(2)}) async-start(bf16[4,128,512]{2,1,0:T(8,128)(2,1)} %bitcast.4), calls=%async_computation.2 | async-start | bytes 1048576 | tf_op jit(solution)/shard_map/all_to_all | solution.py:458
  71.3 1.3 %collective-permute-done.13.refs_3_ = bf16[64,1024]{1,0:T(8,128)(2,1)S(1)} collective-permute-done((bf16[64,1024]{1,0:T(8,128)(2,1)S(1)}, bf16[64,1024]{1,0:T(8,128)(2,1)S(1)}, u32[]{:S(2)}, u32[]{:S(2)}) %collective-permute-start.13) | collective-permute-done | bytes 131104 | tf_op jit(solution)/shard_map/ppermute | solution.py:451
  73.2 2.8 %collective-permute-start.14 = (bf16[256,256]{1,0:T(8,128)(2,1)S(1)}, bf16[256,256]{1,0:T(8,128)(2,1)S(1)}, u32[]{:S(2)}, u32[]{:S(2)}) collective-permute-start(bf16[256,256]{1,0:T(8,128)(2,1)S(1)} %get-tuple-element.66), channel_id=1, source_target_pairs={{0,4},{2,6},{4,0},{6,2},{8,12},{10,14},{12,8},{14,10},{16,20},{18,... | collective-permute-start | bytes 393224 | tf_op jit(solution)/shard_map/ppermute | solution.py:451
  76.0 1.4 %collective-permute-start.15 = (bf16[128,256]{1,0:T(8,128)(2,1)S(1)}, bf16[128,256]{1,0:T(8,128)(2,1)S(1)}, u32[]{:S(2)}, u32[]{:S(2)}) collective-permute-start(bf16[128,256]{1,0:T(8,128)(2,1)S(1)} %get-tuple-element.67), channel_id=1, source_target_pairs={{0,2},{2,0},{4,6},{6,4},{8,10},{10,8},{12,14},{14,12},{16,18},{18,... | collective-permute-start | bytes 196616 | tf_op jit(solution)/shard_map/ppermute | solution.py:451
  77.6 2.1 %add_convert_fusion.2 = bf16[128,2048]{1,0:T(8,128)(2,1)} fusion(bf16[128,2048]{1,0:T(8,128)(2,1)} %collective-permute-done.9, bf16[128,2048]{1,0:T(8,128)(2,1)S(1)} %copy-done.6, bf16[128,2048]{1,0:T(8,128)(2,1)S(1)} %copy-done.3), kind=kLoop, calls=%fused_computation.2 | loop fusion | flops 1572864 | bytes 2097152 | tf_op jit(solution)/shard_map/convert_element_type | solution.py:591
  79.7 2.1 %add_convert_fusion.1 = bf16[128,2048]{1,0:T(8,128)(2,1)} fusion(bf16[128,2048]{1,0:T(8,128)(2,1)} %collective-permute-done.10, bf16[128,2048]{1,0:T(8,128)(2,1)S(1)} %copy-done.9, bf16[128,2048]{1,0:T(8,128)(2,1)S(1)} %copy-done.5), kind=kLoop, calls=%fused_computation.1 | loop fusion | flops 1572864 | bytes 2097152 | tf_op jit(solution)/shard_map/convert_element_type | solution.py:594
  82.6 2.6 %all-to-all-done.2.refs_0_ = bf16[4,128,512]{2,1,0:T(8,128)(2,1)S(1)} async-done(((bf16[4,128,512]{2,1,0:T(8,128)(2,1)}), bf16[4,128,512]{2,1,0:T(8,128)(2,1)S(1)}, u32[]{:S(2)}, u32[]{:S(2)}) %all-to-all-start.2) | async-done | bytes 524320 | tf_op jit(solution)/shard_map/all_to_all | solution.py:458
  (47 shorter events, 8.2 us)
Async XLA Ops:
  3.0 19.6 %all-to-all-start = ((bf16[4,1024,128]{2,1,0:T(8,128)(2,1)}), bf16[4,1024,128]{2,1,0:T(8,128)(2,1)}, u32[]{:S(2)}, u32[]{:S(2)}) async-start(bf16[4,1024,128]{2,1,0:T(8,128)(2,1)} %get-tuple-element.40.refs_9_), calls=%async_computation | async-start | bytes 2097152 | tf_op jit(solution)/shard_map/all_to_all | solution.py:458
  8.4 2.6 %collective-permute-start = (bf16[128,2048]{1,0:T(8,128)(2,1)S(1)}, bf16[128,2048]{1,0:T(8,128)(2,1)S(1)}, u32[]{:S(2)}, u32[]{:S(2)}) collective-permute-start(bf16[128,2048]{1,0:T(8,128)(2,1)S(1)} %copy-done.2), channel_id=1, source_target_pairs={{0,1},{1,0},{2,3},{3,2},{4,5},{5,4},{6,7},{7,6},{8,9},{9,8},{10,11... | collective-permute-start | bytes 1572872 | tf_op jit(solution)/shard_map/ppermute | solution.py:454
  8.4 2.6 %collective-permute-start.1 = (bf16[128,2048]{1,0:T(8,128)(2,1)S(1)}, bf16[128,2048]{1,0:T(8,128)(2,1)S(1)}, u32[]{:S(2)}, u32[]{:S(2)}) collective-permute-start(bf16[128,2048]{1,0:T(8,128)(2,1)S(1)} %copy-done.4), channel_id=1, source_target_pairs={{0,1},{1,0},{2,3},{3,2},{4,5},{5,4},{6,7},{7,6},{8,9},{9,8},{10,11... | collective-permute-start | bytes 1572872 | tf_op jit(solution)/shard_map/ppermute | solution.py:454
  8.9 13.0 %collective-permute-start.2 = (bf16[128,1024]{1,0:T(8,128)(2,1)}, bf16[128,1024]{1,0:T(8,128)(2,1)}, u32[]{:S(2)}, u32[]{:S(2)}) collective-permute-start(bf16[128,1024]{1,0:T(8,128)(2,1)} %get-tuple-element.45), channel_id=1, source_target_pairs={{0,4},{2,6},{4,0},{6,2},{8,12},{10,14},{12,8},{14,10},{16,20},{18,... | collective-permute-start | bytes 786440 | tf_op jit(solution)/shard_map/ppermute | solution.py:451
  22.7 25.1 %all-to-all-start.1 = ((bf16[4,768,256]{2,1,0:T(8,128)(2,1)}), bf16[4,768,256]{2,1,0:T(8,128)(2,1)}, u32[]{:S(2)}, u32[]{:S(2)}) async-start(bf16[4,768,256]{2,1,0:T(8,128)(2,1)} %get-tuple-element.53.refs_7_), calls=%async_computation.1 | async-start | bytes 3145728 | tf_op jit(solution)/shard_map/all_to_all | solution.py:458
  27.0 9.2 %collective-permute-start.5 = (bf16[4,1024,128]{2,1,0:T(8,128)(2,1)}, bf16[4,1024,128]{2,1,0:T(8,128)(2,1)}, u32[]{:S(2)}, u32[]{:S(2)}) collective-permute-start(bf16[4,1024,128]{2,1,0:T(8,128)(2,1)} %all-to-all-done.refs_0_), channel_id=1, source_target_pairs={{0,1},{1,0},{2,3},{3,2},{4,5},{5,4},{6,7},{7,6},{8,9},{9,8},{10,11... | collective-permute-start | bytes 3145736 | tf_op jit(solution)/shard_map/ppermute | solution.py:454
  27.1 8.8 %collective-permute-start.3 = (bf16[128,1024]{1,0:T(8,128)(2,1)}, bf16[128,1024]{1,0:T(8,128)(2,1)}, u32[]{:S(2)}, u32[]{:S(2)}) collective-permute-start(bf16[128,1024]{1,0:T(8,128)(2,1)} %collective-permute-done.2.refs_2_), channel_id=1, source_target_pairs={{0,1},{1,0},{2,3},{3,2},{4,5},{5,4},{6,7},{7,6},{8,9},{9,8},{10,11... | collective-permute-start | bytes 786440 | tf_op jit(solution)/shard_map/ppermute | solution.py:454
  27.6 8.6 %collective-permute-start.4 = (bf16[512,256]{1,0:T(8,128)(2,1)}, bf16[512,256]{1,0:T(8,128)(2,1)}, u32[]{:S(2)}, u32[]{:S(2)}) collective-permute-start(bf16[512,256]{1,0:T(8,128)(2,1)} %get-tuple-element.47.refs_4_), channel_id=1, source_target_pairs={{0,4},{2,6},{4,0},{6,2},{8,12},{10,14},{12,8},{14,10},{16,20},{18,... | collective-permute-start | bytes 786440 | tf_op jit(solution)/shard_map/ppermute | solution.py:451
  39.0 17.5 %collective-permute-start.6 = (bf16[128,1024]{1,0:T(8,128)(2,1)}, bf16[128,1024]{1,0:T(8,128)(2,1)S(1)}, u32[]{:S(2)}, u32[]{:S(2)}) collective-permute-start(bf16[128,1024]{1,0:T(8,128)(2,1)} %get-tuple-element.50), channel_id=1, source_target_pairs={{0,8},{2,10},{4,12},{6,14},{8,0},{10,2},{12,4},{14,6},{16,24},{18,... | collective-permute-start | bytes 786440 | tf_op jit(solution)/shard_map/ppermute | solution.py:451
  40.9 15.6 %collective-permute-start.7 = (bf16[128,1024]{1,0:T(8,128)(2,1)}, bf16[128,1024]{1,0:T(8,128)(2,1)S(1)}, u32[]{:S(2)}, u32[]{:S(2)}) collective-permute-start(bf16[128,1024]{1,0:T(8,128)(2,1)} %get-tuple-element.51), channel_id=1, source_target_pairs={{0,2},{2,0},{4,6},{6,4},{8,10},{10,8},{12,14},{14,12},{16,18},{18,... | collective-permute-start | bytes 786440 | tf_op jit(solution)/shard_map/ppermute | solution.py:451
  42.4 20.6 %collective-permute-start.8 = (bf16[128,1024]{1,0:T(8,128)(2,1)}, bf16[128,1024]{1,0:T(8,128)(2,1)S(1)}, u32[]{:S(2)}, u32[]{:S(2)}) collective-permute-start(bf16[128,1024]{1,0:T(8,128)(2,1)} %get-tuple-element.52), channel_id=1, source_target_pairs={{0,10},{2,8},{4,14},{6,12},{8,2},{10,0},{12,6},{14,4},{16,26},{18,... | collective-permute-start | bytes 786440 | tf_op jit(solution)/shard_map/ppermute | solution.py:451
  48.7 14.4 %copy-start.1 = (bf16[128,1024]{1,0:T(8,128)(2,1)S(1)}, bf16[128,1024]{1,0:T(8,128)(2,1)}, u32[]{:S(2)}) copy-start(bf16[128,1024]{1,0:T(8,128)(2,1)} %get-tuple-element.49.refs_3_.refs_0_) | copy-start | bytes 786436
  52.2 14.6 %collective-permute-start.11 = (bf16[512,512]{1,0:T(8,128)(2,1)S(1)}, bf16[512,512]{1,0:T(8,128)(2,1)S(1)}, u32[]{:S(2)}, u32[]{:S(2)}) collective-permute-start(bf16[512,512]{1,0:T(8,128)(2,1)S(1)} %get-tuple-element.54.refs_4_), channel_id=1, source_target_pairs={{0,4},{2,6},{4,0},{6,2},{8,12},{10,14},{12,8},{14,10},{16,20},{18,... | collective-permute-start | bytes 1572872 | tf_op jit(solution)/shard_map/ppermute | solution.py:451
  53.9 12.9 %collective-permute-start.12 = (bf16[512,256]{1,0:T(8,128)(2,1)S(1)}, bf16[512,256]{1,0:T(8,128)(2,1)S(1)}, u32[]{:S(2)}, u32[]{:S(2)}) collective-permute-start(bf16[512,256]{1,0:T(8,128)(2,1)S(1)} %get-tuple-element.61), channel_id=1, source_target_pairs={{0,16},{2,18},{4,20},{6,22},{8,24},{10,26},{12,28},{14,30},{16,0},... | collective-permute-start | bytes 786440 | tf_op jit(solution)/shard_map/ppermute | solution.py:451
  64.6 13.0 %copy-start.3 = (bf16[128,2048]{1,0:T(8,128)(2,1)S(1)}, bf16[128,2048]{1,0:T(8,128)(2,1)}, u32[]{:S(2)}) copy-start(bf16[128,2048]{1,0:T(8,128)(2,1)} %refs_0_.6) | copy-start | bytes 1572868
  64.6 13.0 %copy-start.6 = (bf16[128,2048]{1,0:T(8,128)(2,1)S(1)}, bf16[128,2048]{1,0:T(8,128)(2,1)}, u32[]{:S(2)}) copy-start(bf16[128,2048]{1,0:T(8,128)(2,1)} %get-tuple-element.43.refs_6_) | copy-start | bytes 1572868
  64.6 13.0 %collective-permute-start.9 = (bf16[128,2048]{1,0:T(8,128)(2,1)}, bf16[128,2048]{1,0:T(8,128)(2,1)}, u32[]{:S(2)}, u32[]{:S(2)}) collective-permute-start(bf16[128,2048]{1,0:T(8,128)(2,1)} %get-tuple-element.56), channel_id=1, source_target_pairs={{0,1},{1,0},{2,3},{3,2},{4,5},{5,4},{6,7},{7,6},{8,9},{9,8},{10,11... | collective-permute-start | bytes 1572872 | tf_op jit(solution)/shard_map/ppermute | solution.py:454
  64.7 8.0 %collective-permute-start.13 = (bf16[64,1024]{1,0:T(8,128)(2,1)S(1)}, bf16[64,1024]{1,0:T(8,128)(2,1)S(1)}, u32[]{:S(2)}, u32[]{:S(2)}) collective-permute-start(bf16[64,1024]{1,0:T(8,128)(2,1)S(1)} %get-tuple-element.55), channel_id=1, source_target_pairs={{0,16},{2,18},{4,20},{6,22},{8,24},{10,26},{12,28},{14,30},{16,0},... | collective-permute-start | bytes 393224 | tf_op jit(solution)/shard_map/ppermute | solution.py:451
  64.8 14.9 %collective-permute-start.10 = (bf16[128,2048]{1,0:T(8,128)(2,1)}, bf16[128,2048]{1,0:T(8,128)(2,1)}, u32[]{:S(2)}, u32[]{:S(2)}) collective-permute-start(bf16[128,2048]{1,0:T(8,128)(2,1)} %get-tuple-element.59), channel_id=1, source_target_pairs={{0,1},{1,0},{2,3},{3,2},{4,5},{5,4},{6,7},{7,6},{8,9},{9,8},{10,11... | collective-permute-start | bytes 1572872 | tf_op jit(solution)/shard_map/ppermute | solution.py:454
  67.7 12.0 %copy-start.9 = (bf16[128,2048]{1,0:T(8,128)(2,1)S(1)}, bf16[128,2048]{1,0:T(8,128)(2,1)}, u32[]{:S(2)}) copy-start(bf16[128,2048]{1,0:T(8,128)(2,1)} %get-tuple-element.57) | copy-start | bytes 1572868
  67.7 17.5 %all-to-all-start.2 = ((bf16[4,128,512]{2,1,0:T(8,128)(2,1)}), bf16[4,128,512]{2,1,0:T(8,128)(2,1)S(1)}, u32[]{:S(2)}, u32[]{:S(2)}) async-start(bf16[4,128,512]{2,1,0:T(8,128)(2,1)} %bitcast.4), calls=%async_computation.2 | async-start | bytes 1048576 | tf_op jit(solution)/shard_map/all_to_all | solution.py:458
  73.2 9.4 %collective-permute-start.14 = (bf16[256,256]{1,0:T(8,128)(2,1)S(1)}, bf16[256,256]{1,0:T(8,128)(2,1)S(1)}, u32[]{:S(2)}, u32[]{:S(2)}) collective-permute-start(bf16[256,256]{1,0:T(8,128)(2,1)S(1)} %get-tuple-element.66), channel_id=1, source_target_pairs={{0,4},{2,6},{4,0},{6,2},{8,12},{10,14},{12,8},{14,10},{16,20},{18,... | collective-permute-start | bytes 393224 | tf_op jit(solution)/shard_map/ppermute | solution.py:451
  76.0 6.0 %collective-permute-start.15 = (bf16[128,256]{1,0:T(8,128)(2,1)S(1)}, bf16[128,256]{1,0:T(8,128)(2,1)S(1)}, u32[]{:S(2)}, u32[]{:S(2)}) collective-permute-start(bf16[128,256]{1,0:T(8,128)(2,1)S(1)} %get-tuple-element.67), channel_id=1, source_target_pairs={{0,2},{2,0},{4,6},{6,4},{8,10},{10,8},{12,14},{14,12},{16,18},{18,... | collective-permute-start | bytes 196616 | tf_op jit(solution)/shard_map/ppermute | solution.py:451
  77.5 5.2 %collective-permute-start.16 = (bf16[128,256]{1,0:T(8,128)(2,1)S(1)}, bf16[128,256]{1,0:T(8,128)(2,1)S(1)}, u32[]{:S(2)}, u32[]{:S(2)}) collective-permute-start(bf16[128,256]{1,0:T(8,128)(2,1)S(1)} %get-tuple-element.68), channel_id=1, source_target_pairs={{0,6},{2,4},{4,2},{6,0},{8,14},{10,12},{12,10},{14,8},{16,22},{18,... | collective-permute-start | bytes 196616 | tf_op jit(solution)/shard_map/ppermute | solution.py:451
  (6 other events, 25.5 us)
